TPU v7x, 256 devices: a whole 4x4x8 slice. The times are simulated.
256 devices in a mesh: frame: 32 (over x_hi, z, core), space: 8 (over y, x_lo).
Axes of the slice: x: 4 (x_hi: 2, x_lo: 2; x = x_hi * 2 + x_lo), y: 4, z: 8, core: 2. Of those that a mesh axis runs over, the one named last changes fastest.
Arguments:
- latents: float32 [64, 1024, 16], P('frame', 'space'), may hold values from -6 to 6
- fresh_noise: float32 [1, 1024, 16], P(None, 'space'), may hold values from -6 to 6
- levels: int32 [64], P('frame'), may hold values from 1 to 64, as said below
- timesteps: int32 [65], replicated, may hold values from 0 to 1000, as said below
- window_offsets: int32 [2], replicated, may hold values from 0 to 15
- time_proj: bfloat16 [256, 6912], replicated, may hold values from -0.1875 to 0.1875
- embed_in: bfloat16 [16, 1152], replicated, may hold values from -1.5 to 1.5
- spatial_proj: bfloat16 [1152, 3456], P('frame'), may hold values from -0.1875 to 0.1875
- spatial_out: bfloat16 [1152, 1152], P('frame'), may hold values from -0.1875 to 0.1875
- temporal_proj: bfloat16 [1152, 3456], P('frame'), may hold values from -0.1875 to 0.1875
- temporal_out: bfloat16 [1152, 1152], P('frame'), may hold values from -0.1875 to 0.1875
- embed_out: bfloat16 [1152, 16], replicated, may hold values from -0.1875 to 0.1875
Outputs:
- queue: float32 [64, 1024, 16], P('frame', 'space')
- velocity: float32 [2, 64, 1024, 16], P(None, 'frame', 'space')
Inputs may be any that keep to these rules, and one draw needn't show every extreme that they name: `levels`: non-decreasing along the queue; the first position has level 1 and the last level 64. `timesteps`: strictly increasing, the first entry 0 and the last 1000.
All inputs are finite; a program needn't handle non-finite values.
Results may differ from a plain program's by a relative error of at most 0.008.
Values may be sent and summed in bfloat16 or wider, within the bound.
A program may use at most 128 MiB of HBM per device.

v0:
```python
import math

import jax
import jax.numpy as jnp
from jax import lax
from jax.sharding import PartitionSpec as P

HEADS = 16
HEAD = 72
WIN = 16
STEPS = 2


epsilon = 1e-06


def shifted(value, axis, steps):
    count = lax.axis_size(axis)
    first, last = (max(0, -steps), min(count, count - steps))
    return lax.ppermute(value, axis, [(source, source + steps) for source in range(first, last)])


def layer_norm(values):
    center = values - jnp.mean(values, -1, keepdims=True)
    spread = jnp.mean(center * center, -1, keepdims=True)
    return center * lax.rsqrt(spread + epsilon)


def head_norm(values):
    wide = values.astype(jnp.float32)
    return (wide * lax.rsqrt(jnp.mean(wide * wide, -1, keepdims=True) + epsilon)).astype(
        jnp.bfloat16
    )


def lookup_table(indices, table):
    hits = indices[:, None] == jnp.arange(table.shape[0], dtype=jnp.int32)[None, :]
    return jnp.sum(jnp.where(hits, table[None, :], 0), axis=1).astype(jnp.float32)


def time_modulation(time_value, time_proj):
    half = time_proj.shape[0] // 2
    freqs = jnp.exp(-math.log(10000.0) * jnp.arange(half, dtype=jnp.float32) / half)
    angles = time_value[:, None] * freqs[None, :]
    features = jnp.concatenate([jnp.cos(angles), jnp.sin(angles)], -1).astype(jnp.bfloat16)
    return jnp.dot(features, time_proj, preferred_element_type=jnp.float32)


def softmax_rows(scores):
    raised = jnp.exp(scores)
    return (raised / jnp.sum(raised, -1, keepdims=True)).astype(jnp.bfloat16)


def spatial_attention(triple):
    frames, tokens = (triple.shape[0], triple.shape[1])
    local_heads = triple.shape[3] // HEAD
    split = triple.reshape(frames, tokens, 3, local_heads, HEAD)
    queries = head_norm(split[:, :, 0])
    keys = head_norm(split[:, :, 1])
    values = split[:, :, 2]
    block = min(512, tokens)
    count = tokens // block
    grouped = jnp.moveaxis(queries.reshape(frames, count, block, local_heads, HEAD), 1, 0)

    def attend(query_block):
        scores = jnp.einsum(
            "fqhd,fkhd->fhqk", query_block, keys, preferred_element_type=jnp.float32
        ) * HEAD ** (-0.5)
        weights = softmax_rows(scores)
        return jnp.einsum(
            "fhqk,fkhd->fqhd", weights, values, preferred_element_type=jnp.float32
        ).astype(jnp.bfloat16)

    mixed = lax.map(attend, grouped)
    return jnp.moveaxis(mixed, 0, 1).reshape(frames, tokens, local_heads * HEAD)


def temporal_attention(triple, offset):
    frames, tokens = (triple.shape[0], triple.shape[1])
    split = triple.reshape(frames, tokens, 3, HEADS, HEAD)
    queries = head_norm(split[:, :, 0])
    keys = head_norm(split[:, :, 1])
    window = (jnp.arange(frames, dtype=jnp.int32) + WIN - offset) // WIN
    same = window[:, None] == window[None, :]
    scores = jnp.einsum(
        "fthd,gthd->thfg", queries, keys, preferred_element_type=jnp.float32
    ) * HEAD ** (-0.5)
    scores = jnp.where(same[None, None], scores, -1e30)
    weights = softmax_rows(scores)
    mixed = jnp.einsum(
        "thfg,gthd->fthd", weights, split[:, :, 2], preferred_element_type=jnp.float32
    )
    return mixed.astype(jnp.bfloat16).reshape(frames, tokens, HEADS * HEAD)


def local(
    latents,
    fresh_noise,
    levels,
    timesteps,
    window_offsets,
    time_proj,
    embed_in,
    spatial_proj,
    spatial_out,
    temporal_proj,
    temporal_out,
    embed_out,
):
    complete = (
        lax.all_gather(spatial_proj, "frame", axis=0, tiled=True),
        lax.all_gather(spatial_out, "frame", axis=0, tiled=True),
        lax.all_gather(temporal_proj, "frame", axis=0, tiled=True),
        lax.all_gather(temporal_out, "frame", axis=0, tiled=True),
    )
    spatial_full, spatial_back, temporal_full, temporal_back = complete
    time_value = lookup_table(levels, timesteps)
    earlier = lookup_table(levels - 1, timesteps)
    step_size = (earlier - time_value) / 1000.0
    modulation = time_modulation(time_value, time_proj)
    pieces = jnp.split(modulation, 6, axis=-1)
    shift_s, scale_s, gate_s, shift_t, scale_t, gate_t = [piece[:, None, :] for piece in pieces]
    latent = latents
    outputs = []
    for step_index in range(STEPS):
        hidden_in = jnp.dot(
            latent.astype(jnp.bfloat16), embed_in, preferred_element_type=jnp.float32
        )
        normed = (layer_norm(hidden_in) * (1.0 + scale_s) + shift_s).astype(jnp.bfloat16)
        triple = jnp.dot(normed, spatial_full, preferred_element_type=jnp.float32).astype(
            jnp.bfloat16
        )
        triple = triple.reshape(triple.shape[0], triple.shape[1], 3, -1)
        by_heads = lax.all_to_all(triple, "space", split_axis=3, concat_axis=1, tiled=True)
        mixed = spatial_attention(by_heads)
        merged = lax.all_to_all(mixed, "space", split_axis=1, concat_axis=2, tiled=True)
        hidden_spatial = hidden_in + gate_s * jnp.dot(
            merged, spatial_back, preferred_element_type=jnp.float32
        )
        normed = (layer_norm(hidden_spatial) * (1.0 + scale_t) + shift_t).astype(jnp.bfloat16)
        by_frames = lax.all_to_all(normed, "frame", split_axis=1, concat_axis=0, tiled=True)
        triple = jnp.dot(by_frames, temporal_full, preferred_element_type=jnp.float32).astype(
            jnp.bfloat16
        )
        mixed = temporal_attention(triple, window_offsets[step_index])
        merged = lax.all_to_all(mixed, "frame", split_axis=0, concat_axis=1, tiled=True)
        hidden_temporal = hidden_spatial + gate_t * jnp.dot(
            merged, temporal_back, preferred_element_type=jnp.float32
        )
        velocity = jnp.dot(
            layer_norm(hidden_temporal).astype(jnp.bfloat16),
            embed_out,
            preferred_element_type=jnp.float32,
        )
        outputs.append(velocity)
        stepped = latent + step_size[:, None, None] * velocity
        if step_index + 1 < STEPS:
            incoming = shifted(stepped[0:1], "frame", -1)
            is_tail = lax.axis_index("frame") == lax.axis_size("frame") - 1
            tail_frame = jnp.where(is_tail, fresh_noise[step_index][None], incoming)
            latent = jnp.concatenate([stepped[1:], tail_frame], 0)
        else:
            latent = stepped
    return (latent, jnp.stack(outputs))


def solution(mesh):
    return jax.shard_map(
        local,
        mesh=mesh,
        in_specs=(
            P("frame", "space", None),
            P(None, "space", None),
            P("frame"),
            P(),
            P(),
            P(),
            P(),
            P("frame", None),
            P("frame", None),
            P("frame", None),
            P("frame", None),
            P(),
        ),
        out_specs=(P("frame", "space", None), P(None, "frame", "space", None)),
        check_vma=False,
    )
```

profile of v0, /device:TPU:1, one launch (start us, length us, event | category | flops | bytes accessed | tf_op | source)
XLA Modules:
  0.0 616.2 jit_solution(3231349407475502211)
XLA Ops:
  15.6 102.7 %all-gather.9.cloned.1.call-done = bf16[32,36,3456]{2,1,0:T(8,128)(2,1)} async-done(((bf16[1,36,3456]{2,1,0:T(8,128)(2,1)}), bf16[32,36,3456]{2,1,0:T(8,128)(2,1)}) %all-gather.9.cloned.1.call-update) | async-done | bytes 7962640 | tf_op jit(solution)/shard_map/all_gather | solution.py:111
  118.3 12.5 %reshape.400 = bf16[1152,3456,1]{1,0,2:T(8,128)(2,1)} reshape(bf16[32,36,3456]{2,1,0:T(8,128)(2,1)} %all-gather.9.cloned.1.call-done) | data formatting | bytes 15925248
  130.8 5.9 convolution_convert_fusion.3
  137.8 9.7 %copy.169 = bf16[2,128,3,1152]{1,0,2,3:T(2,128)(2,1)} copy(bf16[2,128,3,1152]{1,3,2,0:T(8,128)(2,1)S(1)} %bitcast.229) | data formatting | bytes 3538944 | tf_op jit(solution)/shard_map/reshape | solution.py:133
  147.5 4.3 all-to-all-start
  151.8 26.8 %all-to-all-done = bf16[2,128,3,1152]{1,0,2,3:T(2,128)(2,1)S(1)} async-done(((bf16[2,128,3,1152]{1,0,2,3:T(2,128)(2,1)}), bf16[2,128,3,1152]{1,0,2,3:T(2,128)(2,1)S(1)}, u32[]{:S(2)}, u32[]{:S(2)}) %all-to-all-start) | async-done | bytes 1769504 | tf_op jit(solution)/shard_map/all_to_all | solution.py:134
  188.6 7.3 %while.20 = (s32[]{:T(128)}, bf16[2,2,512,2,72]{2,4,3,1,0:T(8,128)(2,1)S(1)}, bf16[2,2,512,2,72]{2,4,3,1,0:T(8,128)(2,1)S(1)}, bf16[2,1024,2,72]{1,3,2,0:T(8,128...) while((s32[]{:T(128)}, bf16[2,2,512,2,72]{2,4,3,1,0:T(8,128)(2,1)S(1)}, ...), condition=%wide.region_8.9_spmd, body=%wide.region_6.8_spmd.sunk | while | flops 614610944 | bytes 18563156 | solution.py:74
  198.8 4.2 all-to-all-start.1
  203.7 3.6 reshape.401
  207.3 8.3 %all-to-all-done.1 = bf16[2,1024,144]{2,0,1:T(2,128)(2,1)} async-done(((bf16[2,1024,144]{2,0,1:T(2,128)(2,1)}), bf16[2,1024,144]{2,0,1:T(2,128)(2,1)}, u32[]{:S(2)}, u32[]{:S(2)}) %all-to-all-start.1) | async-done | bytes 589856 | tf_op jit(solution)/shard_map/all_to_all | solution.py:136
  223.4 9.2 %all-to-all-start.2 = ((bf16[2,128,1152]{2,0,1:T(2,128)(2,1)}), bf16[2,128,1152]{2,0,1:T(2,128)(2,1)S(1)}, u32[]{:S(2)}, u32[]{:S(2)}) async-start(bf16[2,128,1152]{2,0,1:T(2,128)(2,1)} %copy.179), calls=%async_computation.2 | async-start | bytes 1179648 | tf_op jit(solution)/shard_map/all_to_all | solution.py:141
  233.9 80.0 %all-gather.13.cloned.1.call-done = bf16[32,36,3456]{2,1,0:T(8,128)(2,1)} async-done(((bf16[1,36,3456]{2,1,0:T(8,128)(2,1)}), bf16[32,36,3456]{2,1,0:T(8,128)(2,1)}) %all-gather.13.cloned.1.call-update) | async-done | bytes 7962640 | tf_op jit(solution)/shard_map/all_gather | solution.py:113
  313.9 12.4 %reshape.402 = bf16[1152,3456,1]{1,0,2:T(8,128)(2,1)} reshape(bf16[32,36,3456]{2,1,0:T(8,128)(2,1)} %all-gather.13.cloned.1.call-done) | data formatting | bytes 15925248
  329.5 7.0 %convolution_convert_fusion.2 = bf16[64,4,3456]{2,0,1:T(8,128)(2,1)} fusion(bf16[64,4,1152]{2,0,1:T(8,128)(2,1)S(1)} %all_to_all.110, bf16[1152,3456,1]{1,0,2:T(8,128)(2,1)} %reshape.402), kind=kOutput, calls=%fused_computation.26 | convolution fusion | flops 2039316480 | bytes 10321920 | tf_op jit(solution)/shard_map/dot_general | solution.py:142
  336.6 7.7 %reshape.376 = bf16[64,4,3,16,72]{4,3,2,0,1:T(8,128)(2,1)} reshape(bf16[64,4,3456]{2,0,1:T(8,128)(2,1)} %convolution_convert_fusion.2) | data formatting | bytes 3538944 | tf_op jit(solution)/shard_map/reshape | solution.py:80
  351.9 3.6 reshape.409
  355.5 4.9 all-to-all-start.3
  360.5 40.3 %all-gather.15.cloned.1.call-done = bf16[32,36,1152]{2,1,0:T(8,128)(2,1)} async-done(((bf16[1,36,1152]{2,1,0:T(8,128)(2,1)}), bf16[32,36,1152]{2,1,0:T(8,128)(2,1)}) %all-gather.15.cloned.1.call-update) | async-done | bytes 2654224 | tf_op jit(solution)/shard_map/all_gather | solution.py:114
  400.8 5.1 reshape.403
  419.4 7.2 %convolution_convert_fusion.1 = bf16[2,128,3456]{2,1,0:T(8,128)(2,1)} fusion(bf16[1152,3456,1]{1,0,2:T(8,128)(2,1)} %reshape.400, f32[2,128,1152]{2,1,0:T(8,128)S(1)} %get-tuple-element.117, f32[2,128]{1,0:T(2,128)S(1)} %add_rsqrt_fusion.10, f32[2,128]{1,0:T(2,128)S(1)} %broadcast_multiply_fusion.2, f32[2,1152]{1,0:T(2,128)S(1)} %copy-done.26, ...), kind=kOutput, calls=%fused_computation.25 | convolution fusion | flops 2040791040 | bytes 10932224 | tf_op jit(solution)/shard_map/dot_general | solution.py:130
  426.6 3.8 copy.188
  430.4 10.8 %copy.189 = bf16[2,128,3,1152]{1,0,2,3:T(2,128)(2,1)S(1)} copy(bf16[2,128,3,1152]{1,3,2,0:T(8,128)(2,1)} %bitcast.231) | data formatting | bytes 3538944 | tf_op jit(solution)/shard_map/reshape | solution.py:133
  441.3 26.8 %all_to_all.138 = bf16[2,128,3,1152]{1,0,2,3:T(2,128)(2,1)S(1)} all-to-all(bf16[2,128,3,1152]{1,0,2,3:T(2,128)(2,1)S(1)} %copy.189), channel_id=1, replica_groups=mesh['frame'=32,'space'=8] {'space'}, dimensions={3} | all-to-all | bytes 3538944 | tf_op jit(solution)/shard_map/all_to_all | solution.py:134
  470.0 3.8 reshape.379
  483.4 11.1 %while.21 = (s32[]{:T(128)}, bf16[2,2,512,2,72]{2,4,3,1,0:T(8,128)(2,1)}, bf16[2,2,512,2,72]{2,4,3,1,0:T(8,128)(2,1)}, bf16[2,1024,2,72]{1,3,2,0:T(8,128)(2,1)S(1)}, bf16[2,1024,2,72]{1,3,2,0:T(8,128)(2,1)}, /*index=5*/s32[]{:T(128)}) while((s32[]{:T(128)}, bf16[2,2,512,2,72]{2,4,3,1,0:T(8,128)(2,1)}, ...), condition=%wide.region_22.23_spmd, body=%wide.region_20.22_spmd.sunk | while | flops 614610944 | bytes 25641128 | solution.py:74
  498.0 4.4 reshape.411
  502.4 20.4 %all_to_all.139 = bf16[2,1024,144]{2,0,1:T(2,128)(2,1)} all-to-all(bf16[2,1024,144]{2,0,1:T(2,128)(2,1)} %reshape.411), channel_id=1, replica_groups=mesh['frame'=32,'space'=8] {'space'}, dimensions={1} | all-to-all | bytes 1179648 | tf_op jit(solution)/shard_map/all_to_all | solution.py:136
  530.5 7.6 %all-to-all-start.6 = ((bf16[2,128,1152]{2,0,1:T(2,128)(2,1)}), bf16[2,128,1152]{2,0,1:T(2,128)(2,1)S(1)}, u32[]{:S(2)}, u32[]{:S(2)}) async-start(bf16[2,128,1152]{2,0,1:T(2,128)(2,1)} %copy.199), calls=%async_computation.6 | async-start | bytes 1179648 | tf_op jit(solution)/shard_map/all_to_all | solution.py:141
  538.8 18.4 %all-to-all-done.6 = bf16[2,128,1152]{2,0,1:T(2,128)(2,1)S(1)} async-done(((bf16[2,128,1152]{2,0,1:T(2,128)(2,1)}), bf16[2,128,1152]{2,0,1:T(2,128)(2,1)S(1)}, u32[]{:S(2)}, u32[]{:S(2)}) %all-to-all-start.6) | async-done | bytes 589856 | tf_op jit(solution)/shard_map/all_to_all | solution.py:141
  557.8 7.0 %convolution_convert_fusion = bf16[64,4,3456]{2,0,1:T(8,128)(2,1)} fusion(bf16[64,4,1152]{2,0,1:T(8,128)(2,1)S(1)} %all_to_all.125, bf16[1152,3456,1]{1,0,2:T(8,128)(2,1)} %reshape.402), kind=kOutput, calls=%fused_computation.24 | convolution fusion | flops 2039316480 | bytes 10321920 | tf_op jit(solution)/shard_map/dot_general | solution.py:142
  564.8 6.9 %reshape.381 = bf16[64,4,3,16,72]{4,3,2,0,1:T(8,128)(2,1)S(1)} reshape(bf16[64,4,3456]{2,0,1:T(8,128)(2,1)} %convolution_convert_fusion) | data formatting | bytes 3538944 | tf_op jit(solution)/shard_map/reshape | solution.py:80
  578.3 24.3 %all_to_all.140 = bf16[64,4,1152]{2,1,0:T(4,128)(2,1)S(1)} all-to-all(bf16[64,4,1152]{2,1,0:T(4,128)(2,1)S(1)} %reshape.412), channel_id=1, replica_groups=mesh['frame'=32,'space'=8] {'frame'}, dimensions={0} | all-to-all | bytes 1179648 | tf_op jit(solution)/shard_map/all_to_all | solution.py:146
  (198 shorter events, 111.2 us)
Async XLA Ops:
  7.2 7.2 %copy-start = (bf16[256,6912]{1,0:T(8,128)(2,1)S(1)}, bf16[256,6912]{1,0:T(8,128)(2,1)}, u32[]{:S(2)}) copy-start(bf16[256,6912]{1,0:T(8,128)(2,1)} %param.21) | copy-start | bytes 10616836
  7.2 111.1 %all-gather.9.cloned.1.call-start = ((), (), s32[]{:S(2)}) async-start(), calls=%async_computation.8 | async-start | bytes 9123840 | tf_op jit(solution)/shard_map/all_gather | solution.py:111
  7.9 195.7 %all-gather.11.cloned.1.call-start = ((), (), s32[]{:S(2)}) async-start(), calls=%async_computation.9 | async-start | bytes 3041280 | tf_op jit(solution)/shard_map/all_gather | solution.py:112
  8.7 305.2 %all-gather.13.cloned.1.call-start = ((), (), s32[]{:S(2)}) async-start(), calls=%async_computation.10 | async-start | bytes 9123840 | tf_op jit(solution)/shard_map/all_gather | solution.py:113
  15.5 115.2 %copy-start.25 = (f32[2,1152]{1,0:T(2,128)}, f32[2,1152]{1,0:T(2,128)S(1)}, u32[]{:S(2)}) copy-start(f32[2,1152]{1,0:T(2,128)S(1)} %get-tuple-element.97) | copy-start | bytes 27652
  15.6 115.2 %copy-start.27 = (f32[2,1152]{1,0:T(2,128)}, f32[2,1152]{1,0:T(2,128)S(1)}, u32[]{:S(2)}) copy-start(f32[2,1152]{1,0:T(2,128)S(1)} %get-tuple-element.98) | copy-start | bytes 27652
  15.6 115.2 %copy-start.6 = (f32[2,128,1152]{2,1,0:T(8,128)S(1)}, f32[2,128,1152]{2,1,0:T(8,128)}, u32[]{:S(2)}) copy-start(f32[2,128,1152]{2,1,0:T(8,128)} %copy-done.5) | copy-start | bytes 3538948
  15.6 115.2 %copy-start.31 = (f32[2,128]{1,0:T(2,128)S(1)}, f32[2,128]{1,0:T(2,128)}, u32[]{:S(2)}) copy-start(f32[2,128]{1,0:T(2,128)} %add_rsqrt_fusion.13) | copy-start | bytes 3076
  147.5 31.1 %all-to-all-start = ((bf16[2,128,3,1152]{1,0,2,3:T(2,128)(2,1)}), bf16[2,128,3,1152]{1,0,2,3:T(2,128)(2,1)S(1)}, u32[]{:S(2)}, u32[]{:S(2)}) async-start(bf16[2,128,3,1152]{1,0,2,3:T(2,128)(2,1)} %copy.169), calls=%async_computation | async-start | bytes 3538944 | tf_op jit(solution)/shard_map/all_to_all | solution.py:134
  198.8 16.8 %all-to-all-start.1 = ((bf16[2,1024,144]{2,0,1:T(2,128)(2,1)}), bf16[2,1024,144]{2,0,1:T(2,128)(2,1)}, u32[]{:S(2)}, u32[]{:S(2)}) async-start(bf16[2,1024,144]{2,0,1:T(2,128)(2,1)} %reshape.406), calls=%async_computation.1 | async-start | bytes 2097152 | tf_op jit(solution)/shard_map/all_to_all | solution.py:136
  203.1 197.7 %all-gather.15.cloned.1.call-start = ((), (), s32[]{:S(2)}) async-start(), calls=%async_computation.11 | async-start | bytes 3041280 | tf_op jit(solution)/shard_map/all_gather | solution.py:114
  203.6 14.5 %copy-start.16 = (f32[2,1152]{1,0:T(2,128)S(1)}, f32[2,1152]{1,0:T(2,128)}, u32[]{:S(2)}) copy-start(f32[2,1152]{1,0:T(2,128)} %get-tuple-element.99) | copy-start | bytes 27652
  218.1 3.5 copy-start.17
  221.6 10.9 %copy-start.30 = (s32[2]{0:T(128)S(1)}, s32[2]{0:T(128)}, u32[]{:S(2)}) copy-start(s32[2]{0:T(128)} %param.20) | copy-start | bytes 28
  223.4 102.9 %all-to-all-start.2 = ((bf16[2,128,1152]{2,0,1:T(2,128)(2,1)}), bf16[2,128,1152]{2,0,1:T(2,128)(2,1)S(1)}, u32[]{:S(2)}, u32[]{:S(2)}) async-start(bf16[2,128,1152]{2,0,1:T(2,128)(2,1)} %copy.179), calls=%async_computation.2 | async-start | bytes 1179648 | tf_op jit(solution)/shard_map/all_to_all | solution.py:141
  351.9 8.5 %copy-start.32 = (s32[2]{0:T(128)S(1)}, s32[2]{0:T(128)}, u32[]{:S(2)}) copy-start(s32[2]{0:T(128)} %get-tuple-element.58) | copy-start | bytes 28
  351.9 8.5 %copy-start.34 = (s32[2]{0:T(128)S(1)}, s32[2]{0:T(128)}, u32[]{:S(2)}) copy-start(s32[2]{0:T(128)} %copy-done.33) | copy-start | bytes 28
  355.5 50.4 %all-to-all-start.3 = ((bf16[64,4,1152]{2,1,0:T(4,128)(2,1)}), bf16[64,4,1152]{2,1,0:T(4,128)(2,1)S(1)}, u32[]{:S(2)}, u32[]{:S(2)}) async-start(bf16[64,4,1152]{2,1,0:T(4,128)(2,1)} %reshape.409), calls=%async_computation.3 | async-start | bytes 1179648 | tf_op jit(solution)/shard_map/all_to_all | solution.py:146
  408.4 3.5 copy-start.14
  408.4 3.5 copy-start.23
  411.6 6.3 %copy-start.29 = (f32[1,128,16]{1,2,0:T(8,128)S(1)}, f32[1,128,16]{1,2,0:T(8,128)}, u32[]{:S(2)}) copy-start(f32[1,128,16]{1,2,0:T(8,128)} %param.17) | copy-start | bytes 24580
  411.6 6.3 %copy-start.13 = (bf16[16,1152]{1,0:T(8,128)(2,1)S(1)}, bf16[16,1152]{1,0:T(8,128)(2,1)}, u32[]{:S(2)}) copy-start(bf16[16,1152]{1,0:T(8,128)(2,1)} %param.22) | copy-start | bytes 110596
  411.9 7.5 %copy-start.26 = (f32[2,1152]{1,0:T(2,128)S(1)}, f32[2,1152]{1,0:T(2,128)}, u32[]{:S(2)}) copy-start(f32[2,1152]{1,0:T(2,128)} %copy-done.25) | copy-start | bytes 27652
  411.9 7.4 %copy-start.28 = (f32[2,1152]{1,0:T(2,128)S(1)}, f32[2,1152]{1,0:T(2,128)}, u32[]{:S(2)}) copy-start(f32[2,1152]{1,0:T(2,128)} %copy-done.27) | copy-start | bytes 27652
  412.9 13.7 %copy-start.21 = (f32[1,128,16]{1,2,0:T(8,128)}, f32[1,128,16]{1,2,0:T(8,128)S(1)}, u32[]{:S(2)}) copy-start(f32[1,128,16]{1,2,0:T(8,128)S(1)} %get-tuple-element.100) | copy-start | bytes 24580
  412.9 5.0 collective-permute-start
  417.9 8.7 %copy-start.19 = (f32[1,128,16]{1,2,0:T(8,128)}, f32[1,128,16]{1,2,0:T(8,128)S(1)}, u32[]{:S(2)}) copy-start(f32[1,128,16]{1,2,0:T(8,128)S(1)} %broadcast_select_fusion) | copy-start | bytes 24580
  530.5 26.6 %all-to-all-start.6 = ((bf16[2,128,1152]{2,0,1:T(2,128)(2,1)}), bf16[2,128,1152]{2,0,1:T(2,128)(2,1)S(1)}, u32[]{:S(2)}, u32[]{:S(2)}) async-start(bf16[2,128,1152]{2,0,1:T(2,128)(2,1)} %copy.199), calls=%async_computation.6 | async-start | bytes 1179648 | tf_op jit(solution)/shard_map/all_to_all | solution.py:141
  603.8 3.8 copy-start.15
  603.8 3.8 copy-start.20
  603.8 3.8 copy-start.22
  603.8 5.4 copy-start.1
  (16 other events, 28.0 us)
Sparse Core Ops, SparseCore 0:
  10.8 107.4 all-gather.8
  121.0 82.0 all-gather.10
  205.8 107.9 all-gather.12
  316.4 84.3 all-gather.14
where the time goes:
time: 624 us; the launch traced here: 616 us
  waiting for transfers between devices  282 us (45%)
  local copies, waits for them, and re-layouts  134 us (21%)
  blocking collectives  71.6 us (11%)
  matrix products  63.7 us (10%)
  starting transfers between devices  32.5 us (5%)
  other arithmetic  17.7 us (3%)
  between operations  15 us (2%)
    all_gather x1, waiting for transfers between devices, local(): lax.all_gather(spatial_proj, 'frame', axis=0, tiled=True)  103 us
    all_gather x1, waiting for transfers between devices, local(): lax.all_gather(temporal_proj, 'frame', axis=0, tiled=True)  80 us
    all_gather x1, waiting for transfers between devices, local(): lax.all_gather(temporal_out, 'frame', axis=0, tiled=True)  40.3 us
    unnamed x68, local copies, waits for them, and re-layouts  37.5 us
    all_to_all x1, blocking collectives, local(): lax.all_to_all(triple, 'space', split_axis=3, concat_axis=1, tiled=True)  26.8 us
    all_to_all x1, waiting for transfers between devices, local(): lax.all_to_all(triple, 'space', split_axis=3, concat_axis=1, tiled=True)  26.8 us
    all_to_all x1, blocking collectives, local(): lax.all_to_all(mixed, 'frame', split_axis=0, concat_axis=1, tiled=True)  24.3 us
    reshape x2, local copies, waits for them, and re-layouts, local(): triple = triple.reshape(triple.shape[0], triple.shape[1], 3, -1)  20.5 us
  transfers between devices with their start and end apart: 10, of which 7 were waited for; matrix products, arithmetic and copies ran while one was open for 18% of the time, Pallas kernels for 0%

commit v1 on v0

v1 whole, which is shorter than its diff:
```python
import math

import jax
import jax.numpy as jnp
from jax import lax
from jax.sharding import PartitionSpec as P

HEADS = 16
HEAD = 72
WIN = 16
STEPS = 2
GROUPS = 4


epsilon = 1e-06


def layer_norm(values):
    center = values - jnp.mean(values, -1, keepdims=True)
    spread = jnp.mean(center * center, -1, keepdims=True)
    return center * lax.rsqrt(spread + epsilon)


def head_norm(values):
    wide = values.astype(jnp.float32)
    return (wide * lax.rsqrt(jnp.mean(wide * wide, -1, keepdims=True) + epsilon)).astype(
        jnp.bfloat16
    )


def lookup_table(indices, table):
    hits = indices[:, None] == jnp.arange(table.shape[0], dtype=jnp.int32)[None, :]
    return jnp.sum(jnp.where(hits, table[None, :], 0), axis=1).astype(jnp.float32)


def time_modulation(time_value, time_proj):
    half = time_proj.shape[0] // 2
    freqs = jnp.exp(-math.log(10000.0) * jnp.arange(half, dtype=jnp.float32) / half)
    angles = time_value[:, None] * freqs[None, :]
    features = jnp.concatenate([jnp.cos(angles), jnp.sin(angles)], -1).astype(jnp.bfloat16)
    return jnp.dot(features, time_proj, preferred_element_type=jnp.float32)


def softmax_rows(scores):
    raised = jnp.exp(scores)
    return (raised / jnp.sum(raised, -1, keepdims=True)).astype(jnp.bfloat16)


def spatial_block(tokens, embed_in, shift, scale, weights):
    hidden = jnp.dot(tokens, embed_in, preferred_element_type=jnp.float32)
    normed = (layer_norm(hidden) * (1.0 + scale) + shift).astype(jnp.bfloat16)
    triple = jnp.dot(normed, weights, preferred_element_type=jnp.float32).astype(jnp.bfloat16)
    split = triple.reshape(triple.shape[0], 3, HEADS // GROUPS, HEAD)
    queries = head_norm(split[:, 0])
    keys = head_norm(split[:, 1])
    scores = jnp.einsum(
        "qhd,khd->hqk", queries, keys, preferred_element_type=jnp.float32
    ) * HEAD ** (-0.5)
    weights = softmax_rows(scores)
    mixed = jnp.einsum("hqk,khd->qhd", weights, split[:, 2], preferred_element_type=jnp.float32)
    return mixed.astype(jnp.bfloat16).reshape(triple.shape[0], -1)


def temporal_block(mixed, latent, mods, offset, embed_in, spatial_out, proj, out, embed_out):
    gate_s, shift_t, scale_t, gate_t = [mod[:, None, :] for mod in mods]
    frames, tokens = mixed.shape[:2]
    hidden_in = jnp.dot(latent.astype(jnp.bfloat16), embed_in, preferred_element_type=jnp.float32)
    hidden = hidden_in + gate_s * jnp.dot(mixed, spatial_out, preferred_element_type=jnp.float32)
    normed = (layer_norm(hidden) * (1.0 + scale_t) + shift_t).astype(jnp.bfloat16)
    triple = jnp.dot(normed, proj, preferred_element_type=jnp.float32).astype(jnp.bfloat16)
    split = triple.reshape(frames, tokens, 3, HEADS, HEAD)
    queries = head_norm(split[:, :, 0])
    keys = head_norm(split[:, :, 1])
    window = (jnp.arange(frames, dtype=jnp.int32) + WIN - offset) // WIN
    same = window[:, None] == window[None, :]
    scores = jnp.einsum(
        "fthd,gthd->thfg", queries, keys, preferred_element_type=jnp.float32
    ) * HEAD ** (-0.5)
    weights = softmax_rows(jnp.where(same[None, None], scores, -1e30))
    mixed = jnp.einsum(
        "thfg,gthd->fthd", weights, split[:, :, 2], preferred_element_type=jnp.float32
    )
    mixed = mixed.astype(jnp.bfloat16).reshape(frames, tokens, HEADS * HEAD)
    hidden = hidden + gate_t * jnp.dot(mixed, out, preferred_element_type=jnp.float32)
    return jnp.dot(
        layer_norm(hidden).astype(jnp.bfloat16), embed_out, preferred_element_type=jnp.float32
    )


def to_tokens(values):
    return lax.all_to_all(values, "frame", split_axis=1, concat_axis=0, tiled=True)


def to_frames(values):
    return lax.all_to_all(values, "frame", split_axis=0, concat_axis=1, tiled=True)


def local(
    latents,
    fresh_noise,
    levels,
    timesteps,
    window_offsets,
    time_proj,
    embed_in,
    spatial_proj,
    spatial_out,
    temporal_proj,
    temporal_out,
    embed_out,
):
    place, row = lax.axis_index("space"), lax.axis_index("frame")
    which, group = place // GROUPS, place % GROUPS
    heads = spatial_proj.reshape(-1, 3, GROUPS, HEADS // GROUPS * HEAD)
    own = lax.dynamic_index_in_dim(heads, group, 2, keepdims=False)
    spatial_own = lax.all_gather(own.reshape(own.shape[0], -1), "frame", axis=0, tiled=True)
    spatial_back = lax.all_gather(spatial_out, "frame", axis=0, tiled=True)
    temporal_full = lax.all_gather(temporal_proj, "frame", axis=0, tiled=True)
    temporal_back = lax.all_gather(temporal_out, "frame", axis=0, tiled=True)
    all_levels = lax.all_gather(levels, "frame", axis=0, tiled=True)
    time_value = lookup_table(all_levels, timesteps)
    earlier = lookup_table(all_levels - 1, timesteps)
    step_size = (earlier - time_value) / 1000.0
    modulation = time_modulation(time_value, time_proj)
    shift_s, scale_s, gate_s, shift_t, scale_t, gate_t = jnp.split(modulation, 6, axis=-1)
    frame = row * latents.shape[0] + which
    shift_own = lax.dynamic_slice_in_dim(shift_s, frame, 1)
    scale_own = lax.dynamic_slice_in_dim(scale_s, frame, 1)
    latent = to_tokens(latents)
    fresh = lax.dynamic_slice_in_dim(fresh_noise, row * latent.shape[1], latent.shape[1], 1)
    by_frame = latents.astype(jnp.bfloat16)
    outputs = []
    for step_index in range(STEPS):
        whole = lax.all_gather(by_frame, "space", axis=1, tiled=True)
        tokens = lax.dynamic_index_in_dim(whole, which, 0, keepdims=False)
        mixed = spatial_block(tokens, embed_in, shift_own, scale_own, spatial_own)
        parts = mixed.reshape(8, -1, mixed.shape[-1])
        parts = lax.all_to_all(parts, "space", split_axis=0, concat_axis=0)
        parts = parts.reshape(2, GROUPS, parts.shape[1], -1)
        parts = jnp.moveaxis(parts, 1, 2).reshape(2, parts.shape[2], -1)
        velocity = temporal_block(
            to_tokens(parts),
            latent,
            (gate_s, shift_t, scale_t, gate_t),
            window_offsets[step_index],
            embed_in,
            spatial_back,
            temporal_full,
            temporal_back,
            embed_out,
        )
        outputs.append(velocity)
        stepped = latent + step_size[:, None, None] * velocity
        if step_index + 1 < STEPS:
            latent = jnp.concatenate([stepped[1:], fresh[step_index][None]], 0)
            by_frame = to_frames(latent.astype(jnp.bfloat16))
        else:
            latent = stepped
    result = to_frames(jnp.concatenate([latent] + outputs, -1))
    size = latent.shape[-1]
    queue = result[..., :size]
    return (queue, jnp.stack([result[..., size : 2 * size], result[..., 2 * size :]]))


def solution(mesh):
    return jax.shard_map(
        local,
        mesh=mesh,
        in_specs=(
            P("frame", "space", None),
            P(None, "space", None),
            P("frame"),
            P(),
            P(),
            P(),
            P(),
            P("frame", None),
            P("frame", None),
            P("frame", None),
            P("frame", None),
            P(),
        ),
        out_specs=(P("frame", "space", None), P(None, "frame", "space", None)),
        check_vma=False,
    )
```

time: 624 us -> 597 us (0.957)
  local copies, waits for them, and re-layouts: 134 us -> 97.8 us
  blocking collectives: 71.6 us -> 106 us
  waiting for transfers between devices: 282 us -> 265 us
    all_gather x0 -> x2, blocking collectives: none -> 44 us  [local(): whole = lax.all_gather(by_frame, 'space', axis=1, tiled=True)]
    reshape x14 -> x7, local copies, waits for them, and re-layouts: 60.3 us -> 27.9 us  [the longest x2 15.5 us: temporal_block(): split = triple.reshape(frames, tokens, 3, HEADS, HEAD)]
    all_to_all x3, blocking collectives: 71.6 us -> 43.3 us  [the longest x2 30 us: to_frames(): lax.all_to_all(values, 'frame', split_axis=0, concat_axis=1, tiled=True)]
    all_to_all x5 -> x4, waiting for transfers between devices: 53.5 us -> 34.5 us  [the longest x3 25.3 us: to_tokens(): lax.all_to_all(values, 'frame', split_axis=1, concat_axis=0, tiled=True)]
    unnamed x0 -> x1, blocking collectives: none -> 18.5 us
    convert_element_type x6 -> x3, local copies, waits for them, and re-layouts: 13.3 us -> 3.46 us  [the longest x2 3.34 us: temporal_block(): mixed = mixed.astype(jnp.bfloat16).reshape(frames, tokens, HEADS * HEAD)]
    dot_general x24 -> x22, matrix products: 63.1 us -> 57.2 us  [the longest x2 14.9 us: temporal_block(): jnp.dot(normed, proj, preferred_element_type=jnp.float32)]
    all_to_all x14 -> x12, local copies, waits for them, and re-layouts: 16.3 us -> 11.8 us  [the longest x8 10.7 us: to_tokens(): lax.all_to_all(values, 'frame', split_axis=1, concat_axis=0, tiled=True)]
  transfers between devices with their start and end apart: 10 -> 8, of which waited for: 7 -> 7; matrix products, arithmetic and copies ran while one was open for 18% -> 8% of each run, Pallas kernels for 0% -> 0%
where the time goes in v1:
time: 597 us; the launch traced here: 587 us
  waiting for transfers between devices  265 us (44%)
  blocking collectives  106 us (18%)
  local copies, waits for them, and re-layouts  97.8 us (16%)
  matrix products  57.9 us (10%)
  starting transfers between devices  29.7 us (5%)
  other arithmetic  15.4 us (3%)
  between operations  15.3 us (3%)
    all_gather x1, waiting for transfers between devices, local(): temporal_full = lax.all_gather(temporal_proj, 'frame', axis=0, tiled=True)  89.5 us
    all_gather x1, waiting for transfers between devices, local(): temporal_back = lax.all_gather(temporal_out, 'frame', axis=0, tiled=True)  78.8 us
    all_gather x2, blocking collectives, local(): whole = lax.all_gather(by_frame, 'space', axis=1, tiled=True)  44 us
    unnamed x71, local copies, waits for them, and re-layouts  40.4 us
    all_gather x1, waiting for transfers between devices, local(): lax.all_gather(own.reshape(own.shape[0], -1), 'frame', axis=0, tiled=True)  33.9 us
    all_to_all x2, blocking collectives, to_frames(): lax.all_to_all(values, 'frame', split_axis=0, concat_axis=1, tiled=True)  30 us
    all_gather x1, waiting for transfers between devices, local(): spatial_back = lax.all_gather(spatial_out, 'frame', axis=0, tiled=True)  26.6 us
    all_to_all x3, starting transfers between devices, to_tokens(): lax.all_to_all(values, 'frame', split_axis=1, concat_axis=0, tiled=True)  25.3 us
  transfers between devices with their start and end apart: 8, of which 7 were waited for; matrix products, arithmetic and copies ran while one was open for 8% of the time, Pallas kernels for 0%

profile of v1, /device:TPU:1, one launch (start us, length us, event | category | flops | bytes accessed | tf_op | source)
XLA Modules:
  0.0 587.0 jit_solution(9289002624263298334)
XLA Ops:
  18.8 18.5 %all-reduce = s32[64]{0:T(128)S(1)} all-reduce(s32[64]{0:T(128)S(1)} %dynamic-update-slice), channel_id=1, replica_groups=mesh['frame'=32,'space'=8] {'frame'}, use_global_device_ids=true, to_apply=%add | all-reduce | flops 64 | bytes 512
  41.2 20.0 %all_gather.22 = bf16[2,1024,16]{1,2,0:T(8,128)(2,1)S(1)} all-gather(bf16[2,128,16]{1,2,0:T(8,128)(2,1)S(1)} %convert_element_type.170), channel_id=1, replica_groups=mesh['frame'=32,'space'=8] {'space'}, dimensions={1}, use_global_device_ids=true | all-gather | bytes 73728 | tf_op jit(solution)/shard_map/all_gather | solution.py:134
  64.2 33.9 %all-gather.9.cloned.1.call-done = bf16[32,36,864]{2,1,0:T(8,128)(2,1)} async-done(((bf16[1,36,864]{2,1,0:T(8,128)(2,1)}), bf16[32,36,864]{2,1,0:T(8,128)(2,1)}) %all-gather.9.cloned.1.call-update) | async-done | bytes 1990672 | tf_op jit(solution)/shard_map/all_gather | solution.py:116
  98.1 4.1 reshape.375
  102.2 5.9 %fusion.27 = bf16[1024,864]{0,1:T(8,128)(2,1)S(1)} fusion(bf16[1152,864]{1,0:T(8,128)(2,1)} %reshape.375, f32[1024,1152]{1,0:T(8,128)} %copy-done.2, f32[1152]{0:T(1024)S(1)} %get-tuple-element.57, f32[1152]{0:T(1024)S(1)} %get-tuple-element.58, f32[1024]{0:T(1024)S(1)} %add_rsqrt_fusion.9, f32[1024]{0:T(1024)S(1)} %broadcast_multiply_fusion.1), kind=kOutput, calls=%fused_computation.53 | convolution fusion | flops 2045214720 | bytes 8496128 | tf_op jit(solution)/shard_map/dot_general | solution.py:52
  111.5 3.1 fusion.33
  115.6 4.2 all-to-all-start.1
  120.7 9.2 %all-to-all-done.1 = bf16[8,128,288]{1,2,0:T(8,128)(2,1)S(1)} async-done(((bf16[8,128,288]{1,2,0:T(8,128)(2,1)}), bf16[8,128,288]{1,2,0:T(8,128)(2,1)S(1)}, u32[]{:S(2)}, u32[]{:S(2)}) %all-to-all-start.1) | async-done | bytes 589856 | tf_op jit(solution)/shard_map/all_to_all | solution.py:138
  129.8 7.7 %all-to-all-start = ((f32[32,1,128]{2,1,0:T(1,128)}), f32[32,1,128]{2,1,0:T(1,128)S(1)}, u32[]{:S(2)}, u32[]{:S(2)}) async-start(f32[32,1,128]{2,1,0:T(1,128)} %reshape.397), calls=%async_computation | async-start | bytes 32768 | tf_op jit(solution)/shard_map/all_to_all | solution.py:91
  139.3 7.5 %all-to-all-done = f32[32,1,128]{2,1,0:T(1,128)S(1)} async-done(((f32[32,1,128]{2,1,0:T(1,128)}), f32[32,1,128]{2,1,0:T(1,128)S(1)}, u32[]{:S(2)}, u32[]{:S(2)}) %all-to-all-start) | async-done | bytes 16416 | tf_op jit(solution)/shard_map/all_to_all | solution.py:91
  146.8 5.2 all-to-all-start.2
  157.6 26.6 %all-gather.11.cloned.1.call-done = bf16[32,36,1152]{2,1,0:T(8,128)(2,1)} async-done(((bf16[1,36,1152]{2,1,0:T(8,128)(2,1)}), bf16[32,36,1152]{2,1,0:T(8,128)(2,1)}) %all-gather.11.cloned.1.call-update) | async-done | bytes 2654224 | tf_op jit(solution)/shard_map/all_gather | solution.py:117
  184.3 5.2 reshape.386
  189.5 78.8 %all-gather.15.cloned.1.call-done = bf16[32,36,1152]{2,1,0:T(8,128)(2,1)} async-done(((bf16[1,36,1152]{2,1,0:T(8,128)(2,1)}), bf16[32,36,1152]{2,1,0:T(8,128)(2,1)}) %all-gather.15.cloned.1.call-update) | async-done | bytes 2654224 | tf_op jit(solution)/shard_map/all_gather | solution.py:119
  268.3 3.6 reshape.388
  276.8 3.3 fusion.112
  281.5 89.5 %all-gather.13.cloned.1.call-done = bf16[32,36,3456]{2,1,0:T(8,128)(2,1)} async-done(((bf16[1,36,3456]{2,1,0:T(8,128)(2,1)}), bf16[32,36,3456]{2,1,0:T(8,128)(2,1)}) %all-gather.13.cloned.1.call-update) | async-done | bytes 7962640 | tf_op jit(solution)/shard_map/all_gather | solution.py:118
  370.9 12.4 %reshape.387 = bf16[1152,3456,1]{1,0,2:T(8,128)(2,1)} reshape(bf16[32,36,3456]{2,1,0:T(8,128)(2,1)} %all-gather.13.cloned.1.call-done) | data formatting | bytes 15925248
  383.4 7.8 %convolution_convert_fusion.1 = bf16[64,4,3456]{2,0,1:T(8,128)(2,1)} fusion(bf16[1152,3456,1]{1,0,2:T(8,128)(2,1)} %reshape.387, f32[64,4,1152]{2,0,1:T(8,128)} %copy-done.4, f32[64,1152]{1,0:T(8,128)} %get-tuple-element.21, f32[64,1152]{1,0:T(8,128)} %get-tuple-element.22, f32[64,4]{0,1:T(4,128)S(1)} %add_rsqrt_fusion.13, ...), kind=kOutput, calls=%fused_computation.9 | convolution fusion | flops 2040791040 | bytes 11503616 | tf_op jit(solution)/shard_map/dot_general | solution.py:70
  391.1 7.7 %reshape.356 = bf16[64,4,3,16,72]{4,3,2,0,1:T(8,128)(2,1)} reshape(bf16[64,4,3456]{2,0,1:T(8,128)(2,1)} %convolution_convert_fusion.1) | data formatting | bytes 3538944 | tf_op jit(solution)/shard_map/reshape | solution.py:71
  406.6 3.1 reshape.357
  413.3 14.0 %all_to_all.100 = bf16[64,4,16]{2,1,0:T(4,128)(2,1)S(1)} all-to-all(bf16[64,4,16]{2,1,0:T(4,128)(2,1)S(1)} %copy.107), channel_id=1, replica_groups=mesh['frame'=32,'space'=8] {'frame'}, dimensions={0} | all-to-all | bytes 16384 | tf_op jit(solution)/shard_map/all_to_all | solution.py:95
  427.4 23.9 %all_gather.27 = bf16[2,1024,16]{2,1,0:T(8,128)(2,1)S(1)} all-gather(bf16[2,128,16]{2,1,0:T(8,128)(2,1)S(1)} %bitcast.223), channel_id=1, replica_groups=mesh['frame'=32,'space'=8] {'space'}, dimensions={1}, use_global_device_ids=true | all-gather | bytes 73728 | tf_op jit(solution)/shard_map/all_gather | solution.py:134
  453.8 3.0 fusion.26
  460.1 3.1 fusion.32
  463.4 13.3 %all_to_all.101 = bf16[8,128,288]{1,2,0:T(8,128)(2,1)} all-to-all(bf16[8,128,288]{1,2,0:T(8,128)(2,1)S(1)} %copy.111), channel_id=1, replica_groups=mesh['frame'=32,'space'=8] {'space'}, dimensions={0} | all-to-all | bytes 1179648 | tf_op jit(solution)/shard_map/all_to_all | solution.py:138
  479.7 12.5 %all-to-all-start.5 = ((bf16[2,128,1152]{2,0,1:T(2,128)(2,1)}), bf16[2,128,1152]{2,0,1:T(2,128)(2,1)}, u32[]{:S(2)}, u32[]{:S(2)}) async-start(bf16[2,128,1152]{2,0,1:T(2,128)(2,1)} %copy.112), calls=%async_computation.5 | async-start | bytes 1179648 | tf_op jit(solution)/shard_map/all_to_all | solution.py:91
  493.7 17.8 %all-to-all-done.5 = bf16[2,128,1152]{2,0,1:T(2,128)(2,1)} async-done(((bf16[2,128,1152]{2,0,1:T(2,128)(2,1)}), bf16[2,128,1152]{2,0,1:T(2,128)(2,1)}, u32[]{:S(2)}, u32[]{:S(2)}) %all-to-all-start.5) | async-done | bytes 589856 | tf_op jit(solution)/shard_map/all_to_all | solution.py:91
  516.5 3.4 fusion.115
  520.9 7.2 %convolution_convert_fusion = bf16[64,4,3456]{2,0,1:T(8,128)(2,1)} fusion(bf16[1152,3456,1]{1,0,2:T(8,128)(2,1)} %reshape.387, f32[64,4,1152]{2,0,1:T(8,128)S(1)} %get-tuple-element.48, f32[64,4]{0,1:T(4,128)S(1)} %add_rsqrt_fusion.11, f32[64,4]{0,1:T(4,128)S(1)} %broadcast_multiply_fusion.3, f32[64,1152]{1,0:T(8,128)S(1)} %copy-done.7, ...), kind=kOutput, calls=%fused_computation.8 | convolution fusion | flops 2040791040 | bytes 11503616 | tf_op jit(solution)/shard_map/dot_general | solution.py:70
  528.1 7.7 %reshape.361 = bf16[64,4,3,16,72]{4,3,2,0,1:T(8,128)(2,1)} reshape(bf16[64,4,3456]{2,0,1:T(8,128)(2,1)} %convolution_convert_fusion) | data formatting | bytes 3538944 | tf_op jit(solution)/shard_map/reshape | solution.py:71
  553.1 16.0 %all_to_all.102 = f32[32,1,384]{2,1,0:T(1,128)} all-to-all(f32[32,1,384]{2,1,0:T(1,128)} %reshape.399), channel_id=1, replica_groups=mesh['frame'=32,'space'=8] {'frame'}, dimensions={0} | all-to-all | bytes 98304 | tf_op jit(solution)/shard_map/all_to_all | solution.py:95
  (172 shorter events, 92.6 us)
Async XLA Ops:
  7.2 32.3 %copy-start = (bf16[256,6912]{1,0:T(8,128)(2,1)S(1)}, bf16[256,6912]{1,0:T(8,128)(2,1)}, u32[]{:S(2)}) copy-start(bf16[256,6912]{1,0:T(8,128)(2,1)} %param.17) | copy-start | bytes 10616836
  7.2 90.9 %all-gather.9.cloned.1.call-start = ((), (), s32[]{:S(2)}) async-start(), calls=%async_computation.7 | async-start | bytes 2365440 | tf_op jit(solution)/shard_map/all_gather | solution.py:116
  13.2 171.1 %all-gather.11.cloned.1.call-start = ((), (), s32[]{:S(2)}) async-start(), calls=%async_computation.8 | async-start | bytes 3041280 | tf_op jit(solution)/shard_map/all_gather | solution.py:117
  14.0 254.3 %all-gather.15.cloned.1.call-start = ((), (), s32[]{:S(2)}) async-start(), calls=%async_computation.10 | async-start | bytes 3041280 | tf_op jit(solution)/shard_map/all_gather | solution.py:119
  14.7 356.2 %all-gather.13.cloned.1.call-start = ((), (), s32[]{:S(2)}) async-start(), calls=%async_computation.9 | async-start | bytes 9123840 | tf_op jit(solution)/shard_map/all_gather | solution.py:118
  40.2 21.0 %copy-start.6 = (bf16[16,1152]{1,0:T(8,128)(2,1)S(1)}, bf16[16,1152]{1,0:T(8,128)(2,1)}, u32[]{:S(2)}) copy-start(bf16[16,1152]{1,0:T(8,128)(2,1)} %param.18) | copy-start | bytes 110596
  41.2 61.1 %copy-start.18 = (f32[1152]{0:T(1024)}, f32[1152]{0:T(1024)S(1)}, u32[]{:S(2)}) copy-start(f32[1152]{0:T(1024)S(1)} %get-tuple-element.58) | copy-start | bytes 13828
  62.1 2.1 copy-start.2
  114.5 5.2 copy-start.17
  115.6 36.4 %copy-start.24 = (s32[64]{0:T(128)S(1)}, s32[64]{0:T(128)}, u32[]{:S(2)}) copy-start(s32[64]{0:T(128)} %get-tuple-element.12) | copy-start | bytes 772
  115.6 36.4 %copy-start.26 = (s32[64]{0:T(128)S(1)}, s32[64]{0:T(128)}, u32[]{:S(2)}) copy-start(s32[64]{0:T(128)} %copy-done.25) | copy-start | bytes 772
  115.6 36.5 %copy-start.20 = (f32[1,128,16]{1,2,0:T(8,128)S(1)}, f32[1,128,16]{1,2,0:T(8,128)}, u32[]{:S(2)}) copy-start(f32[1,128,16]{1,2,0:T(8,128)} %param.13) | copy-start | bytes 24580
  115.6 36.8 %copy-start.21 = (s32[2]{0:T(128)S(1)}, s32[2]{0:T(128)}, u32[]{:S(2)}) copy-start(s32[2]{0:T(128)} %param.16) | copy-start | bytes 28
  115.6 14.3 %all-to-all-start.1 = ((bf16[8,128,288]{1,2,0:T(8,128)(2,1)}), bf16[8,128,288]{1,2,0:T(8,128)(2,1)S(1)}, u32[]{:S(2)}, u32[]{:S(2)}) async-start(bf16[8,128,288]{1,2,0:T(8,128)(2,1)} %copy.97), calls=%async_computation.1 | async-start | bytes 1179648 | tf_op jit(solution)/shard_map/all_to_all | solution.py:138
  129.8 16.9 %all-to-all-start = ((f32[32,1,128]{2,1,0:T(1,128)}), f32[32,1,128]{2,1,0:T(1,128)S(1)}, u32[]{:S(2)}, u32[]{:S(2)}) async-start(f32[32,1,128]{2,1,0:T(1,128)} %reshape.397), calls=%async_computation | async-start | bytes 32768 | tf_op jit(solution)/shard_map/all_to_all | solution.py:91
  146.8 125.1 %all-to-all-start.2 = ((bf16[2,128,1152]{2,0,1:T(2,128)(2,1)}), bf16[2,128,1152]{2,0,1:T(2,128)(2,1)}, u32[]{:S(2)}, u32[]{:S(2)}) async-start(bf16[2,128,1152]{2,0,1:T(2,128)(2,1)} %copy.98), calls=%async_computation.2 | async-start | bytes 1179648 | tf_op jit(solution)/shard_map/all_to_all | solution.py:91
  152.0 2.5 copy-start.22
  152.3 260.7 %copy-start.11 = (f32[1,4,16]{0,2,1:T(8,128)}, f32[1,4,16]{0,2,1:T(8,128)S(1)}, u32[]{:S(2)}) copy-start(f32[1,4,16]{0,2,1:T(8,128)S(1)} %copy.133) | copy-start | bytes 772
  280.2 1.1 copy-start.4
  409.7 2.8 copy-start.15
  413.0 39.2 %copy-start.13 = (f32[64,4,16]{0,2,1:T(8,128)}, f32[64,4,16]{0,2,1:T(8,128)S(1)}, u32[]{:S(2)}) copy-start(f32[64,4,16]{0,2,1:T(8,128)S(1)} %fusion.54) | copy-start | bytes 49156
  413.1 39.1 %copy-start.9 = (f32[63,4,16]{0,2,1:T(8,128)}, f32[63,4,16]{0,2,1:T(8,128)S(1)}, u32[]{:S(2)}) copy-start(f32[63,4,16]{0,2,1:T(8,128)S(1)} %slice_add_fusion.1) | copy-start | bytes 48388
  452.2 1.6 copy-start.5
  452.2 1.6 copy-start.19
  479.7 31.8 %all-to-all-start.5 = ((bf16[2,128,1152]{2,0,1:T(2,128)(2,1)}), bf16[2,128,1152]{2,0,1:T(2,128)(2,1)}, u32[]{:S(2)}, u32[]{:S(2)}) async-start(bf16[2,128,1152]{2,0,1:T(2,128)(2,1)} %copy.112), calls=%async_computation.5 | async-start | bytes 1179648 | tf_op jit(solution)/shard_map/all_to_all | solution.py:91
  516.5 4.4 copy-start.7
  516.5 4.4 copy-start.8
  545.9 2.7 copy-start.10
  545.9 2.7 copy-start.12
  545.9 2.7 copy-start.16
  545.9 2.7 copy-start.23
  548.3 31.9 %copy-start.1 = (bf16[256,6912]{1,0:T(8,128)(2,1)S(1)}, bf16[256,6912]{1,0:T(8,128)(2,1)}, u32[]{:S(2)}) copy-start(bf16[256,6912]{1,0:T(8,128)(2,1)} %param.17) | copy-start | bytes 10616836
  (3 other events, 2.4 us)
Sparse Core Ops, SparseCore 0:
  13.3 84.7 all-gather.8
  100.8 83.4 all-gather.10
  187.0 81.2 all-gather.14
  270.9 99.9 all-gather.12

commit v2 on v1

--- a/solution.py
+++ b/solution.py
@@ -3,6 +3,8 @@
 import jax
 import jax.numpy as jnp
 from jax import lax
+from jax.experimental import pallas as pl
+from jax.experimental.pallas import tpu as pltpu
 from jax.sharding import PartitionSpec as P
 
 HEADS = 16
@@ -10,6 +12,11 @@
 WIN = 16
 STEPS = 2
 GROUPS = 4
+LANES = 128
+SUB = 8
+BLOCK = 256
+SHARPEN = HEAD ** (-0.5) * math.log2(math.e)
+VMEM_BYTES = 56 * 2**20
 
 
 epsilon = 1e-06
@@ -19,13 +26,6 @@
     center = values - jnp.mean(values, -1, keepdims=True)
     spread = jnp.mean(center * center, -1, keepdims=True)
     return center * lax.rsqrt(spread + epsilon)
-
-
-def head_norm(values):
-    wide = values.astype(jnp.float32)
-    return (wide * lax.rsqrt(jnp.mean(wide * wide, -1, keepdims=True) + epsilon)).astype(
-        jnp.bfloat16
-    )
 
 
 def lookup_table(indices, table):
@@ -41,50 +41,141 @@
     return jnp.dot(features, time_proj, preferred_element_type=jnp.float32)
 
 
-def softmax_rows(scores):
-    raised = jnp.exp(scores)
-    return (raised / jnp.sum(raised, -1, keepdims=True)).astype(jnp.bfloat16)
+def head_scale(values):
+    return lax.rsqrt(jnp.mean(values * values, -1, keepdims=True) + epsilon)
+
+
+def one_column(rows):
+    lane = lax.broadcasted_iota(jnp.int32, (rows, LANES - HEAD), 1)
+    return jnp.where(lane == 0, 1.0, 0.0).astype(jnp.bfloat16)
+
+
+def contract_last(left, right):
+    return lax.dot_general(
+        left, right, (((1,), (1,)), ((), ())), preferred_element_type=jnp.float32
+    )
+
+
+def spatial_kernel(tokens, embed, shift, scale, weights, out, triple, qs, ks, vs):
+    rows, local_heads = tokens.shape[0], HEADS // GROUPS
+    for first in range(0, rows, BLOCK):
+        here = pl.ds(first, BLOCK)
+        hidden = jnp.dot(tokens[here, :], embed[...], preferred_element_type=jnp.float32)
+        normed = layer_norm(hidden) * (1.0 + scale[...]) + shift[...]
+        triple[...] = jnp.dot(
+            normed.astype(jnp.bfloat16), weights[...], preferred_element_type=jnp.float32
+        )
+        for head in range(local_heads):
+            query = triple[:, head * HEAD : (head + 1) * HEAD]
+            key = triple[:, (local_heads + head) * HEAD : (local_heads + head + 1) * HEAD]
+            value = triple[:, (2 * local_heads + head) * HEAD : (2 * local_heads + head + 1) * HEAD]
+            qs[head, here, :] = (query * (head_scale(query) * SHARPEN)).astype(jnp.bfloat16)
+            ks[head, here, :] = (key * head_scale(key)).astype(jnp.bfloat16)
+            vs[head, here, :HEAD] = value.astype(jnp.bfloat16)
+            vs[head, here, HEAD:] = one_column(BLOCK)
+    for first in range(0, rows, BLOCK):
+        here = pl.ds(first, BLOCK)
+        for head in range(local_heads):
+            raised = jnp.exp2(contract_last(qs[head, here, :], ks[head])).astype(jnp.bfloat16)
+            mix = jnp.dot(raised, vs[head], preferred_element_type=jnp.float32)
+            mix = mix[:, :HEAD] / mix[:, HEAD : HEAD + 1]
+            out[here, head * HEAD : (head + 1) * HEAD] = mix.astype(jnp.bfloat16)
 
 
 def spatial_block(tokens, embed_in, shift, scale, weights):
-    hidden = jnp.dot(tokens, embed_in, preferred_element_type=jnp.float32)
-    normed = (layer_norm(hidden) * (1.0 + scale) + shift).astype(jnp.bfloat16)
-    triple = jnp.dot(normed, weights, preferred_element_type=jnp.float32).astype(jnp.bfloat16)
-    split = triple.reshape(triple.shape[0], 3, HEADS // GROUPS, HEAD)
-    queries = head_norm(split[:, 0])
-    keys = head_norm(split[:, 1])
-    scores = jnp.einsum(
-        "qhd,khd->hqk", queries, keys, preferred_element_type=jnp.float32
-    ) * HEAD ** (-0.5)
-    weights = softmax_rows(scores)
-    mixed = jnp.einsum("hqk,khd->qhd", weights, split[:, 2], preferred_element_type=jnp.float32)
-    return mixed.astype(jnp.bfloat16).reshape(triple.shape[0], -1)
+    rows, local_heads = tokens.shape[0], HEADS // GROUPS
+    return pl.pallas_call(
+        spatial_kernel,
+        out_shape=jax.ShapeDtypeStruct((rows, local_heads * HEAD), jnp.bfloat16),
+        in_specs=[pl.BlockSpec(memory_space=pltpu.VMEM)] * 5,
+        out_specs=pl.BlockSpec(memory_space=pltpu.VMEM),
+        scratch_shapes=[
+            pltpu.VMEM((BLOCK, 3 * local_heads * HEAD), jnp.float32),
+            pltpu.VMEM((local_heads, rows, HEAD), jnp.bfloat16),
+            pltpu.VMEM((local_heads, rows, HEAD), jnp.bfloat16),
+            pltpu.VMEM((local_heads, rows, LANES), jnp.bfloat16),
+        ],
+        compiler_params=pltpu.CompilerParams(vmem_limit_bytes=VMEM_BYTES),
+        name="spatial",
+    )(tokens, embed_in, shift, scale, weights)
+
+
+def temporal_kernel(
+    offset, mixed, latent, gate_s, shift_t, scale_t, gate_t,
+    embed_in, spatial_out, proj, out, embed_out, velocity, triple, mix,
+):
+    rows, frames = mixed.shape[0], gate_s.shape[0]
+    tokens = rows // frames
+    width = HEADS * HEAD
+
+    def spread(mod):
+        wide = jnp.broadcast_to(
+            mod.reshape(frames // SUB, 1, SUB, width), (frames // SUB, tokens, SUB, width)
+        )
+        return wide.reshape(rows, width)
+
+    hidden_in = jnp.dot(
+        latent[...].astype(jnp.bfloat16), embed_in[...], preferred_element_type=jnp.float32
+    )
+    back = jnp.dot(mixed[...], spatial_out[...], preferred_element_type=jnp.float32)
+    hidden = hidden_in + spread(gate_s[...]) * back
+    normed = layer_norm(hidden) * (1.0 + spread(scale_t[...])) + spread(shift_t[...])
+    triple[...] = jnp.dot(
+        normed.astype(jnp.bfloat16), proj[...], preferred_element_type=jnp.float32
+    )
+
+    def place(index):
+        block, rest = index // (tokens * SUB), index % (tokens * SUB)
+        frame = block * SUB + rest % SUB
+        return (frame + WIN - offset[0]) // WIN, rest // SUB
+
+    window_row, token_row = place(lax.broadcasted_iota(jnp.int32, (rows, rows), 0))
+    window_col, token_col = place(lax.broadcasted_iota(jnp.int32, (rows, rows), 1))
+    same = (window_row == window_col) & (token_row == token_col)
+    ones = one_column(rows)
+    for head in range(HEADS):
+        query = triple[:, head * HEAD : (head + 1) * HEAD]
+        key = triple[:, width + head * HEAD : width + (head + 1) * HEAD]
+        value = triple[:, 2 * width + head * HEAD : 2 * width + (head + 1) * HEAD]
+        query = (query * (head_scale(query) * SHARPEN)).astype(jnp.bfloat16)
+        key = (key * head_scale(key)).astype(jnp.bfloat16)
+        value = jnp.concatenate([value.astype(jnp.bfloat16), ones], -1)
+        raised = jnp.where(same, jnp.exp2(contract_last(query, key)), 0.0).astype(jnp.bfloat16)
+        part = jnp.dot(raised, value, preferred_element_type=jnp.float32)
+        part = part[:, :HEAD] / part[:, HEAD : HEAD + 1]
+        mix[:, head * HEAD : (head + 1) * HEAD] = part.astype(jnp.bfloat16)
+    forth = jnp.dot(mix[...], out[...], preferred_element_type=jnp.float32)
+    hidden = hidden + spread(gate_t[...]) * forth
+    velocity[...] = jnp.dot(
+        layer_norm(hidden).astype(jnp.bfloat16), embed_out[...], preferred_element_type=jnp.float32
+    )
 
 
 def temporal_block(mixed, latent, mods, offset, embed_in, spatial_out, proj, out, embed_out):
-    gate_s, shift_t, scale_t, gate_t = [mod[:, None, :] for mod in mods]
     frames, tokens = mixed.shape[:2]
-    hidden_in = jnp.dot(latent.astype(jnp.bfloat16), embed_in, preferred_element_type=jnp.float32)
-    hidden = hidden_in + gate_s * jnp.dot(mixed, spatial_out, preferred_element_type=jnp.float32)
-    normed = (layer_norm(hidden) * (1.0 + scale_t) + shift_t).astype(jnp.bfloat16)
-    triple = jnp.dot(normed, proj, preferred_element_type=jnp.float32).astype(jnp.bfloat16)
-    split = triple.reshape(frames, tokens, 3, HEADS, HEAD)
-    queries = head_norm(split[:, :, 0])
-    keys = head_norm(split[:, :, 1])
-    window = (jnp.arange(frames, dtype=jnp.int32) + WIN - offset) // WIN
-    same = window[:, None] == window[None, :]
-    scores = jnp.einsum(
-        "fthd,gthd->thfg", queries, keys, preferred_element_type=jnp.float32
-    ) * HEAD ** (-0.5)
-    weights = softmax_rows(jnp.where(same[None, None], scores, -1e30))
-    mixed = jnp.einsum(
-        "thfg,gthd->fthd", weights, split[:, :, 2], preferred_element_type=jnp.float32
-    )
-    mixed = mixed.astype(jnp.bfloat16).reshape(frames, tokens, HEADS * HEAD)
-    hidden = hidden + gate_t * jnp.dot(mixed, out, preferred_element_type=jnp.float32)
-    return jnp.dot(
-        layer_norm(hidden).astype(jnp.bfloat16), embed_out, preferred_element_type=jnp.float32
-    )
+
+    def fold(value):
+        parts = value.reshape(frames // SUB, SUB, tokens, -1)
+        return jnp.moveaxis(parts, 1, 2).reshape(frames * tokens, -1)
+
+    velocity = pl.pallas_call(
+        temporal_kernel,
+        out_shape=jax.ShapeDtypeStruct((frames * tokens, latent.shape[-1]), jnp.float32),
+        in_specs=[pl.BlockSpec(memory_space=pltpu.SMEM)]
+        + [pl.BlockSpec(memory_space=pltpu.VMEM)] * 11,
+        out_specs=pl.BlockSpec(memory_space=pltpu.VMEM),
+        scratch_shapes=[
+            pltpu.VMEM((frames * tokens, 3 * HEADS * HEAD), jnp.float32),
+            pltpu.VMEM((frames * tokens, HEADS * HEAD), jnp.bfloat16),
+        ],
+        compiler_params=pltpu.CompilerParams(vmem_limit_bytes=VMEM_BYTES),
+        name="temporal",
+    )(
+        offset[None], fold(mixed), fold(latent), *mods,
+        embed_in, spatial_out, proj, out, embed_out,
+    )
+    velocity = velocity.reshape(frames // SUB, tokens, SUB, -1)
+    return jnp.moveaxis(velocity, 1, 2).reshape(frames, tokens, -1)
 
 
 def to_tokens(values):

time: 597 us -> 580 us (0.972)
  Pallas kernels: 0 us -> 67.3 us
  matrix products: 57.9 us -> 0.74 us
  waiting for transfers between devices: 265 us -> 251 us
    pallas_call x0 -> x4, Pallas kernels: none -> 67.3 us  [the longest x2 36.2 us: temporal_block(): pl.pallas_call(temporal_kernel, out_shape=jax.ShapeDtypeStruct((frames *...]
    dot_general x22 -> x0, matrix products: 57.2 us -> none  [the longest x2 14.9 us: temporal_block(): jnp.dot(normed, proj, preferred_element_type=jnp.float32)]
    all_gather x1, waiting for transfers between devices: 26.6 us -> 11.2 us  [local(): spatial_back = lax.all_gather(spatial_out, 'frame', axis=0, tiled=True)]
    reshape x4 -> x6, local copies, waits for them, and re-layouts: 21 us -> 10.8 us  [the longest x2 4.46 us: local(): parts = mixed.reshape(8, -1, mixed.shape[-1])]
    all_to_all x8 -> x5, local copies, waits for them, and re-layouts: 10.7 us -> 4.12 us  [to_tokens(): lax.all_to_all(values, 'frame', split_axis=1, concat_axis=0, tiled=True)]
    unnamed x71 -> x33, local copies, waits for them, and re-layouts: 40.4 us -> 45.5 us
  transfers between devices with their start and end apart: 8 -> 8, of which waited for: 7 -> 7; matrix products, arithmetic and copies ran while one was open for 8% -> 9% of each run, Pallas kernels for 0% -> 3%
where the time goes in v2:
time: 580 us; the launch traced here: 574 us
  waiting for transfers between devices  251 us (43%)
  blocking collectives  106 us (18%)
  local copies, waits for them, and re-layouts  92.5 us (16%)
  Pallas kernels  67.3 us (12%)
  starting transfers between devices  29.3 us (5%)
  between operations  14.9 us (3%)
  other arithmetic  12.2 us (2%)
    all_gather x1, waiting for transfers between devices, local(): temporal_full = lax.all_gather(temporal_proj, 'frame', axis=0, tiled=True)  95.3 us
    all_gather x1, waiting for transfers between devices, local(): temporal_back = lax.all_gather(temporal_out, 'frame', axis=0, tiled=True)  77.8 us
    unnamed x33, local copies, waits for them, and re-layouts  45.5 us
    all_gather x2, blocking collectives, local(): whole = lax.all_gather(by_frame, 'space', axis=1, tiled=True)  44 us
    pallas_call x2, Pallas kernels, temporal_block(): pl.pallas_call(temporal_kernel, out_shape=jax.ShapeDtypeStruct((frames *...  36.2 us
    all_gather x1, waiting for transfers between devices, local(): lax.all_gather(own.reshape(own.shape[0], -1), 'frame', axis=0, tiled=True)  34.1 us
    pallas_call x2, Pallas kernels, spatial_block(): pl.pallas_call(spatial_kernel, out_shape=jax.ShapeDtypeStruct((rows, loca...  31.1 us
    all_to_all x2, blocking collectives, to_frames(): lax.all_to_all(values, 'frame', split_axis=0, concat_axis=1, tiled=True)  30.1 us
  transfers between devices with their start and end apart: 8, of which 7 were waited for; matrix products, arithmetic and copies ran while one was open for 9% of the time, Pallas kernels for 3%

profile of v2, /device:TPU:1, one launch (start us, length us, event | category | flops | bytes accessed | tf_op | source)
XLA Modules:
  0.0 573.9 jit_solution(5355126118682217079)
XLA Ops:
  7.2 2.1 reshape.87
  9.3 2.2 dynamic-slice_reduce_fusion
  18.1 18.5 %all-reduce = s32[64]{0:T(128)S(1)} all-reduce(s32[64]{0:T(128)S(1)} %dynamic-update-slice), channel_id=1, replica_groups=mesh['frame'=32,'space'=8] {'frame'}, use_global_device_ids=true, to_apply=%add | all-reduce | flops 64 | bytes 512
  39.2 19.9 %all_gather.22 = bf16[2,1024,16]{1,2,0:T(8,128)(2,1)S(1)} all-gather(bf16[2,128,16]{1,2,0:T(8,128)(2,1)S(1)} %convert_element_type.27), channel_id=1, replica_groups=mesh['frame'=32,'space'=8] {'space'}, dimensions={1}, use_global_device_ids=true | all-gather | bytes 73728 | tf_op jit(solution)/shard_map/all_gather | solution.py:225
  64.0 34.1 %all-gather.9.cloned.1.call-done = bf16[32,36,864]{2,1,0:T(8,128)(2,1)} async-done(((bf16[1,36,864]{2,1,0:T(8,128)(2,1)}), bf16[32,36,864]{2,1,0:T(8,128)(2,1)}) %all-gather.9.cloned.1.call-update) | async-done | bytes 1990672 | tf_op jit(solution)/shard_map/all_gather | solution.py:207
  98.1 4.3 reshape.111.weights
  102.4 15.5 %spatial.2 = bf16[1024,288]{1,0:T(8,128)(2,1)} custom-call(bf16[1024,16]{1,0:T(8,128)(2,1)} %bitcast.82, bf16[16,1152]{1,0:T(8,128)(2,1)} %embed_in.3, f32[1,1152]{1,0:T(1,128)} %get-tuple-element.30.shift, f32[1,1152]{1,0:T(1,128)} %get-tuple-element.29.scale, bf16[1152,864]{1,0:T(8,128)(2,1)} %reshape.111.weights), custom_call_target="tpu_custom_call" | custom-call | tf_op jit(solution)/shard_map/spatial/pallas_call | solution.py:87
  117.9 2.2 copy.131
  120.1 4.2 all-to-all-start.1
  126.8 7.7 %all-to-all-done.1 = bf16[8,128,288]{1,2,0:T(8,128)(2,1)} async-done(((bf16[8,128,288]{1,2,0:T(8,128)(2,1)}), bf16[8,128,288]{1,2,0:T(8,128)(2,1)}, u32[]{:S(2)}, u32[]{:S(2)}) %all-to-all-start.1) | async-done | bytes 589856 | tf_op jit(solution)/shard_map/all_to_all | solution.py:229
  134.5 7.5 %all-to-all-start = ((f32[32,1,128]{2,1,0:T(1,128)}), f32[32,1,128]{2,1,0:T(1,128)S(1)}, u32[]{:S(2)}, u32[]{:S(2)}) async-start(f32[32,1,128]{2,1,0:T(1,128)} %reshape.123), calls=%async_computation | async-start | bytes 32768 | tf_op jit(solution)/shard_map/all_to_all | solution.py:182
  142.1 3.0 copy.132
  145.0 6.3 %all-to-all-done = f32[32,1,128]{2,1,0:T(1,128)S(1)} async-done(((f32[32,1,128]{2,1,0:T(1,128)}), f32[32,1,128]{2,1,0:T(1,128)S(1)}, u32[]{:S(2)}, u32[]{:S(2)}) %all-to-all-start) | async-done | bytes 16416 | tf_op jit(solution)/shard_map/all_to_all | solution.py:182
  151.3 5.6 all-to-all-start.2
  172.7 11.2 %all-gather.11.cloned.1.call-done = bf16[32,36,1152]{2,1,0:T(8,128)(2,1)} async-done(((bf16[1,36,1152]{2,1,0:T(8,128)(2,1)}), bf16[32,36,1152]{2,1,0:T(8,128)(2,1)}) %all-gather.11.cloned.1.call-update) | async-done | bytes 2654224 | tf_op jit(solution)/shard_map/all_gather | solution.py:208
  184.0 5.2 reshape.113.spatial_out
  189.1 77.8 %all-gather.15.cloned.1.call-done = bf16[32,36,1152]{2,1,0:T(8,128)(2,1)} async-done(((bf16[1,36,1152]{2,1,0:T(8,128)(2,1)}), bf16[32,36,1152]{2,1,0:T(8,128)(2,1)}) %all-gather.15.cloned.1.call-update) | async-done | bytes 2654224 | tf_op jit(solution)/shard_map/all_gather | solution.py:210
  267.0 5.2 reshape.117.out
  274.3 95.3 %all-gather.13.cloned.1.call-done = bf16[32,36,3456]{2,1,0:T(8,128)(2,1)} async-done(((bf16[1,36,3456]{2,1,0:T(8,128)(2,1)}), bf16[32,36,3456]{2,1,0:T(8,128)(2,1)}) %all-gather.13.cloned.1.call-update) | async-done | bytes 7962640 | tf_op jit(solution)/shard_map/all_gather | solution.py:209
  369.6 12.4 %reshape.115.proj = bf16[1152,3456]{1,0:T(8,128)(2,1)} reshape(bf16[32,36,3456]{2,1,0:T(8,128)(2,1)} %all-gather.13.cloned.1.call-done) | data formatting | bytes 15925248
  382.1 18.1 %temporal.2 = f32[256,16]{1,0:T(8,128)} custom-call(s32[1]{0:T(128)} %get-tuple-element.27.offset, bf16[256,1152]{1,0:T(8,128)(2,1)} %bitcast.78, f32[256,16]{1,0:T(8,128)} %bitcast.90, f32[64,1152]{1,0:T(8,128)} %get-tuple-element.19.gate_s, f32[64,1152]{1,0:T(8,128)} %get-tuple-element.18.shift_t, f32[64,1152]{1,0:T(8,128)} %get-tuple-element.17.scale_t, ...), custom_call_target="tpu_custom_call" | custom-call | tf_op jit(solution)/shard_map/temporal/pallas_call | solution.py:161
  406.4 14.2 %all_to_all.94 = bf16[64,4,16]{2,1,0:T(4,128)(2,1)S(1)} all-to-all(bf16[64,4,16]{2,1,0:T(4,128)(2,1)} %copy.142), channel_id=1, replica_groups=mesh['frame'=32,'space'=8] {'frame'}, dimensions={0} | all-to-all | bytes 16384 | tf_op jit(solution)/shard_map/all_to_all | solution.py:186
  420.6 24.1 %all_gather.27 = bf16[2,1024,16]{2,1,0:T(8,128)(2,1)S(1)} all-gather(bf16[2,128,16]{2,1,0:T(8,128)(2,1)S(1)} %bitcast.95), channel_id=1, replica_groups=mesh['frame'=32,'space'=8] {'space'}, dimensions={1}, use_global_device_ids=true | all-gather | bytes 73728 | tf_op jit(solution)/shard_map/all_gather | solution.py:225
  445.4 15.6 %spatial.3 = bf16[1024,288]{1,0:T(8,128)(2,1)} custom-call(bf16[1024,16]{1,0:T(8,128)(2,1)} %dynamic-slice_bitcast_fusion.tokens, bf16[16,1152]{1,0:T(8,128)(2,1)} %embed_in.3, f32[1,1152]{1,0:T(1,128)} %get-tuple-element.30.shift, f32[1,1152]{1,0:T(1,128)} %get-tuple-element.29.scale, bf16[1152,864]{1,0:T(8,128)(2,1)} %reshape.111.weights), custom_call_target="tpu_custom_call" | custom-call | tf_op jit(solution)/shard_map/spatial/pallas_call | solution.py:87
  461.1 2.2 copy.145
  463.3 13.5 %all_to_all.95 = bf16[8,128,288]{1,2,0:T(8,128)(2,1)} all-to-all(bf16[8,128,288]{1,2,0:T(8,128)(2,1)} %copy.145), channel_id=1, replica_groups=mesh['frame'=32,'space'=8] {'space'}, dimensions={0} | all-to-all | bytes 1179648 | tf_op jit(solution)/shard_map/all_to_all | solution.py:229
  476.9 2.9 copy.146
  479.8 11.9 %all-to-all-start.5 = ((bf16[2,128,1152]{2,0,1:T(2,128)(2,1)}), bf16[2,128,1152]{2,0,1:T(2,128)(2,1)}, u32[]{:S(2)}, u32[]{:S(2)}) async-start(bf16[2,128,1152]{2,0,1:T(2,128)(2,1)} %copy.146), calls=%async_computation.5 | async-start | bytes 1179648 | tf_op jit(solution)/shard_map/all_to_all | solution.py:182
  494.8 16.4 %all-to-all-done.5 = bf16[2,128,1152]{2,0,1:T(2,128)(2,1)} async-done(((bf16[2,128,1152]{2,0,1:T(2,128)(2,1)}), bf16[2,128,1152]{2,0,1:T(2,128)(2,1)}, u32[]{:S(2)}, u32[]{:S(2)}) %all-to-all-start.5) | async-done | bytes 589856 | tf_op jit(solution)/shard_map/all_to_all | solution.py:182
  513.3 18.1 %temporal.3 = f32[256,16]{1,0:T(8,128)} custom-call(s32[1]{0:T(128)} %get-tuple-element.28.offset, bf16[256,1152]{1,0:T(8,128)(2,1)} %bitcast.77, f32[256,16]{1,0:T(8,128)} %bitcast.91, f32[64,1152]{1,0:T(8,128)} %get-tuple-element.19.gate_s, f32[64,1152]{1,0:T(8,128)} %get-tuple-element.18.shift_t, f32[64,1152]{1,0:T(8,128)} %get-tuple-element.17.scale_t, ...), custom_call_target="tpu_custom_call" | custom-call | tf_op jit(solution)/shard_map/temporal/pallas_call | solution.py:161
  540.1 15.9 %all_to_all.96 = f32[32,1,384]{2,1,0:T(1,128)} all-to-all(f32[32,1,384]{2,1,0:T(1,128)} %reshape.125), channel_id=1, replica_groups=mesh['frame'=32,'space'=8] {'frame'}, dimensions={0} | all-to-all | bytes 98304 | tf_op jit(solution)/shard_map/all_to_all | solution.py:186
  556.1 2.1 reduce.3
  (84 shorter events, 63.7 us)
Async XLA Ops:
  7.2 54.3 %copy-start = (bf16[256,6912]{1,0:T(8,128)(2,1)S(1)}, bf16[256,6912]{1,0:T(8,128)(2,1)}, u32[]{:S(2)}) copy-start(bf16[256,6912]{1,0:T(8,128)(2,1)} %param.17) | copy-start | bytes 10616836
  7.2 90.9 %all-gather.9.cloned.1.call-start = ((), (), s32[]{:S(2)}) async-start(), calls=%async_computation.7 | async-start | bytes 2365440 | tf_op jit(solution)/shard_map/all_gather | solution.py:207
  13.2 170.8 %all-gather.11.cloned.1.call-start = ((), (), s32[]{:S(2)}) async-start(), calls=%async_computation.8 | async-start | bytes 3041280 | tf_op jit(solution)/shard_map/all_gather | solution.py:208
  13.9 253.0 %all-gather.15.cloned.1.call-start = ((), (), s32[]{:S(2)}) async-start(), calls=%async_computation.10 | async-start | bytes 3041280 | tf_op jit(solution)/shard_map/all_gather | solution.py:210
  14.7 354.9 %all-gather.13.cloned.1.call-start = ((), (), s32[]{:S(2)}) async-start(), calls=%async_computation.9 | async-start | bytes 9123840 | tf_op jit(solution)/shard_map/all_gather | solution.py:209
  37.9 0.5 copy-start.7
  102.4 21.9 %copy-start.2 = (f32[2,128,16]{1,2,0:T(8,128)S(1)}, f32[2,128,16]{1,2,0:T(8,128)}, u32[]{:S(2)}) copy-start(f32[2,128,16]{1,2,0:T(8,128)} %param.12) | copy-start | bytes 49156
  120.1 14.4 %all-to-all-start.1 = ((bf16[8,128,288]{1,2,0:T(8,128)(2,1)}), bf16[8,128,288]{1,2,0:T(8,128)(2,1)}, u32[]{:S(2)}, u32[]{:S(2)}) async-start(bf16[8,128,288]{1,2,0:T(8,128)(2,1)} %copy.131), calls=%async_computation.1 | async-start | bytes 1179648 | tf_op jit(solution)/shard_map/all_to_all | solution.py:229
  134.5 16.8 %all-to-all-start = ((f32[32,1,128]{2,1,0:T(1,128)}), f32[32,1,128]{2,1,0:T(1,128)S(1)}, u32[]{:S(2)}, u32[]{:S(2)}) async-start(f32[32,1,128]{2,1,0:T(1,128)} %reshape.123), calls=%async_computation | async-start | bytes 32768 | tf_op jit(solution)/shard_map/all_to_all | solution.py:182
  151.3 13.2 %copy-start.3 = (f32[32,1,128]{2,1,0:T(1,128)}, f32[32,1,128]{2,1,0:T(1,128)S(1)}, u32[]{:S(2)}) copy-start(f32[32,1,128]{2,1,0:T(1,128)S(1)} %all-to-all-done) | copy-start | bytes 49156
  151.3 120.8 %all-to-all-start.2 = ((bf16[2,128,1152]{2,0,1:T(2,128)(2,1)}), bf16[2,128,1152]{2,0,1:T(2,128)(2,1)}, u32[]{:S(2)}, u32[]{:S(2)}) async-start(bf16[2,128,1152]{2,0,1:T(2,128)(2,1)} %copy.132), calls=%async_computation.2 | async-start | bytes 1179648 | tf_op jit(solution)/shard_map/all_to_all | solution.py:182
  157.6 0.5 copy-start.4
  168.3 0.6 copy-start.1
  382.1 21.3 %copy-start.6 = (f32[63]{0:T(128)S(1)}, f32[63]{0:T(128)}, u32[]{:S(2)}) copy-start(f32[63]{0:T(128)} %slice.24) | copy-start | bytes 760
  479.8 31.4 %all-to-all-start.5 = ((bf16[2,128,1152]{2,0,1:T(2,128)(2,1)}), bf16[2,128,1152]{2,0,1:T(2,128)(2,1)}, u32[]{:S(2)}, u32[]{:S(2)}) async-start(bf16[2,128,1152]{2,0,1:T(2,128)(2,1)} %copy.146), calls=%async_computation.5 | async-start | bytes 1179648 | tf_op jit(solution)/shard_map/all_to_all | solution.py:182
  513.3 21.3 %copy-start.5 = (f32[64]{0:T(128)S(1)}, f32[64]{0:T(128)}, u32[]{:S(2)}) copy-start(f32[64]{0:T(128)} %copy-done.4) | copy-start | bytes 772
Sparse Core Ops, SparseCore 0:
  13.3 84.7 all-gather.8
  100.8 83.1 all-gather.10
  186.6 80.2 all-gather.14
  269.6 99.9 all-gather.12

commit v3 on v2

--- a/solution.py
+++ b/solution.py
@@ -14,6 +14,9 @@
 GROUPS = 4
 LANES = 128
 SUB = 8
+TILE = 16
+TOP = 32
+MESH = pl.DeviceIdType.MESH
 BLOCK = 256
 SHARPEN = HEAD ** (-0.5) * math.log2(math.e)
 VMEM_BYTES = 56 * 2**20
@@ -39,6 +42,235 @@
     angles = time_value[:, None] * freqs[None, :]
     features = jnp.concatenate([jnp.cos(angles), jnp.sin(angles)], -1).astype(jnp.bfloat16)
     return jnp.dot(features, time_proj, preferred_element_type=jnp.float32)
+
+
+def sites():
+    frame, space = lax.axis_index("frame"), lax.axis_index("space")
+    return frame // 16, frame // 2 % 8, frame % 2, space // 2, space % 2
+
+
+def site_id(high, z, core, y, low):
+    return {"frame": high * 16 + z * 2 + core, "space": y * 2 + low}
+
+
+def meet(peers):
+    barrier = pltpu.get_barrier_semaphore()
+    for peer in peers:
+        pl.semaphore_signal(barrier, inc=1, device_id=peer, device_id_type=MESH)
+    pl.semaphore_wait(barrier, len(peers))
+
+
+def gather_kernel(
+    proj_s, out_s, proj_t, out_t, own_out, rest_out,
+    own_main, own_rest, main, rest, tail_s, tail_t, send_sem, recv_sem,
+):
+    high, z, core, y, low = sites()
+    up = site_id(high, (z + 1) % 8, core, y, low)
+    down = site_id(high, (z + 7) % 8, core, y, low)
+    across = site_id(1 - high, z, core, y, 1 - low)
+    north = site_id(high, z, core, (y + 1) % 4, low)
+    south = site_id(high, z, core, (y + 3) % 4, low)
+    sibling = site_id(high, z, 1 - core, y, low)
+    meet([up, down, across, north, south, sibling])
+
+    def slot(half, level):
+        return half * 16 + (level % 8) * 2 + core
+
+    mine = slot(high, z)
+    group = y
+    span = HEADS // GROUPS * HEAD
+    width = HEADS * HEAD
+    source = lax.broadcasted_iota(jnp.int32, (width, span), 0)
+    target = lax.broadcasted_iota(jnp.int32, (width, span), 1)
+    chosen = jnp.where(source == target + group * span, 1.0, 0.0).astype(jnp.bfloat16)
+    here = pl.ds(pl.multiple_of(mine * TOP, TOP), TOP)
+    for part in range(3):
+        piece = jnp.dot(
+            proj_s[:, part * width : (part + 1) * width], chosen, preferred_element_type=jnp.float32
+        )
+        own_main[here, part * span : (part + 1) * span] = piece[:TOP].astype(jnp.bfloat16)
+        tail_s[0:4, part * span : (part + 1) * span] = piece[TOP:]
+    own_main[here, 3 * span :] = jnp.zeros((TOP, own_main.shape[1] - 3 * span), jnp.bfloat16)
+    tail_s[0:4, 3 * span :] = jnp.zeros((4, tail_s.shape[1] - 3 * span), jnp.float32)
+    first = 0
+    for piece in (out_s, proj_t, out_t):
+        columns = pl.ds(first, piece.shape[1])
+        main[here, columns] = piece[:TOP, :]
+        tail_t[0:4, columns] = piece[TOP:, :].astype(jnp.float32)
+        first += piece.shape[1]
+    tail_t[0:4, first:] = jnp.zeros((4, tail_t.shape[1] - first), jnp.float32)
+    below = pl.ds(pl.multiple_of(mine * TILE, TILE), TILE)
+    for packed, tail in ((own_rest, tail_s), (rest, tail_t)):
+        size = packed.shape[1]
+        quarters = [tail[0:4, a * size : (a + 1) * size] for a in range(4)]
+        packed[below, :] = jnp.concatenate(quarters, 0).astype(jnp.bfloat16)
+
+    arrays = ((own_main, TOP), (own_rest, TILE), (main, TOP), (rest, TILE))
+    started = []
+
+    def copies(kind, which, peer, index, half=None):
+        made = []
+        for number in (2 * kind, 2 * kind + 1):
+            array, rows = arrays[number]
+            first, count = which * rows, rows
+            if half is not None:
+                if rows == TOP:
+                    first, count = first + half * TILE, TILE
+                elif half == 1:
+                    continue
+            piece = array.at[pl.ds(pl.multiple_of(first, TILE), count), :]
+            made.append(
+                pltpu.make_async_remote_copy(
+                    src_ref=piece,
+                    dst_ref=piece,
+                    send_sem=send_sem.at[index, number],
+                    recv_sem=recv_sem.at[index, number],
+                    device_id=peer,
+                    device_id_type=MESH,
+                )
+            )
+        return made
+
+    def send(kind, which, peer, index, half=None):
+        for copy in copies(kind, which, peer, index, half):
+            copy.start()
+            started.append(copy)
+
+    def arrive(kind, which, peer, index, half=None):
+        for copy in copies(kind, which, peer, index, half):
+            copy.wait_recv()
+
+    HANDED, ACROSS = 16, 32
+    handed = ([], [])
+
+    def hand(kind, which):
+        send(kind, which, sibling, HANDED + len(handed[kind]))
+        handed[kind].append(which)
+
+    def ring(kind, reach):
+        for hop in range(1, 5):
+            half = (0, 1) if hop == 4 else (None, None)
+            lower, upper = slot(high, z + 8 - hop), slot(high, z + hop)
+            arrive(kind, lower, up, hop - 1, half[0])
+            if hop < 4:
+                send(kind, lower, up, hop, 0 if hop == 3 else None)
+            arrive(kind, upper, down, 4 + hop - 1, half[1])
+            if hop < 4:
+                send(kind, upper, down, 4 + hop, 1 if hop == 3 else None)
+                hand(kind, lower)
+                reach(hop, lower)
+            hand(kind, upper)
+            reach(hop, upper)
+
+    for kind in (0, 1):
+        send(kind, mine, up, 0)
+        send(kind, mine, down, 4)
+        hand(kind, mine)
+        if kind == 0:
+            send(kind, mine, across, ACROSS)
+
+    passed = [mine]
+
+    def pass_across(hop, which):
+        send(0, which, across, ACROSS + len(passed))
+        passed.append(which)
+
+    ring(0, pass_across)
+    for index, which in enumerate(passed):
+        other = which + 16 - 32 * high
+        arrive(0, other, across, ACROSS + index)
+        hand(0, other)
+
+    def two_across(hop, which):
+        if hop == 2 and len(handed[1]) == 5:
+            send(1, slot(high, z + y + 7), across, 8)
+        if hop == 4:
+            send(1, slot(high, z + y + 3), across, 9)
+
+    ring(1, two_across)
+    near, far = slot(1 - high, z + y + 7), slot(1 - high, z + y + 3)
+    before, after, opposite = (y + 3) % 4, (y + 1) % 4, (y + 2) % 4
+    for which, index in ((near, 0), (far, 1)):
+        arrive(1, which, across, 8 + index)
+        send(1, which, north, 10 + index)
+        send(1, which, south, 12 + index)
+        hand(1, which)
+    steps = (
+        (before, 7, north, 10, 14),
+        (after, 7, south, 12, None),
+        (after, 3, south, 13, 15),
+        (before, 3, north, 11, None),
+        (opposite, 7, north, 14, None),
+        (opposite, 3, south, 15, None),
+    )
+    for place, shift, way, index, onward in steps:
+        which = slot(1 - high, z + place + shift)
+        arrive(1, which, way, index)
+        if onward is not None:
+            send(1, which, way, onward)
+        hand(1, which)
+    for kind in (0, 1):
+        for index, which in enumerate(handed[kind]):
+            arrive(kind, which + 1 - 2 * core, sibling, HANDED + index)
+    for copy in started:
+        copy.wait_send()
+
+    for top, low_rows, whole in ((own_main, own_rest, own_out), (main, rest, rest_out)):
+        size = low_rows.shape[1]
+        for quarter in range(4):
+            lo, hi = quarter * size, min((quarter + 1) * size, whole.shape[1])
+            order = restore_order(quarter)
+
+            @pl.loop(0, 8)
+            def _(quad):
+                pieces = jnp.concatenate(
+                    [
+                        top[pl.ds(pl.multiple_of(quad * 4 * TOP, 4 * TOP), 4 * TOP), lo:hi],
+                        low_rows[pl.ds(pl.multiple_of(quad * 4 * TILE, 4 * TILE), 4 * TILE), : hi - lo],
+                    ],
+                    0,
+                )
+                rows = jnp.dot(order, pieces, preferred_element_type=jnp.float32)
+                whole[pl.ds(pl.multiple_of(quad * 144, 16), 144), lo:hi] = rows.astype(jnp.bfloat16)
+
+
+def restore_order(quarter):
+    row = lax.broadcasted_iota(jnp.int32, (144, 4 * TOP + 4 * TILE), 0)
+    column = lax.broadcasted_iota(jnp.int32, (144, 4 * TOP + 4 * TILE), 1)
+    device, inner = row // 36, row % 36
+    source = jnp.where(
+        inner < TOP, device * TOP + inner, 4 * TOP + device * TILE + quarter * 4 + inner - TOP
+    )
+    return jnp.where(source == column, 1.0, 0.0).astype(jnp.bfloat16)
+
+
+def gather_weights(spatial_proj, spatial_out, temporal_proj, temporal_out):
+    width = HEADS * HEAD
+    own, other = 7 * LANES, 5 * width
+    packed = (2 * LANES, 12 * LANES)
+    return pl.pallas_call(
+        gather_kernel,
+        out_shape=[
+            jax.ShapeDtypeStruct((width, own), jnp.bfloat16),
+            jax.ShapeDtypeStruct((width, other), jnp.bfloat16),
+        ],
+        in_specs=[pl.BlockSpec(memory_space=pltpu.VMEM)] * 4,
+        out_specs=[pl.BlockSpec(memory_space=pltpu.VMEM)] * 2,
+        scratch_shapes=[
+            pltpu.VMEM((32 * TOP, own), jnp.bfloat16),
+            pltpu.VMEM((32 * TILE, packed[0]), jnp.bfloat16),
+            pltpu.VMEM((32 * TOP, other), jnp.bfloat16),
+            pltpu.VMEM((32 * TILE, packed[1]), jnp.bfloat16),
+            pltpu.VMEM((SUB, 4 * packed[0]), jnp.float32),
+            pltpu.VMEM((SUB, 4 * packed[1]), jnp.float32),
+            pltpu.SemaphoreType.DMA((40, 4)),
+            pltpu.SemaphoreType.DMA((40, 4)),
+        ],
+        compiler_params=pltpu.CompilerParams(
+            collective_id=0, has_side_effects=True, vmem_limit_bytes=VMEM_BYTES
+        ),
+        name="gather",
+    )(spatial_proj, spatial_out, temporal_proj, temporal_out)
 
 
 def head_scale(values):
@@ -90,7 +322,7 @@
         in_specs=[pl.BlockSpec(memory_space=pltpu.VMEM)] * 5,
         out_specs=pl.BlockSpec(memory_space=pltpu.VMEM),
         scratch_shapes=[
-            pltpu.VMEM((BLOCK, 3 * local_heads * HEAD), jnp.float32),
+            pltpu.VMEM((BLOCK, weights.shape[1]), jnp.float32),
             pltpu.VMEM((local_heads, rows, HEAD), jnp.bfloat16),
             pltpu.VMEM((local_heads, rows, HEAD), jnp.bfloat16),
             pltpu.VMEM((local_heads, rows, LANES), jnp.bfloat16),
@@ -102,7 +334,7 @@
 
 def temporal_kernel(
     offset, mixed, latent, gate_s, shift_t, scale_t, gate_t,
-    embed_in, spatial_out, proj, out, embed_out, velocity, triple, mix,
+    embed_in, shared, embed_out, velocity, triple, mix,
 ):
     rows, frames = mixed.shape[0], gate_s.shape[0]
     tokens = rows // frames
@@ -117,11 +349,11 @@
     hidden_in = jnp.dot(
         latent[...].astype(jnp.bfloat16), embed_in[...], preferred_element_type=jnp.float32
     )
-    back = jnp.dot(mixed[...], spatial_out[...], preferred_element_type=jnp.float32)
+    back = jnp.dot(mixed[...], shared[:, :width], preferred_element_type=jnp.float32)
     hidden = hidden_in + spread(gate_s[...]) * back
     normed = layer_norm(hidden) * (1.0 + spread(scale_t[...])) + spread(shift_t[...])
     triple[...] = jnp.dot(
-        normed.astype(jnp.bfloat16), proj[...], preferred_element_type=jnp.float32
+        normed.astype(jnp.bfloat16), shared[:, width : 4 * width], preferred_element_type=jnp.float32
     )
 
     def place(index):
@@ -144,14 +376,14 @@
         part = jnp.dot(raised, value, preferred_element_type=jnp.float32)
         part = part[:, :HEAD] / part[:, HEAD : HEAD + 1]
         mix[:, head * HEAD : (head + 1) * HEAD] = part.astype(jnp.bfloat16)
-    forth = jnp.dot(mix[...], out[...], preferred_element_type=jnp.float32)
+    forth = jnp.dot(mix[...], shared[:, 4 * width :], preferred_element_type=jnp.float32)
     hidden = hidden + spread(gate_t[...]) * forth
     velocity[...] = jnp.dot(
         layer_norm(hidden).astype(jnp.bfloat16), embed_out[...], preferred_element_type=jnp.float32
     )
 
 
-def temporal_block(mixed, latent, mods, offset, embed_in, spatial_out, proj, out, embed_out):
+def temporal_block(mixed, latent, mods, offset, embed_in, shared, embed_out):
     frames, tokens = mixed.shape[:2]
 
     def fold(value):
@@ -162,7 +394,7 @@
         temporal_kernel,
         out_shape=jax.ShapeDtypeStruct((frames * tokens, latent.shape[-1]), jnp.float32),
         in_specs=[pl.BlockSpec(memory_space=pltpu.SMEM)]
-        + [pl.BlockSpec(memory_space=pltpu.VMEM)] * 11,
+        + [pl.BlockSpec(memory_space=pltpu.VMEM)] * 9,
         out_specs=pl.BlockSpec(memory_space=pltpu.VMEM),
         scratch_shapes=[
             pltpu.VMEM((frames * tokens, 3 * HEADS * HEAD), jnp.float32),
@@ -172,7 +404,7 @@
         name="temporal",
     )(
         offset[None], fold(mixed), fold(latent), *mods,
-        embed_in, spatial_out, proj, out, embed_out,
+        embed_in, shared, embed_out,
     )
     velocity = velocity.reshape(frames // SUB, tokens, SUB, -1)
     return jnp.moveaxis(velocity, 1, 2).reshape(frames, tokens, -1)
@@ -201,13 +433,8 @@
     embed_out,
 ):
     place, row = lax.axis_index("space"), lax.axis_index("frame")
-    which, group = place // GROUPS, place % GROUPS
-    heads = spatial_proj.reshape(-1, 3, GROUPS, HEADS // GROUPS * HEAD)
-    own = lax.dynamic_index_in_dim(heads, group, 2, keepdims=False)
-    spatial_own = lax.all_gather(own.reshape(own.shape[0], -1), "frame", axis=0, tiled=True)
-    spatial_back = lax.all_gather(spatial_out, "frame", axis=0, tiled=True)
-    temporal_full = lax.all_gather(temporal_proj, "frame", axis=0, tiled=True)
-    temporal_back = lax.all_gather(temporal_out, "frame", axis=0, tiled=True)
+    which = place % 2
+    spatial_own, shared = gather_weights(spatial_proj, spatial_out, temporal_proj, temporal_out)
     all_levels = lax.all_gather(levels, "frame", axis=0, tiled=True)
     time_value = lookup_table(all_levels, timesteps)
     earlier = lookup_table(all_levels - 1, timesteps)
@@ -227,17 +454,15 @@
         mixed = spatial_block(tokens, embed_in, shift_own, scale_own, spatial_own)
         parts = mixed.reshape(8, -1, mixed.shape[-1])
         parts = lax.all_to_all(parts, "space", split_axis=0, concat_axis=0)
-        parts = parts.reshape(2, GROUPS, parts.shape[1], -1)
-        parts = jnp.moveaxis(parts, 1, 2).reshape(2, parts.shape[2], -1)
+        parts = parts.reshape(GROUPS, 2, parts.shape[1], -1)
+        parts = jnp.transpose(parts, (1, 2, 0, 3)).reshape(2, parts.shape[2], -1)
         velocity = temporal_block(
             to_tokens(parts),
             latent,
             (gate_s, shift_t, scale_t, gate_t),
             window_offsets[step_index],
             embed_in,
-            spatial_back,
-            temporal_full,
-            temporal_back,
+            shared,
             embed_out,
         )
         outputs.append(velocity)

time: 580 us -> 431 us (0.74)
  waiting for transfers between devices: 251 us -> 34.3 us
  Pallas kernels: 67.3 us -> 180 us
  local copies, waits for them, and re-layouts: 92.5 us -> 62.5 us
  between operations: 14.9 us -> 1.7 us
    all_gather x4 -> x0, waiting for transfers between devices: 218 us -> none  [the longest x1 95.3 us: local(): temporal_full = lax.all_gather(temporal_proj, 'frame', axis=0, tiled=True)]
    pallas_call x0 -> x1, Pallas kernels: none -> 112 us  [gather_weights(): pl.pallas_call(gather_kernel, out_shape=[jax.ShapeDtypeStruct((width, own...]
    unnamed x33 -> x26, local copies, waits for them, and re-layouts: 45.5 us -> 16.2 us
  transfers between devices with their start and end apart: 8 -> 4, of which waited for: 7 -> 4; matrix products, arithmetic and copies ran while one was open for 9% -> 6% of each run, Pallas kernels for 3% -> 0%
where the time goes in v3:
time: 431 us; the launch traced here: 425 us
  Pallas kernels  180 us (42%)
  blocking collectives  107 us (25%)
  local copies, waits for them, and re-layouts  62.5 us (15%)
  waiting for transfers between devices  34.3 us (8%)
  starting transfers between devices  27.6 us (6%)
  other arithmetic  11.6 us (3%)
    pallas_call x1, Pallas kernels, gather_weights(): pl.pallas_call(gather_kernel, out_shape=[jax.ShapeDtypeStruct((width, own...  112 us
    all_gather x2, blocking collectives, local(): whole = lax.all_gather(by_frame, 'space', axis=1, tiled=True)  46.6 us
    pallas_call x2, Pallas kernels, temporal_block(): pl.pallas_call(temporal_kernel, out_shape=jax.ShapeDtypeStruct((frames *...  36.1 us
    pallas_call x2, Pallas kernels, spatial_block(): pl.pallas_call(spatial_kernel, out_shape=jax.ShapeDtypeStruct((rows, loca...  31.6 us
    all_to_all x2, blocking collectives, to_frames(): lax.all_to_all(values, 'frame', split_axis=0, concat_axis=1, tiled=True)  30.9 us
    all_to_all x3, waiting for transfers between devices, to_tokens(): lax.all_to_all(values, 'frame', split_axis=1, concat_axis=0, tiled=True)  25.7 us
    all_to_all x3, starting transfers between devices, to_tokens(): lax.all_to_all(values, 'frame', split_axis=1, concat_axis=0, tiled=True)  23.4 us
    unnamed x1, blocking collectives  18.5 us
  transfers between devices with their start and end apart: 4, of which 4 were waited for; matrix products, arithmetic and copies ran while one was open for 6% of the time, Pallas kernels for 0%

profile of v3, /device:TPU:1, one launch (start us, length us, event | category | flops | bytes accessed | tf_op | source)
XLA Modules:
  0.0 425.5 jit_solution(1887590273970038898)
XLA Ops:
  3.6 18.5 %all-reduce = s32[64]{0:T(128)S(1)} all-reduce(s32[64]{0:T(128)S(1)} %dynamic-update-slice), channel_id=1, replica_groups=mesh['frame'=32,'space'=8] {'frame'}, use_global_device_ids=true, to_apply=%add | all-reduce | flops 64 | bytes 512
  26.1 21.4 %all_gather.10 = bf16[2,1024,16]{1,2,0:T(8,128)(2,1)} all-gather(bf16[2,128,16]{1,2,0:T(8,128)(2,1)S(1)} %convert_element_type.27), channel_id=1, replica_groups=mesh['frame'=32,'space'=8] {'space'}, dimensions={1}, use_global_device_ids=true | all-gather | bytes 73728 | tf_op jit(solution)/shard_map/all_gather | solution.py:452
  51.9 111.9 %gather.1 = (bf16[1152,896]{1,0:T(8,128)(2,1)}, bf16[1152,5760]{1,0:T(8,128)(2,1)}) custom-call(bf16[36,3456]{1,0:T(8,128)(2,1)} %proj_s.1, bf16[36,1152]{1,0:T(8,128)(2,1)} %out_s.1, bf16[36,3456]{1,0:T(8,128)(2,1)} %proj_t.1, bf16[36,1152]{1,0:T(8,128)(2,1)} %out_t.1), custom_call_target="tpu_custom_call" | custom-call | tf_op jit(solution)/shard_map/gather/pallas_call | solution.py:251
  163.8 15.9 %spatial.2 = bf16[1024,288]{1,0:T(8,128)(2,1)} custom-call(bf16[1024,16]{1,0:T(8,128)(2,1)} %bitcast.79, bf16[16,1152]{1,0:T(8,128)(2,1)} %embed_in.3, f32[1,1152]{1,0:T(1,128)} %get-tuple-element.34.shift, f32[1,1152]{1,0:T(1,128)} %get-tuple-element.33.scale, bf16[1152,896]{1,0:T(8,128)(2,1)} %get-tuple-element.4.weights), custom_call_target="tpu_custom_call" | custom-call | tf_op jit(solution)/shard_map/spatial/pallas_call | solution.py:319
  179.7 2.2 copy.130
  181.9 4.2 all-to-all-start.1
  186.9 1.7 reshape.103
  188.6 8.6 %all-to-all-done.1 = bf16[8,128,288]{1,2,0:T(8,128)(2,1)} async-done(((bf16[8,128,288]{1,2,0:T(8,128)(2,1)}), bf16[8,128,288]{1,2,0:T(8,128)(2,1)}, u32[]{:S(2)}, u32[]{:S(2)}) %all-to-all-start.1) | async-done | bytes 589856 | tf_op jit(solution)/shard_map/all_to_all | solution.py:456
  197.2 6.3 %all-to-all-start = ((f32[32,1,128]{2,1,0:T(1,128)}), f32[32,1,128]{2,1,0:T(1,128)S(1)}, u32[]{:S(2)}, u32[]{:S(2)}) async-start(f32[32,1,128]{2,1,0:T(1,128)} %reshape.103), calls=%async_computation | async-start | bytes 32768 | tf_op jit(solution)/shard_map/all_to_all | solution.py:414
  203.6 1.9 copy.131
  205.5 3.0 copy.132
  208.5 4.4 %all-to-all-done = f32[32,1,128]{2,1,0:T(1,128)S(1)} async-done(((f32[32,1,128]{2,1,0:T(1,128)}), f32[32,1,128]{2,1,0:T(1,128)S(1)}, u32[]{:S(2)}, u32[]{:S(2)}) %all-to-all-start) | async-done | bytes 16416 | tf_op jit(solution)/shard_map/all_to_all | solution.py:414
  212.8 5.5 %all-to-all-start.2 = ((bf16[2,128,1152]{2,0,1:T(2,128)(2,1)}), bf16[2,128,1152]{2,0,1:T(2,128)(2,1)}, u32[]{:S(2)}, u32[]{:S(2)}) async-start(bf16[2,128,1152]{2,0,1:T(2,128)(2,1)} %copy.132), calls=%async_computation.2 | async-start | bytes 1179648 | tf_op jit(solution)/shard_map/all_to_all | solution.py:414
  218.3 1.7 copy.137.embed_out
  231.2 1.6 copy.164
  232.8 4.9 %all-to-all-done.2 = bf16[2,128,1152]{2,0,1:T(2,128)(2,1)} async-done(((bf16[2,128,1152]{2,0,1:T(2,128)(2,1)}), bf16[2,128,1152]{2,0,1:T(2,128)(2,1)}, u32[]{:S(2)}, u32[]{:S(2)}) %all-to-all-start.2) | async-done | bytes 589856 | tf_op jit(solution)/shard_map/all_to_all | solution.py:414
  239.9 18.1 %temporal.2 = f32[256,16]{1,0:T(8,128)} custom-call(s32[1]{0:T(128)} %get-tuple-element.31.offset, bf16[256,1152]{1,0:T(8,128)(2,1)} %bitcast.75, f32[256,16]{1,0:T(8,128)} %bitcast.88, f32[64,1152]{1,0:T(8,128)} %get-tuple-element.23.gate_s, f32[64,1152]{1,0:T(8,128)} %get-tuple-element.22.shift_t, f32[64,1152]{1,0:T(8,128)} %get-tuple-element.21.scale_t, ...), custom_call_target="tpu_custom_call" | custom-call | tf_op jit(solution)/shard_map/temporal/pallas_call | solution.py:393
  264.2 14.9 %all_to_all.94 = bf16[64,4,16]{2,1,0:T(4,128)(2,1)S(1)} all-to-all(bf16[64,4,16]{2,1,0:T(4,128)(2,1)} %copy.142), channel_id=1, replica_groups=mesh['frame'=32,'space'=8] {'frame'}, dimensions={0} | all-to-all | bytes 16384 | tf_op jit(solution)/shard_map/all_to_all | solution.py:418
  279.2 25.2 %all_gather.11 = bf16[2,1024,16]{2,1,0:T(8,128)(2,1)S(1)} all-gather(bf16[2,128,16]{2,1,0:T(8,128)(2,1)S(1)} %bitcast.91), channel_id=1, replica_groups=mesh['frame'=32,'space'=8] {'space'}, dimensions={1}, use_global_device_ids=true | all-gather | bytes 73728 | tf_op jit(solution)/shard_map/all_gather | solution.py:452
  305.1 15.7 %spatial.3 = bf16[1024,288]{1,0:T(8,128)(2,1)} custom-call(bf16[1024,16]{1,0:T(8,128)(2,1)} %dynamic-slice_bitcast_fusion.tokens, bf16[16,1152]{1,0:T(8,128)(2,1)} %embed_in.3, f32[1,1152]{1,0:T(1,128)} %get-tuple-element.34.shift, f32[1,1152]{1,0:T(1,128)} %get-tuple-element.33.scale, bf16[1152,896]{1,0:T(8,128)(2,1)} %get-tuple-element.4.weights), custom_call_target="tpu_custom_call" | custom-call | tf_op jit(solution)/shard_map/spatial/pallas_call | solution.py:319
  320.8 2.2 copy.145
  323.0 11.4 %all_to_all.95 = bf16[8,128,288]{1,2,0:T(8,128)(2,1)S(1)} all-to-all(bf16[8,128,288]{1,2,0:T(8,128)(2,1)} %copy.145), channel_id=1, replica_groups=mesh['frame'=32,'space'=8] {'space'}, dimensions={0} | all-to-all | bytes 1179648 | tf_op jit(solution)/shard_map/all_to_all | solution.py:456
  335.3 3.0 copy.147
  338.3 11.6 %all-to-all-start.5 = ((bf16[2,128,1152]{2,0,1:T(2,128)(2,1)}), bf16[2,128,1152]{2,0,1:T(2,128)(2,1)}, u32[]{:S(2)}, u32[]{:S(2)}) async-start(bf16[2,128,1152]{2,0,1:T(2,128)(2,1)} %copy.147), calls=%async_computation.5 | async-start | bytes 1179648 | tf_op jit(solution)/shard_map/all_to_all | solution.py:414
  353.0 16.4 %all-to-all-done.5 = bf16[2,128,1152]{2,0,1:T(2,128)(2,1)} async-done(((bf16[2,128,1152]{2,0,1:T(2,128)(2,1)}), bf16[2,128,1152]{2,0,1:T(2,128)(2,1)}, u32[]{:S(2)}, u32[]{:S(2)}) %all-to-all-start.5) | async-done | bytes 589856 | tf_op jit(solution)/shard_map/all_to_all | solution.py:414
  371.5 18.0 %temporal.3 = f32[256,16]{1,0:T(8,128)} custom-call(s32[1]{0:T(128)} %get-tuple-element.32.offset, bf16[256,1152]{1,0:T(8,128)(2,1)} %bitcast.74, f32[256,16]{1,0:T(8,128)} %bitcast.87, f32[64,1152]{1,0:T(8,128)} %get-tuple-element.23.gate_s, f32[64,1152]{1,0:T(8,128)} %get-tuple-element.22.shift_t, f32[64,1152]{1,0:T(8,128)} %get-tuple-element.21.scale_t, ...), custom_call_target="tpu_custom_call" | custom-call | tf_op jit(solution)/shard_map/temporal/pallas_call | solution.py:393
  391.1 1.6 copy.154
  394.9 1.6 copy.157
  396.6 1.7 reshape.105
  398.2 15.9 %all_to_all.96 = f32[32,1,384]{2,1,0:T(1,128)} all-to-all(f32[32,1,384]{2,1,0:T(1,128)} %reshape.105), channel_id=1, replica_groups=mesh['frame'=32,'space'=8] {'frame'}, dimensions={0} | all-to-all | bytes 98304 | tf_op jit(solution)/shard_map/all_to_all | solution.py:418
  414.2 2.2 reduce.1
  416.3 1.6 reshape.106
  (66 shorter events, 48.9 us)
Async XLA Ops:
  0.6 23.4 %copy-start = (bf16[256,6912]{1,0:T(8,128)(2,1)S(1)}, bf16[256,6912]{1,0:T(8,128)(2,1)}, u32[]{:S(2)}) copy-start(bf16[256,6912]{1,0:T(8,128)(2,1)} %param.17) | copy-start | bytes 10616836
  23.5 0.6 copy-start.6
  24.0 2.1 copy-start.1
  181.9 15.3 %all-to-all-start.1 = ((bf16[8,128,288]{1,2,0:T(8,128)(2,1)}), bf16[8,128,288]{1,2,0:T(8,128)(2,1)}, u32[]{:S(2)}, u32[]{:S(2)}) async-start(bf16[8,128,288]{1,2,0:T(8,128)(2,1)} %copy.130), calls=%async_computation.1 | async-start | bytes 1179648 | tf_op jit(solution)/shard_map/all_to_all | solution.py:456
  197.2 15.6 %all-to-all-start = ((f32[32,1,128]{2,1,0:T(1,128)}), f32[32,1,128]{2,1,0:T(1,128)S(1)}, u32[]{:S(2)}, u32[]{:S(2)}) async-start(f32[32,1,128]{2,1,0:T(1,128)} %reshape.103), calls=%async_computation | async-start | bytes 32768 | tf_op jit(solution)/shard_map/all_to_all | solution.py:414
  212.8 13.1 %copy-start.2 = (f32[32,1,128]{2,1,0:T(1,128)}, f32[32,1,128]{2,1,0:T(1,128)S(1)}, u32[]{:S(2)}) copy-start(f32[32,1,128]{2,1,0:T(1,128)S(1)} %all-to-all-done) | copy-start | bytes 49156
  212.8 24.8 %all-to-all-start.2 = ((bf16[2,128,1152]{2,0,1:T(2,128)(2,1)}), bf16[2,128,1152]{2,0,1:T(2,128)(2,1)}, u32[]{:S(2)}, u32[]{:S(2)}) async-start(bf16[2,128,1152]{2,0,1:T(2,128)(2,1)} %copy.132), calls=%async_computation.2 | async-start | bytes 1179648 | tf_op jit(solution)/shard_map/all_to_all | solution.py:414
  220.7 0.5 copy-start.3
  239.9 21.2 %copy-start.5 = (f32[63]{0:T(128)S(1)}, f32[63]{0:T(128)}, u32[]{:S(2)}) copy-start(f32[63]{0:T(128)} %slice.24) | copy-start | bytes 760
  338.3 31.1 %all-to-all-start.5 = ((bf16[2,128,1152]{2,0,1:T(2,128)(2,1)}), bf16[2,128,1152]{2,0,1:T(2,128)(2,1)}, u32[]{:S(2)}, u32[]{:S(2)}) async-start(bf16[2,128,1152]{2,0,1:T(2,128)(2,1)} %copy.147), calls=%async_computation.5 | async-start | bytes 1179648 | tf_op jit(solution)/shard_map/all_to_all | solution.py:414
  371.5 21.2 %copy-start.4 = (f32[64]{0:T(128)S(1)}, f32[64]{0:T(128)}, u32[]{:S(2)}) copy-start(f32[64]{0:T(128)} %copy-done.3) | copy-start | bytes 772

commit v4 on v3

--- a/solution.py
+++ b/solution.py
@@ -1,3 +1,4 @@
+import functools
 import math
 
 import jax
@@ -11,6 +12,7 @@
 HEAD = 72
 WIN = 16
 STEPS = 2
+PATCH = 16
 GROUPS = 4
 LANES = 128
 SUB = 8
@@ -36,12 +38,10 @@
     return jnp.sum(jnp.where(hits, table[None, :], 0), axis=1).astype(jnp.float32)
 
 
-def time_modulation(time_value, time_proj):
-    half = time_proj.shape[0] // 2
+def time_features(time_value, half):
     freqs = jnp.exp(-math.log(10000.0) * jnp.arange(half, dtype=jnp.float32) / half)
     angles = time_value[:, None] * freqs[None, :]
-    features = jnp.concatenate([jnp.cos(angles), jnp.sin(angles)], -1).astype(jnp.bfloat16)
-    return jnp.dot(features, time_proj, preferred_element_type=jnp.float32)
+    return jnp.concatenate([jnp.cos(angles), jnp.sin(angles)], -1).astype(jnp.bfloat16)
 
 
 def sites():
@@ -60,9 +60,33 @@
     pl.semaphore_wait(barrier, len(peers))
 
 
+def frame_peer(distance):
+    return {"frame": (lax.axis_index("frame") + distance) % 32, "space": lax.axis_index("space")}
+
+
+def swap_rows(source, landing, send_sem, recv_sem):
+    me = lax.axis_index("frame")
+    flying = []
+    for distance in range(1, 32):
+        peer = frame_peer(distance)
+        copy = pltpu.make_async_remote_copy(
+            src_ref=source.at[pl.ds(pl.multiple_of(peer["frame"] * SUB, SUB), SUB), :],
+            dst_ref=landing.at[pl.ds(pl.multiple_of(me * SUB, SUB), SUB), :],
+            send_sem=send_sem.at[distance - 1],
+            recv_sem=recv_sem.at[distance - 1],
+            device_id=peer,
+            device_id_type=MESH,
+        )
+        copy.start()
+        flying.append(copy)
+    here = pl.ds(pl.multiple_of(me * SUB, SUB), SUB)
+    landing[here, :] = source[here, :]
+    return flying
+
+
 def gather_kernel(
-    proj_s, out_s, proj_t, out_t, own_out, rest_out,
-    own_main, own_rest, main, rest, tail_s, tail_t, send_sem, recv_sem,
+    proj_s, out_s, proj_t, out_t, facts, own_out, rest_out, facts_out,
+    own_main, own_rest, main, rest, tail_s, tail_t, landing, send_sem, recv_sem, swap_send, swap_recv,
 ):
     high, z, core, y, low = sites()
     up = site_id(high, (z + 1) % 8, core, y, low)
@@ -71,7 +95,8 @@
     north = site_id(high, z, core, (y + 1) % 4, low)
     south = site_id(high, z, core, (y + 3) % 4, low)
     sibling = site_id(high, z, 1 - core, y, low)
-    meet([up, down, across, north, south, sibling])
+    meet([across, north, south] + [frame_peer(distance) for distance in range(1, 32)])
+    swapped = swap_rows(facts, landing, swap_send, swap_recv)
 
     def slot(half, level):
         return half * 16 + (level % 8) * 2 + core
@@ -214,6 +239,9 @@
             arrive(kind, which + 1 - 2 * core, sibling, HANDED + index)
     for copy in started:
         copy.wait_send()
+    for copy in swapped:
+        copy.wait()
+    facts_out[...] = landing[...]
 
     for top, low_rows, whole in ((own_main, own_rest, own_out), (main, rest, rest_out)):
         size = low_rows.shape[1]
@@ -244,7 +272,7 @@
     return jnp.where(source == column, 1.0, 0.0).astype(jnp.bfloat16)
 
 
-def gather_weights(spatial_proj, spatial_out, temporal_proj, temporal_out):
+def gather_weights(spatial_proj, spatial_out, temporal_proj, temporal_out, facts):
     width = HEADS * HEAD
     own, other = 7 * LANES, 5 * width
     packed = (2 * LANES, 12 * LANES)
@@ -253,9 +281,10 @@
         out_shape=[
             jax.ShapeDtypeStruct((width, own), jnp.bfloat16),
             jax.ShapeDtypeStruct((width, other), jnp.bfloat16),
+            jax.ShapeDtypeStruct(facts.shape, jnp.float32),
         ],
-        in_specs=[pl.BlockSpec(memory_space=pltpu.VMEM)] * 4,
-        out_specs=[pl.BlockSpec(memory_space=pltpu.VMEM)] * 2,
+        in_specs=[pl.BlockSpec(memory_space=pltpu.VMEM)] * 5,
+        out_specs=[pl.BlockSpec(memory_space=pltpu.VMEM)] * 3,
         scratch_shapes=[
             pltpu.VMEM((32 * TOP, own), jnp.bfloat16),
             pltpu.VMEM((32 * TILE, packed[0]), jnp.bfloat16),
@@ -263,14 +292,17 @@
             pltpu.VMEM((32 * TILE, packed[1]), jnp.bfloat16),
             pltpu.VMEM((SUB, 4 * packed[0]), jnp.float32),
             pltpu.VMEM((SUB, 4 * packed[1]), jnp.float32),
+            pltpu.VMEM(facts.shape, jnp.float32),
             pltpu.SemaphoreType.DMA((40, 4)),
             pltpu.SemaphoreType.DMA((40, 4)),
+            pltpu.SemaphoreType.DMA((31,)),
+            pltpu.SemaphoreType.DMA((31,)),
         ],
         compiler_params=pltpu.CompilerParams(
             collective_id=0, has_side_effects=True, vmem_limit_bytes=VMEM_BYTES
         ),
         name="gather",
-    )(spatial_proj, spatial_out, temporal_proj, temporal_out)
+    )(spatial_proj, spatial_out, temporal_proj, temporal_out, facts)
 
 
 def head_scale(values):
@@ -288,12 +320,49 @@
     )
 
 
-def spatial_kernel(tokens, embed, shift, scale, weights, out, triple, qs, ks, vs):
-    rows, local_heads = tokens.shape[0], HEADS // GROUPS
+def spatial_kernel(
+    latents, features, time_proj, embed, weights, out,
+    tokens, mixed, parts, stage, landing, triple, qs, ks, vs,
+    share_send, share_recv, part_send, part_recv, row_send, row_recv,
+):
+    high, z, core, y, low = sites()
+    place = y * 2 + low
+    width, local_heads = HEADS * HEAD, HEADS // GROUPS
+    span = local_heads * HEAD
+
+    def plane_peer(dy, a, b, c):
+        return site_id((high + b) % 2, z, (core + c) % 2, (y + dy) % 4, (low + a) % 2)
+
+    offsets = [(dy, a, b, c) for dy in range(4) for a in range(2) for b in range(2) for c in range(2)]
+    above = [site_id(high, (z + d) % 8, core, y, low) for d in range(1, 8)]
+    meet([plane_peer(*offset) for offset in offsets[1:]] + above)
+
+    shares = []
+    mine = pl.ds(pl.multiple_of(place * LANES, LANES), LANES)
+    for d in range(1, 8):
+        other = (place + d) % 8
+        copy = pltpu.make_async_remote_copy(
+            src_ref=latents.at[other % 2],
+            dst_ref=tokens.at[mine, :],
+            send_sem=share_send.at[d - 1],
+            recv_sem=share_recv.at[d - 1],
+            device_id={"frame": lax.axis_index("frame"), "space": other},
+            device_id_type=MESH,
+        )
+        copy.start()
+        shares.append(copy)
+    tokens[mine, :] = latents[low]
+    mods = jnp.dot(features[...], time_proj[:, : 2 * width], preferred_element_type=jnp.float32)
+    shift, scale = mods[:1, :width], 1.0 + mods[:1, width:]
+    mixed[:, span:] = jnp.zeros((mixed.shape[0], mixed.shape[1] - span), jnp.bfloat16)
+    for copy in shares:
+        copy.wait()
+
+    rows = tokens.shape[0]
     for first in range(0, rows, BLOCK):
         here = pl.ds(first, BLOCK)
-        hidden = jnp.dot(tokens[here, :], embed[...], preferred_element_type=jnp.float32)
-        normed = layer_norm(hidden) * (1.0 + scale[...]) + shift[...]
+        hidden = jnp.dot(tokens[here, :PATCH], embed[...], preferred_element_type=jnp.float32)
+        normed = layer_norm(hidden) * scale + shift
         triple[...] = jnp.dot(
             normed.astype(jnp.bfloat16), weights[...], preferred_element_type=jnp.float32
         )
@@ -305,61 +374,129 @@
             ks[head, here, :] = (key * head_scale(key)).astype(jnp.bfloat16)
             vs[head, here, :HEAD] = value.astype(jnp.bfloat16)
             vs[head, here, HEAD:] = one_column(BLOCK)
-    for first in range(0, rows, BLOCK):
-        here = pl.ds(first, BLOCK)
+
+    sent = []
+    own_part = pl.ds(pl.multiple_of((high * 4 + core * 2 + low) * 32, 32), 32)
+    for dy in range(4):
+        first = (y + dy) % 4 * BLOCK
+        here = pl.ds(pl.multiple_of(first, BLOCK), BLOCK)
         for head in range(local_heads):
             raised = jnp.exp2(contract_last(qs[head, here, :], ks[head])).astype(jnp.bfloat16)
             mix = jnp.dot(raised, vs[head], preferred_element_type=jnp.float32)
             mix = mix[:, :HEAD] / mix[:, HEAD : HEAD + 1]
-            out[here, head * HEAD : (head + 1) * HEAD] = mix.astype(jnp.bfloat16)
-
-
-def spatial_block(tokens, embed_in, shift, scale, weights):
-    rows, local_heads = tokens.shape[0], HEADS // GROUPS
+            mixed[here, head * HEAD : (head + 1) * HEAD] = mix.astype(jnp.bfloat16)
+        for index, (step, a, b, c) in enumerate(offsets):
+            if step != dy:
+                continue
+            target = (low + a) % 2 * 4 + (high + b) % 2 * 2 + (core + c) % 2
+            piece = pl.ds(pl.multiple_of(first + target * 32, 32), 32)
+            if index == 0:
+                parts[y, own_part, :] = mixed[piece, :]
+                continue
+            copy = pltpu.make_async_remote_copy(
+                src_ref=mixed.at[piece, :],
+                dst_ref=parts.at[y, own_part, :],
+                send_sem=part_send.at[index - 1],
+                recv_sem=part_recv.at[index - 1],
+                device_id=plane_peer(step, a, b, c),
+                device_id_type=MESH,
+            )
+            copy.start()
+            sent.append(copy)
+    for copy in sent:
+        copy.wait()
+
+    target = lax.broadcasted_iota(jnp.int32, (2 * LANES, 2 * LANES), 0)
+    source = lax.broadcasted_iota(jnp.int32, (2 * LANES, 2 * LANES), 1)
+    moved = target % 32 // 8 * 64 + target % 2 * 32 + target // 32 * 4 + target % 8 // 2
+    order = jnp.where(moved == source, 1.0, 0.0).astype(jnp.bfloat16)
+    for group in range(GROUPS):
+        piece = jnp.dot(order, parts[group], preferred_element_type=jnp.float32)
+        stage[:, group * span : (group + 1) * span] = piece[:, :span].astype(jnp.bfloat16)
+    flying = []
+    for d in range(1, 8):
+        for half in range(2):
+            origin = pl.ds(pl.multiple_of((z + d) % 8 * 32 + half * TILE, TILE), TILE)
+            goal = pl.ds(pl.multiple_of(half * LANES + z * TILE, TILE), TILE)
+            copy = pltpu.make_async_remote_copy(
+                src_ref=stage.at[origin, :],
+                dst_ref=landing.at[goal, :],
+                send_sem=row_send.at[d - 1, half],
+                recv_sem=row_recv.at[d - 1, half],
+                device_id=above[d - 1],
+                device_id_type=MESH,
+            )
+            copy.start()
+            flying.append(copy)
+    for half in range(2):
+        origin = pl.ds(pl.multiple_of(z * 32 + half * TILE, TILE), TILE)
+        goal = pl.ds(pl.multiple_of(half * LANES + z * TILE, TILE), TILE)
+        landing[goal, :] = stage[origin, :]
+    for copy in flying:
+        copy.wait()
+    out[...] = landing[...]
+
+
+def spatial_block(latents, features, time_proj, embed_in, weights):
+    width, local_heads, rows = HEADS * HEAD, HEADS // GROUPS, 8 * LANES
+    vmem = pl.BlockSpec(memory_space=pltpu.VMEM)
     return pl.pallas_call(
         spatial_kernel,
-        out_shape=jax.ShapeDtypeStruct((rows, local_heads * HEAD), jnp.bfloat16),
-        in_specs=[pl.BlockSpec(memory_space=pltpu.VMEM)] * 5,
-        out_specs=pl.BlockSpec(memory_space=pltpu.VMEM),
+        out_shape=jax.ShapeDtypeStruct((2 * LANES, width), jnp.bfloat16),
+        in_specs=[vmem] * 5,
+        out_specs=vmem,
         scratch_shapes=[
+            pltpu.VMEM((rows, LANES), jnp.bfloat16),
+            pltpu.VMEM((rows, 3 * LANES), jnp.bfloat16),
+            pltpu.VMEM((GROUPS, 2 * LANES, 3 * LANES), jnp.bfloat16),
+            pltpu.VMEM((2 * LANES, width), jnp.bfloat16),
+            pltpu.VMEM((2 * LANES, width), jnp.bfloat16),
             pltpu.VMEM((BLOCK, weights.shape[1]), jnp.float32),
             pltpu.VMEM((local_heads, rows, HEAD), jnp.bfloat16),
             pltpu.VMEM((local_heads, rows, HEAD), jnp.bfloat16),
             pltpu.VMEM((local_heads, rows, LANES), jnp.bfloat16),
+            pltpu.SemaphoreType.DMA((7,)),
+            pltpu.SemaphoreType.DMA((7,)),
+            pltpu.SemaphoreType.DMA((31,)),
+            pltpu.SemaphoreType.DMA((31,)),
+            pltpu.SemaphoreType.DMA((7, 2)),
+            pltpu.SemaphoreType.DMA((7, 2)),
         ],
-        compiler_params=pltpu.CompilerParams(vmem_limit_bytes=VMEM_BYTES),
+        compiler_params=pltpu.CompilerParams(
+            collective_id=1, has_side_effects=True, vmem_limit_bytes=VMEM_BYTES
+        ),
         name="spatial",
-    )(tokens, embed_in, shift, scale, weights)
+    )(latents, features, time_proj, embed_in, weights)
 
 
 def temporal_kernel(
-    offset, mixed, latent, gate_s, shift_t, scale_t, gate_t,
-    embed_in, shared, embed_out, velocity, triple, mix,
+    last, offset, mixed, facts, state, fresh, time_proj, embed_in, shared, embed_out, *rest,
 ):
-    rows, frames = mixed.shape[0], gate_s.shape[0]
-    tokens = rows // frames
-    width = HEADS * HEAD
-
-    def spread(mod):
-        wide = jnp.broadcast_to(
-            mod.reshape(frames // SUB, 1, SUB, width), (frames // SUB, tokens, SUB, width)
-        )
-        return wide.reshape(rows, width)
+    if last:
+        queue, velocities, outgoing, landing, triple, mix, send_sem, recv_sem = rest
+    else:
+        latents, outgoing, landing, triple, mix, send_sem, recv_sem = rest
+    meet([frame_peer(distance) for distance in range(1, 32)])
+    rows, width = mixed.shape[0], HEADS * HEAD
+    features = facts[:, LANES:].astype(jnp.bfloat16)
+
+    def mod(part):
+        columns = time_proj[:, part * width : (part + 1) * width]
+        return jnp.dot(features, columns, preferred_element_type=jnp.float32)
 
     hidden_in = jnp.dot(
-        latent[...].astype(jnp.bfloat16), embed_in[...], preferred_element_type=jnp.float32
+        state[:, :PATCH].astype(jnp.bfloat16), embed_in[...], preferred_element_type=jnp.float32
     )
     back = jnp.dot(mixed[...], shared[:, :width], preferred_element_type=jnp.float32)
-    hidden = hidden_in + spread(gate_s[...]) * back
-    normed = layer_norm(hidden) * (1.0 + spread(scale_t[...])) + spread(shift_t[...])
+    hidden = hidden_in + mod(2) * back
+    normed = layer_norm(hidden) * (1.0 + mod(4)) + mod(3)
     triple[...] = jnp.dot(
         normed.astype(jnp.bfloat16), shared[:, width : 4 * width], preferred_element_type=jnp.float32
     )
 
     def place(index):
-        block, rest = index // (tokens * SUB), index % (tokens * SUB)
-        frame = block * SUB + rest % SUB
-        return (frame + WIN - offset[0]) // WIN, rest // SUB
+        frame = index // SUB * 2 + index % 2
+        return (frame + WIN - offset[0]) // WIN, index % SUB // 2
 
     window_row, token_row = place(lax.broadcasted_iota(jnp.int32, (rows, rows), 0))
     window_col, token_col = place(lax.broadcasted_iota(jnp.int32, (rows, rows), 1))
@@ -377,45 +514,100 @@
         part = part[:, :HEAD] / part[:, HEAD : HEAD + 1]
         mix[:, head * HEAD : (head + 1) * HEAD] = part.astype(jnp.bfloat16)
     forth = jnp.dot(mix[...], shared[:, 4 * width :], preferred_element_type=jnp.float32)
-    hidden = hidden + spread(gate_t[...]) * forth
-    velocity[...] = jnp.dot(
+    hidden = hidden + mod(5) * forth
+    velocity = jnp.dot(
         layer_norm(hidden).astype(jnp.bfloat16), embed_out[...], preferred_element_type=jnp.float32
     )
-
-
-def temporal_block(mixed, latent, mods, offset, embed_in, shared, embed_out):
-    frames, tokens = mixed.shape[:2]
-
-    def fold(value):
-        parts = value.reshape(frames // SUB, SUB, tokens, -1)
-        return jnp.moveaxis(parts, 1, 2).reshape(frames * tokens, -1)
-
-    velocity = pl.pallas_call(
-        temporal_kernel,
-        out_shape=jax.ShapeDtypeStruct((frames * tokens, latent.shape[-1]), jnp.float32),
+    stepped = state[:, :PATCH] + facts[:, PATCH : PATCH + 1] * velocity
+    outgoing[:, 3 * PATCH :] = jnp.zeros((rows, LANES - 3 * PATCH), jnp.float32)
+    if last:
+        outgoing[:, :PATCH] = stepped
+        outgoing[:, PATCH : 2 * PATCH] = state[:, PATCH : 2 * PATCH]
+        outgoing[:, 2 * PATCH : 3 * PATCH] = velocity
+    else:
+        outgoing[:, PATCH : 2 * PATCH] = velocity
+        outgoing[:, 2 * PATCH : 3 * PATCH] = jnp.zeros((rows, PATCH), jnp.float32)
+        outgoing[:, :PATCH] = stepped
+        wide = outgoing[...]
+        index = lax.broadcasted_iota(jnp.int32, (rows, LANES), 0)
+        first = index % 2 == 0
+        ahead = jnp.where(first, pltpu.roll(wide, rows - 1, 0), pltpu.roll(wide, rows - 7, 0))
+        tail = jnp.concatenate([fresh[...]] * (rows // SUB), 0)
+        ahead = jnp.where(first | (index < rows - SUB), ahead, tail)
+        outgoing[:, :PATCH] = ahead[:, :PATCH]
+    for copy in swap_rows(outgoing, landing, send_sem, recv_sem):
+        copy.wait()
+    if last:
+        for j in range(2):
+            piece = landing[pl.ds(j, LANES, stride=2), :]
+            queue[j] = piece[:, :PATCH]
+            velocities[0, j] = piece[:, PATCH : 2 * PATCH]
+            velocities[1, j] = piece[:, 2 * PATCH : 3 * PATCH]
+    else:
+        target = lax.broadcasted_iota(jnp.int32, (LANES, 2 * LANES), 0)
+        source = lax.broadcasted_iota(jnp.int32, (LANES, 2 * LANES), 1)
+        moved = target // 64 * 16 + target % 32 // 4 * 2 + target // 32 % 2
+        moved = moved * SUB + target % 4 * 2
+        lane = lax.broadcasted_iota(jnp.int32, (rows, LANES), 1)
+        clean = jnp.where(lane < PATCH, landing[...], 0.0).astype(jnp.bfloat16)
+        for j in range(2):
+            order = jnp.where(moved + j == source, 1.0, 0.0).astype(jnp.bfloat16)
+            latents[j] = jnp.dot(order, clean, preferred_element_type=jnp.float32).astype(
+                jnp.bfloat16
+            )
+
+
+def temporal_block(last, offset, mixed, facts, state, fresh, time_proj, embed_in, shared, embed_out):
+    width, rows = HEADS * HEAD, mixed.shape[0]
+    vmem = pl.BlockSpec(memory_space=pltpu.VMEM)
+    local = (2, LANES, PATCH)
+    if last:
+        shapes = [
+            jax.ShapeDtypeStruct(local, jnp.float32),
+            jax.ShapeDtypeStruct((STEPS, *local), jnp.float32),
+        ]
+        scratch = [pltpu.VMEM((rows, LANES), jnp.float32)]
+    else:
+        shapes = [
+            jax.ShapeDtypeStruct((2, LANES, LANES), jnp.bfloat16),
+            jax.ShapeDtypeStruct((rows, LANES), jnp.float32),
+        ]
+        scratch = []
+    return pl.pallas_call(
+        functools.partial(temporal_kernel, last),
+        out_shape=shapes,
         in_specs=[pl.BlockSpec(memory_space=pltpu.SMEM)]
-        + [pl.BlockSpec(memory_space=pltpu.VMEM)] * 9,
-        out_specs=pl.BlockSpec(memory_space=pltpu.VMEM),
-        scratch_shapes=[
-            pltpu.VMEM((frames * tokens, 3 * HEADS * HEAD), jnp.float32),
-            pltpu.VMEM((frames * tokens, HEADS * HEAD), jnp.bfloat16),
+        + [vmem] * 8,
+        out_specs=[vmem] * 2,
+        scratch_shapes=scratch
+        + [
+            pltpu.VMEM((rows, LANES), jnp.float32),
+            pltpu.VMEM((rows, 3 * width), jnp.float32),
+            pltpu.VMEM((rows, width), jnp.bfloat16),
+            pltpu.SemaphoreType.DMA((31,)),
+            pltpu.SemaphoreType.DMA((31,)),
         ],
-        compiler_params=pltpu.CompilerParams(vmem_limit_bytes=VMEM_BYTES),
+        compiler_params=pltpu.CompilerParams(
+            collective_id=3 if last else 2, has_side_effects=True, vmem_limit_bytes=VMEM_BYTES
+        ),
         name="temporal",
-    )(
-        offset[None], fold(mixed), fold(latent), *mods,
-        embed_in, shared, embed_out,
-    )
-    velocity = velocity.reshape(frames // SUB, tokens, SUB, -1)
-    return jnp.moveaxis(velocity, 1, 2).reshape(frames, tokens, -1)
-
-
-def to_tokens(values):
-    return lax.all_to_all(values, "frame", split_axis=1, concat_axis=0, tiled=True)
-
-
-def to_frames(values):
-    return lax.all_to_all(values, "frame", split_axis=0, concat_axis=1, tiled=True)
+    )(offset[None], mixed, facts, state, fresh, time_proj, embed_in, shared, embed_out)
+
+
+def row_facts(latents, step_size, features):
+    count, tokens, size = latents.shape
+    rows = latents.reshape(count, 32, tokens // 32, size)
+    rows = jnp.transpose(rows, (1, 2, 0, 3)).reshape(2 * tokens, size)
+    steps = jnp.broadcast_to(step_size[None], (tokens, count)).reshape(2 * tokens, 1)
+    wide = jnp.broadcast_to(features.astype(jnp.float32)[None], (tokens, count, 2 * LANES))
+    gap = jnp.zeros((2 * tokens, LANES - size - 1), jnp.float32)
+    return jnp.concatenate([rows, steps, gap, wide.reshape(2 * tokens, 2 * LANES)], -1)
+
+
+def plane_rows(latents):
+    rows = latents.astype(jnp.bfloat16).reshape(2, 2, 8, 2, 4, PATCH)
+    rows = jnp.swapaxes(rows, 2, 3).reshape(2, LANES, PATCH)
+    return jnp.pad(rows, ((0, 0), (0, 0), (0, LANES - PATCH)))
 
 
 def local(
@@ -432,50 +624,33 @@
     temporal_out,
     embed_out,
 ):
-    place, row = lax.axis_index("space"), lax.axis_index("frame")
-    which = place % 2
-    spatial_own, shared = gather_weights(spatial_proj, spatial_out, temporal_proj, temporal_out)
-    all_levels = lax.all_gather(levels, "frame", axis=0, tiled=True)
-    time_value = lookup_table(all_levels, timesteps)
-    earlier = lookup_table(all_levels - 1, timesteps)
-    step_size = (earlier - time_value) / 1000.0
-    modulation = time_modulation(time_value, time_proj)
-    shift_s, scale_s, gate_s, shift_t, scale_t, gate_t = jnp.split(modulation, 6, axis=-1)
-    frame = row * latents.shape[0] + which
-    shift_own = lax.dynamic_slice_in_dim(shift_s, frame, 1)
-    scale_own = lax.dynamic_slice_in_dim(scale_s, frame, 1)
-    latent = to_tokens(latents)
-    fresh = lax.dynamic_slice_in_dim(fresh_noise, row * latent.shape[1], latent.shape[1], 1)
-    by_frame = latents.astype(jnp.bfloat16)
-    outputs = []
+    which, row = lax.axis_index("space") % 2, lax.axis_index("frame")
+    time_value = lookup_table(levels, timesteps)
+    earlier = lookup_table(levels - 1, timesteps)
+    features = time_features(time_value, time_proj.shape[0] // 2)
+    facts = row_facts(latents, (earlier - time_value) / 1000.0, features)
+    spatial_own, shared, facts = gather_weights(
+        spatial_proj, spatial_out, temporal_proj, temporal_out, facts
+    )
+    own = jnp.broadcast_to(lax.dynamic_index_in_dim(features, which, 0), (TILE, 2 * LANES))
+    fresh = lax.dynamic_slice_in_dim(fresh_noise[0], row * 4, 4)
+    fresh = jnp.pad(jnp.repeat(fresh, 2, axis=0), ((0, 0), (0, LANES - PATCH)))
+    tokens, state = plane_rows(latents), facts[:, :LANES]
     for step_index in range(STEPS):
-        whole = lax.all_gather(by_frame, "space", axis=1, tiled=True)
-        tokens = lax.dynamic_index_in_dim(whole, which, 0, keepdims=False)
-        mixed = spatial_block(tokens, embed_in, shift_own, scale_own, spatial_own)
-        parts = mixed.reshape(8, -1, mixed.shape[-1])
-        parts = lax.all_to_all(parts, "space", split_axis=0, concat_axis=0)
-        parts = parts.reshape(GROUPS, 2, parts.shape[1], -1)
-        parts = jnp.transpose(parts, (1, 2, 0, 3)).reshape(2, parts.shape[2], -1)
-        velocity = temporal_block(
-            to_tokens(parts),
-            latent,
-            (gate_s, shift_t, scale_t, gate_t),
+        mixed = spatial_block(tokens, own, time_proj, embed_in, spatial_own)
+        tokens, state = temporal_block(
+            step_index == STEPS - 1,
             window_offsets[step_index],
+            mixed,
+            facts,
+            state,
+            fresh,
+            time_proj,
             embed_in,
             shared,
             embed_out,
         )
-        outputs.append(velocity)
-        stepped = latent + step_size[:, None, None] * velocity
-        if step_index + 1 < STEPS:
-            latent = jnp.concatenate([stepped[1:], fresh[step_index][None]], 0)
-            by_frame = to_frames(latent.astype(jnp.bfloat16))
-        else:
-            latent = stepped
-    result = to_frames(jnp.concatenate([latent] + outputs, -1))
-    size = latent.shape[-1]
-    queue = result[..., :size]
-    return (queue, jnp.stack([result[..., size : 2 * size], result[..., 2 * size :]]))
+    return tokens, state
 
 
 def solution(mesh):

time: 431 us -> 313 us (0.73)
  Pallas kernels: 180 us -> 294 us
  blocking collectives: 107 us -> 0 us
  local copies, waits for them, and re-layouts: 62.5 us -> 11.2 us
  waiting for transfers between devices: 34.3 us -> 0 us
  starting transfers between devices: 27.6 us -> 0 us
  other arithmetic: 11.6 us -> 2.62 us
    pallas_call x4, Pallas kernels: 67.7 us -> 173 us  [the longest x2 103 us: spatial_block(): pl.pallas_call(spatial_kernel, out_shape=jax.ShapeDtypeStruct((2 * LANES,...]
    all_gather x2 -> x0, blocking collectives: 46.6 us -> none  [local(): whole = lax.all_gather(by_frame, 'space', axis=1, tiled=True)]
    all_to_all x3 -> x0, blocking collectives: 42.3 us -> none  [the longest x2 30.9 us: to_frames(): lax.all_to_all(values, 'frame', split_axis=0, concat_axis=1, tiled=True)]
    all_to_all x4 -> x0, waiting for transfers between devices: 34.3 us -> none  [the longest x3 25.7 us: to_tokens(): lax.all_to_all(values, 'frame', split_axis=1, concat_axis=0, tiled=True)]
    all_to_all x4 -> x0, starting transfers between devices: 27.6 us -> none  [the longest x3 23.4 us: to_tokens(): lax.all_to_all(values, 'frame', split_axis=1, concat_axis=0, tiled=True)]
    unnamed x1 -> x0, blocking collectives: 18.5 us -> none
    reshape x8 -> x2, local copies, waits for them, and re-layouts: 16.7 us -> 0.26 us  [the longest x1 0.18 us: row_facts(): wide.reshape(2 * tokens, 2 * LANES)]
    unnamed x26 -> x4, local copies, waits for them, and re-layouts: 16.2 us -> 2.47 us
  transfers between devices with their start and end apart: 4 -> 0, of which waited for: 4 -> 0; matrix products, arithmetic and copies ran while one was open for 6% -> 0% of each run, Pallas kernels for 0% -> 0%
where the time goes in v4:
time: 313 us; the launch traced here: 309 us
  Pallas kernels  294 us (94%)
  local copies, waits for them, and re-layouts  11.2 us (4%)
    pallas_call x1, Pallas kernels, gather_weights(): pl.pallas_call(gather_kernel, out_shape=[jax.ShapeDtypeStruct((width, own...  122 us
    pallas_call x2, Pallas kernels, spatial_block(): pl.pallas_call(spatial_kernel, out_shape=jax.ShapeDtypeStruct((2 * LANES,...  103 us
    pallas_call x2, Pallas kernels, temporal_block(): pl.pallas_call(functools.partial(temporal_kernel, last), out_shape=shapes...  69.5 us

profile of v4, /device:TPU:1, one launch (start us, length us, event | category | flops | bytes accessed | tf_op | source)
XLA Modules:
  0.0 309.2 jit_solution(13179497113241580202)
XLA Ops:
  0.6 0.0 copy-start
  0.7 0.7 broadcast_add_fusion
  1.3 0.9 fusion.3
  2.2 0.1 fusion
  2.4 1.3 fusion.4
  3.7 0.1 pad.12.clone
  3.8 0.6 broadcast_in_dim.52.features
  4.4 0.0 copy-done
  4.4 0.1 constant_dynamic-slice_fusion
  4.5 0.1 copy.36
  4.6 0.6 pad.9.fresh
  5.2 0.1 reshape.90
  5.3 0.8 copy.31
  6.1 0.6 pad.8.latents
  6.8 0.1 copy.34
  6.9 0.1 broadcast_in_dim.55
  7.0 0.2 reshape.88
  7.1 0.9 pad_maximum_fusion.facts
  8.0 1.6 copy.37.embed_out
  9.7 121.7 %gather.1 = (bf16[1152,896]{1,0:T(8,128)(2,1)}, bf16[1152,5760]{1,0:T(8,128)(2,1)}, f32[256,384]{1,0:T(8,128)}) custom-call(bf16[36,3456]{1,0:T(8,128)(2,1)} %proj_s.1, bf16[36,1152]{1,0:T(8,128)(2,1)} %out_s.1, bf16[36,3456]{1,0:T(8,128)(2,1)} %proj_t.1, bf16[36,1152]{1,0:T(8,128)(2,1)} %out_t.1, f32[256,384]{1,0:T(8,128)} %pad_maximum_fusion.facts), custom_call_target="tpu_custom_call" | custom-call | tf_op jit(solution)/shard_map/gather/pallas_call | solution.py:279
  131.4 1.6 slice.11.state
  133.0 50.3 %spatial.2.mixed = bf16[256,1152]{1,0:T(8,128)(2,1)} custom-call(bf16[2,128,128]{2,1,0:T(8,128)(2,1)} %pad.8.latents, bf16[16,256]{1,0:T(8,128)(2,1)} %broadcast_in_dim.52.features, bf16[256,6912]{1,0:T(8,128)(2,1)} %time_proj.7, bf16[16,1152]{1,0:T(8,128)(2,1)} %embed_in.3, bf16[1152,896]{1,0:T(8,128)(2,1)} %get-tuple-element.7.weights), custom_call_target="tpu_custom_call" | custom-call | tf_op jit(solution)/shard_map/spatial/pallas_call | solution.py:443
  183.2 34.1 %temporal.2 = (bf16[2,128,128]{2,1,0:T(8,128)(2,1)}, f32[256,128]{1,0:T(8,128)}) custom-call(s32[1]{0:T(128)} %get-tuple-element.22.offset, bf16[256,1152]{1,0:T(8,128)(2,1)} %spatial.2.mixed, f32[256,384]{1,0:T(8,128)} %get-tuple-element.8.facts, f32[256,128]{1,0:T(8,128)} %slice.11.state, f32[8,128]{1,0:T(8,128)} %pad.9.fresh, ...), custom_call_target="tpu_custom_call" | custom-call | tf_op jit(solution)/shard_map/temporal/pallas_call | solution.py:576
  217.4 53.0 %spatial.3.mixed = bf16[256,1152]{1,0:T(8,128)(2,1)} custom-call(bf16[2,128,128]{2,1,0:T(8,128)(2,1)} %get-tuple-element.10.latents, bf16[16,256]{1,0:T(8,128)(2,1)} %broadcast_in_dim.52.features, bf16[256,6912]{1,0:T(8,128)(2,1)} %time_proj.7, bf16[16,1152]{1,0:T(8,128)(2,1)} %embed_in.3, bf16[1152,896]{1,0:T(8,128)(2,1)} %get-tuple-element.7.weights), custom_call_target="tpu_custom_call" | custom-call | tf_op jit(solution)/shard_map/spatial/pallas_call | solution.py:443
  270.4 35.3 %temporal.3 = (f32[2,128,16]{2,1,0:T(8,128)}, f32[2,2,128,16]{3,2,1,0:T(8,128)}) custom-call(s32[1]{0:T(128)} %get-tuple-element.23.offset, bf16[256,1152]{1,0:T(8,128)(2,1)} %spatial.3.mixed, f32[256,384]{1,0:T(8,128)} %get-tuple-element.8.facts, f32[256,128]{1,0:T(8,128)} %get-tuple-element.11.state, f32[8,128]{1,0:T(8,128)} %pad.9.fresh, ...), custom_call_target="tpu_custom_call" | custom-call | tf_op jit(solution)/shard_map/temporal/pallas_call | solution.py:576
  305.8 1.6 copy.39
  307.3 1.7 copy.40
  (10 shorter events, 0.1 us)
Async XLA Ops:
  0.6 3.8 %copy-start = (f32[1,128,16]{1,2,0:T(8,128)S(1)}, f32[1,128,16]{1,2,0:T(8,128)}, u32[]{:S(2)}) copy-start(f32[1,128,16]{1,2,0:T(8,128)} %param.13) | copy-start | bytes 24580

commit v5 on v1

v5 whole, which is shorter than its diff:
```python
import functools
import math

import jax
import jax.numpy as jnp
from jax import lax
from jax.experimental import pallas as pl
from jax.experimental.pallas import tpu as pltpu
from jax.sharding import PartitionSpec as P

HEADS = 16
HEAD = 72
WIN = 16
STEPS = 2
PATCH = 16
GROUPS = 4
LANES = 128
SUB = 8
TILE = 16
TOP = 32
MESH = pl.DeviceIdType.MESH
CHUNKS = ((0, 8), (8, 33), (33, 59))
HANDED, ACROSS = 16, 32
BLOCK = 256
SHARPEN = HEAD ** (-0.5) * math.log2(math.e)
VMEM_BYTES = 61 * 2**20


epsilon = 1e-06


def layer_norm(values):
    center = values - jnp.mean(values, -1, keepdims=True)
    spread = jnp.mean(center * center, -1, keepdims=True)
    return center * lax.rsqrt(spread + epsilon)


def lookup_table(indices, table):
    hits = indices[:, None] == jnp.arange(table.shape[0], dtype=jnp.int32)[None, :]
    return jnp.sum(jnp.where(hits, table[None, :], 0), axis=1).astype(jnp.float32)


def time_features(time_value, half):
    freqs = jnp.exp(-math.log(10000.0) * jnp.arange(half, dtype=jnp.float32) / half)
    angles = time_value[:, None] * freqs[None, :]
    return jnp.concatenate([jnp.cos(angles), jnp.sin(angles)], -1).astype(jnp.bfloat16)


def head_scale(values):
    return lax.rsqrt(jnp.mean(values * values, -1, keepdims=True) + epsilon)


def one_column(rows):
    lane = lax.broadcasted_iota(jnp.int32, (rows, LANES - HEAD), 1)
    return jnp.where(lane == 0, 1.0, 0.0).astype(jnp.bfloat16)


def contract_last(left, right):
    return lax.dot_general(
        left, right, (((1,), (1,)), ((), ())), preferred_element_type=jnp.float32
    )


def sites():
    frame, space = lax.axis_index("frame"), lax.axis_index("space")
    return frame // 16, frame // 2 % 8, frame % 2, space // 2, space % 2


def site_id(high, z, core, y, low):
    return {"frame": high * 16 + z * 2 + core, "space": y * 2 + low}


def meet(peers):
    barrier = pltpu.get_barrier_semaphore()
    for peer in peers:
        pl.semaphore_signal(barrier, inc=1, device_id=peer, device_id_type=MESH)
    pl.semaphore_wait(barrier, len(peers))


def swap_rows(source, landing, send_sem, recv_sem):
    me, space = lax.axis_index("frame"), lax.axis_index("space")
    here = pl.ds(pl.multiple_of(me * SUB, SUB), SUB)
    flying = []
    for distance in range(1, 32):
        peer = (me + distance) % 32
        flying.append(
            remote(
                source.at[pl.ds(pl.multiple_of(peer * SUB, SUB), SUB), :],
                landing.at[here, :],
                send_sem.at[distance - 1],
                recv_sem.at[distance - 1],
                {"frame": peer, "space": space},
            )
        )
    for copy in flying:
        copy.start()
    landing[here, :] = source[here, :]
    return flying


def remote(source, target, send_sem, recv_sem, peer):
    return pltpu.make_async_remote_copy(
        src_ref=source,
        dst_ref=target,
        send_sem=send_sem,
        recv_sem=recv_sem,
        device_id=peer,
        device_id_type=MESH,
    )


def restore_order(quarter):
    row = lax.broadcasted_iota(jnp.int32, (144, 4 * TOP + 4 * TILE), 0)
    column = lax.broadcasted_iota(jnp.int32, (144, 4 * TOP + 4 * TILE), 1)
    device, inner = row // 36, row % 36
    source = jnp.where(
        inner < TOP, device * TOP + inner, 4 * TOP + device * TILE + quarter * 4 + inner - TOP
    )
    return jnp.where(source == column, 1.0, 0.0).astype(jnp.bfloat16)


class Gather:
    def __init__(self, blocks, send_sem, recv_sem):
        self.blocks, self.send_sem, self.recv_sem = blocks, send_sem, recv_sem
        high, z, core, y, low = sites()
        self.place = (high, z, core, y, low)
        self.up = site_id(high, (z + 1) % 8, core, y, low)
        self.down = site_id(high, (z + 7) % 8, core, y, low)
        self.across = site_id(1 - high, z, core, y, 1 - low)
        self.north = site_id(high, z, core, (y + 1) % 4, low)
        self.south = site_id(high, z, core, (y + 3) % 4, low)
        self.sibling = site_id(high, z, 1 - core, y, low)
        self.mine = self.slot(high, z)
        self.handed = ([], [], [])
        self.passed = []
        self.started = []

    def slot(self, half, level):
        return half * 16 + level % 8 * 2 + self.place[2]

    def copy(self, kind, which, peer, index, half=None):
        first, last = CHUNKS[kind]
        if half is not None:
            middle = (first + last) // 2
            first, last = (first, middle) if half == 0 else (middle, last)
        piece = self.blocks.at[which, first:last]
        return remote(
            piece, piece, self.send_sem.at[index, kind], self.recv_sem.at[index, kind], peer
        )

    def send(self, kind, which, peer, index, half=None):
        copy = self.copy(kind, which, peer, index, half)
        copy.start()
        self.started.append(copy)

    def arrive(self, kind, which, peer, index, half=None):
        self.copy(kind, which, peer, index, half).wait_recv()

    def hand(self, kind, which):
        self.send(kind, which, self.sibling, HANDED + len(self.handed[kind]))
        self.handed[kind].append(which)

    def begin(self, kind):
        self.send(kind, self.mine, self.up, 0)
        self.send(kind, self.mine, self.down, 4)
        if kind == 0:
            self.pass_across(self.mine)
        self.hand(kind, self.mine)

    def pass_across(self, which):
        self.send(0, which, self.across, ACROSS + len(self.passed))
        self.passed.append(which)

    def hop(self, kind, hop):
        high, z, core, y, low = self.place
        half = (0, 1) if hop == 4 else (None, None)
        lower, upper = self.slot(high, z + 8 - hop), self.slot(high, z + hop)
        self.arrive(kind, lower, self.up, hop - 1, half[0])
        if hop < 4:
            self.send(kind, lower, self.up, hop, 0 if hop == 3 else None)
        self.arrive(kind, upper, self.down, 4 + hop - 1, half[1])
        if hop < 4:
            self.send(kind, upper, self.down, 4 + hop, 1 if hop == 3 else None)
        if kind == 0:
            for which in (lower, upper)[hop // 4 :]:
                self.pass_across(which)
        elif hop == 2:
            self.send(kind, self.slot(high, z + y + 7), self.across, 8)
        elif hop == 4:
            self.send(kind, self.slot(high, z + y + 3), self.across, 9)
        for which in (lower, upper)[hop // 4 :]:
            self.hand(kind, which)

    def finish_own(self):
        for index, which in enumerate(self.passed):
            other = which + 16 - 32 * self.place[0]
            self.arrive(0, other, self.across, ACROSS + index)
            self.hand(0, other)

    def cross(self, kind, far):
        high, z, core, y, low = self.place
        which = self.slot(1 - high, z + y + (3 if far else 7))
        self.arrive(kind, which, self.across, 8 + far)
        self.send(kind, which, self.north, 10 + far)
        self.send(kind, which, self.south, 12 + far)
        self.hand(kind, which)

    def round_y(self, kind, step):
        high, z, core, y, low = self.place
        turn, shift, north, index, onward = (
            (3, 7, True, 10, 14),
            (1, 7, False, 12, None),
            (1, 3, False, 13, 15),
            (3, 3, True, 11, None),
            (2, 7, True, 14, None),
            (2, 3, False, 15, None),
        )[step]
        way = self.north if north else self.south
        which = self.slot(1 - high, z + (y + turn) % 4 + shift)
        self.arrive(kind, which, way, index)
        if onward is not None:
            self.send(kind, which, way, onward)
        self.hand(kind, which)

    def collect(self, kind):
        for index, which in enumerate(self.handed[kind]):
            self.arrive(kind, which + 1 - 2 * self.place[2], self.sibling, HANDED + index)

    def events(self):
        kinds = (1, 2)
        plan = [functools.partial(self.hop, kind, hop) for hop in (1, 2, 3) for kind in kinds]
        plan += [functools.partial(self.cross, kind, 0) for kind in kinds]
        plan += [functools.partial(self.hop, kind, 4) for kind in kinds]
        plan += [functools.partial(self.round_y, kind, step) for step in (0, 1) for kind in kinds]
        plan += [functools.partial(self.cross, kind, 1) for kind in kinds]
        plan += [functools.partial(self.round_y, kind, step) for step in (4, 2, 3, 5) for kind in kinds]
        return plan


def pack_rows(blocks, mine, first, tail, pieces):
    tile = 0
    for count, top, low in pieces:
        for number in range(count):
            blocks[mine, first + tile] = top(number)
            tail[0:4, tile * LANES : (tile + 1) * LANES] = low(number)
            tile += 1
    total = tail.shape[1] // LANES
    if total > tile:
        tail[0:4, tile * LANES :] = jnp.zeros((4, (total - tile) * LANES), jnp.float32)
    quarter = total // 4
    rest = first + tile
    for number in range(quarter):
        rows = [
            tail[0:4, (a * quarter + number) * LANES : (a * quarter + number + 1) * LANES]
            for a in range(4)
        ]
        packed = jnp.concatenate(rows, 0).astype(jnp.bfloat16)
        blocks[mine, rest + number // 2, number % 2 * TILE : (number % 2 + 1) * TILE, :] = packed


def restore_rows(blocks, whole, first, tiles, quarter):
    rest = first + tiles
    for a in range(4):
        order = restore_order(a)
        start, stop = a * quarter, min((a + 1) * quarter, tiles)

        @pl.loop(0, 8)
        def _(quad):
            four = pl.ds(quad * 4, 4)
            rows = pl.ds(pl.multiple_of(quad * 144, 16), 144)
            for begin in range(start, stop, 4):
                end = min(begin + 4, stop)
                columns = []
                for tile in range(begin, end):
                    number = tile - start
                    low = blocks[
                        four, rest + number // 2, number % 2 * TILE : (number % 2 + 1) * TILE, :
                    ]
                    top = blocks[four, first + tile]
                    columns.append(
                        jnp.concatenate(
                            [top.reshape(4 * TOP, LANES), low.reshape(4 * TILE, LANES)], 0
                        )
                    )
                joined = jnp.concatenate(columns, 1)
                result = jnp.dot(order, joined, preferred_element_type=jnp.float32)
                whole[rows, begin * LANES : end * LANES] = result.astype(jnp.bfloat16)


def network_kernel(
    offsets, latents, features, facts, fresh, time_proj, embed_in, embed_out,
    proj_s, out_s, proj_t, out_t, queue, velocities,
    blocks, tail, own, shared, info, mods, tokens, mixed, parts, stage, landing,
    state, outgoing, back, again, triple, qs, ks, vs, mix,
    gather_send, gather_recv, fact_send, fact_recv, share_send, share_recv,
    part_send, part_recv, row_send, row_recv, swap_send, swap_recv,
):
    high, z, core, y, low = sites()
    place, row = y * 2 + low, lax.axis_index("frame")
    width, local_heads = HEADS * HEAD, HEADS // GROUPS
    span = local_heads * HEAD

    def plane_peer(dy, a, b, c):
        return site_id((high + b) % 2, z, (core + c) % 2, (y + dy) % 4, (low + a) % 2)

    offs = [(dy, a, b, c) for dy in range(4) for a in range(2) for b in range(2) for c in range(2)]
    above = [site_id(high, (z + d) % 8, core, y, low) for d in range(1, 8)]
    frames = [(h, d, c) for h in range(2) for d in range(1, 8) for c in range(2)]
    meet(
        [plane_peer(*offset) for offset in offs[1:]]
        + [site_id((high + h) % 2, (z + d) % 8, (core + c) % 2, y, low) for h, d, c in frames]
    )

    gather = Gather(blocks, gather_send, gather_recv)
    source = lax.broadcasted_iota(jnp.int32, (width, span), 0)
    target = lax.broadcasted_iota(jnp.int32, (width, span), 1)
    chosen = jnp.where(source == target + y * span, 1.0, 0.0).astype(jnp.bfloat16)
    own_rows = triple
    for part in range(3):
        own_rows[0:36, part * span : (part + 1) * span] = jnp.dot(
            proj_s[:, part * width : (part + 1) * width], chosen, preferred_element_type=jnp.float32
        )
    own_rows[0:36, 3 * span : 7 * LANES] = jnp.zeros((36, 7 * LANES - 3 * span), jnp.float32)

    def wide_piece(number):
        return own_rows[0:TOP, number * LANES : (number + 1) * LANES].astype(jnp.bfloat16)

    def wide_rest(number):
        return own_rows[TOP:36, number * LANES : (number + 1) * LANES]

    pack_rows(blocks, gather.mine, 0, tail.at[:, : 8 * LANES], [(7, wide_piece, wide_rest)])
    gather.begin(0)

    def pieces(ref):
        return (
            ref.shape[1] // LANES,
            lambda number: ref[:TOP, number * LANES : (number + 1) * LANES],
            lambda number: ref[TOP:, number * LANES : (number + 1) * LANES].astype(jnp.float32),
        )

    pack_rows(blocks, gather.mine, 8, tail, [pieces(out_s), pieces(proj_t), pieces(out_t)])
    gather.begin(1)
    gather.begin(2)

    mine = pl.ds(pl.multiple_of(place * LANES, LANES), LANES)

    def share(step, source):
        flying = []
        for d in range(1, 8):
            other = (place + d) % 8
            copy = remote(
                source.at[other % 2],
                tokens.at[step, mine, :],
                share_send.at[step, d - 1],
                share_recv.at[step, d - 1],
                {"frame": row, "space": other},
            )
            copy.start()
            flying.append(copy)
        tokens[step, mine, :] = source[low]
        return flying

    shares = share(0, latents)
    fact_copies = swap_rows(facts, info, fact_send, fact_recv)
    plan = gather.events()

    def advance(count):
        for _ in range(min(count, len(plan))):
            plan.pop(0)()

    gather.hop(0, 1)
    gather.hop(0, 2)
    advance(1)
    gather.hop(0, 3)
    advance(1)
    gather.hop(0, 4)
    gather.finish_own()
    gather.collect(0)
    restore_rows(blocks, own, 0, 7, 2)
    first_mods = jnp.dot(features[...], time_proj[:, : 2 * width], preferred_element_type=jnp.float32)
    shift, scale = first_mods[:1, :width], 1.0 + first_mods[:1, width:]
    mixed[:, :, span:] = jnp.zeros((STEPS, 8 * LANES, 3 * LANES - span), jnp.bfloat16)

    def spatial(step, shares, between):
        for copy in shares:
            copy.wait()
        for first in range(0, 8 * LANES, BLOCK):
            here = pl.ds(first, BLOCK)
            hidden = jnp.dot(
                tokens[step, here, :PATCH], embed_in[...], preferred_element_type=jnp.float32
            )
            normed = layer_norm(hidden) * scale + shift
            triple[:, : 7 * LANES] = jnp.dot(
                normed.astype(jnp.bfloat16), own[...], preferred_element_type=jnp.float32
            )
            for head in range(local_heads):
                query = triple[:, head * HEAD : (head + 1) * HEAD]
                key = triple[:, span + head * HEAD : span + (head + 1) * HEAD]
                value = triple[:, 2 * span + head * HEAD : 2 * span + (head + 1) * HEAD]
                qs[head, here, :] = (query * (head_scale(query) * SHARPEN)).astype(jnp.bfloat16)
                ks[head, here, :] = (key * head_scale(key)).astype(jnp.bfloat16)
                vs[head, here, :HEAD] = value.astype(jnp.bfloat16)
                vs[head, here, HEAD:] = one_column(BLOCK)
            between()
        sent = []
        own_part = pl.ds(pl.multiple_of((high * 4 + core * 2 + low) * 32, 32), 32)
        for dy in range(4):
            first = (y + dy) % 4 * BLOCK
            here = pl.ds(pl.multiple_of(first, BLOCK), BLOCK)
            for head in range(local_heads):
                raised = jnp.exp2(contract_last(qs[head, here, :], ks[head])).astype(jnp.bfloat16)
                part = jnp.dot(raised, vs[head], preferred_element_type=jnp.float32)
                part = part[:, :HEAD] / part[:, HEAD : HEAD + 1]
                mixed[step, here, head * HEAD : (head + 1) * HEAD] = part.astype(jnp.bfloat16)
            for index, (way, a, b, c) in enumerate(offs):
                if way != dy:
                    continue
                target = (low + a) % 2 * 4 + (high + b) % 2 * 2 + (core + c) % 2
                piece = pl.ds(pl.multiple_of(first + target * 32, 32), 32)
                if index == 0:
                    parts[step, y, own_part, :] = mixed[step, piece, :]
                    continue
                copy = remote(
                    mixed.at[step, piece, :],
                    parts.at[step, y, own_part, :],
                    part_send.at[step, index - 1],
                    part_recv.at[step, index - 1],
                    plane_peer(way, a, b, c),
                )
                copy.start()
                sent.append(copy)
            between()
        for copy in sent:
            copy.wait()
        target = lax.broadcasted_iota(jnp.int32, (2 * LANES, 2 * LANES), 0)
        source = lax.broadcasted_iota(jnp.int32, (2 * LANES, 2 * LANES), 1)
        moved = target % 32 // 8 * 64 + target % 2 * 32 + target // 32 * 4 + target % 8 // 2
        order = jnp.where(moved == source, 1.0, 0.0).astype(jnp.bfloat16)
        for group in range(GROUPS):
            piece = jnp.dot(order, parts[step, group], preferred_element_type=jnp.float32)
            stage[step, :, group * span : (group + 1) * span] = piece[:, :span].astype(jnp.bfloat16)
        flying = []
        for d in range(1, 8):
            for half in range(2):
                origin = pl.ds(pl.multiple_of((z + d) % 8 * 32 + half * TILE, TILE), TILE)
                goal = pl.ds(pl.multiple_of(half * LANES + z * TILE, TILE), TILE)
                copy = remote(
                    stage.at[step, origin, :],
                    landing.at[step, goal, :],
                    row_send.at[step, d - 1, half],
                    row_recv.at[step, d - 1, half],
                    above[d - 1],
                )
                copy.start()
                flying.append(copy)
        for half in range(2):
            origin = pl.ds(pl.multiple_of(z * 32 + half * TILE, TILE), TILE)
            goal = pl.ds(pl.multiple_of(half * LANES + z * TILE, TILE), TILE)
            landing[step, goal, :] = stage[step, origin, :]
        return flying

    rows = 2 * LANES

    def temporal(step):
        hidden_in = jnp.dot(
            state[:, :PATCH].astype(jnp.bfloat16), embed_in[...], preferred_element_type=jnp.float32
        )
        out = jnp.dot(landing[step], shared[:, :width], preferred_element_type=jnp.float32)
        hidden = hidden_in + mods[0] * out
        normed = layer_norm(hidden) * (1.0 + mods[2]) + mods[1]
        triple[...] = jnp.dot(
            normed.astype(jnp.bfloat16),
            shared[:, width : 4 * width],
            preferred_element_type=jnp.float32,
        )

        def place_of(index):
            frame = index // SUB * 2 + index % 2
            return (frame + WIN - offsets[step]) // WIN * SUB + index % SUB // 2

        same = place_of(lax.broadcasted_iota(jnp.int32, (rows, 1), 0)) == place_of(
            lax.broadcasted_iota(jnp.int32, (1, rows), 1)
        )
        ones = one_column(rows)
        for head in range(HEADS):
            query = triple[:, head * HEAD : (head + 1) * HEAD]
            key = triple[:, width + head * HEAD : width + (head + 1) * HEAD]
            value = triple[:, 2 * width + head * HEAD : 2 * width + (head + 1) * HEAD]
            query = (query * (head_scale(query) * SHARPEN)).astype(jnp.bfloat16)
            key = (key * head_scale(key)).astype(jnp.bfloat16)
            value = jnp.concatenate([value.astype(jnp.bfloat16), ones], -1)
            raised = jnp.where(same, jnp.exp2(contract_last(query, key)), 0.0)
            part = jnp.dot(raised.astype(jnp.bfloat16), value, preferred_element_type=jnp.float32)
            part = part[:, :HEAD] / part[:, HEAD : HEAD + 1]
            mix[:, head * HEAD : (head + 1) * HEAD] = part.astype(jnp.bfloat16)
        out = jnp.dot(mix[...], shared[:, 4 * width :], preferred_element_type=jnp.float32)
        hidden = hidden + mods[3] * out
        velocity = jnp.dot(
            layer_norm(hidden).astype(jnp.bfloat16),
            embed_out[...],
            preferred_element_type=jnp.float32,
        )
        return state[:, :PATCH] + info[:, PATCH : PATCH + 1] * velocity, velocity

    pace = [1, 1, 1, 1, 1, 1, 1, 1]
    flying = spatial(0, shares, lambda: advance(pace.pop(0)))
    for copy in fact_copies:
        copy.wait()
    facts_rows = info[:, LANES:].astype(jnp.bfloat16)
    for part in range(4):
        columns = time_proj[:, (part + 2) * width : (part + 3) * width]
        mods[part] = jnp.dot(facts_rows, columns, preferred_element_type=jnp.float32)
    state[...] = info[:, :LANES]
    advance(len(plan))
    for kind in (1, 2):
        gather.collect(kind)
    restore_rows(blocks, shared, 8, 45, 12)
    for copy in flying:
        copy.wait()
    stepped, velocity = temporal(0)
    outgoing[...] = jnp.zeros((STEPS, rows, LANES), jnp.float32)
    outgoing[0, :, :PATCH] = stepped
    wide = outgoing[0]
    index = lax.broadcasted_iota(jnp.int32, (rows, LANES), 0)
    first = index % 2 == 0
    ahead = jnp.where(first, pltpu.roll(wide, rows - 1, 0), pltpu.roll(wide, rows - 7, 0))
    added = jnp.concatenate([fresh[...]] * (rows // SUB), 0)
    ahead = jnp.where(first | (index < rows - SUB), ahead, added)
    outgoing[0] = ahead
    flying = swap_rows(outgoing.at[0], back.at[0], swap_send.at[0], swap_recv.at[0])
    state[:, :PATCH] = ahead[:, :PATCH]
    state[:, PATCH : 2 * PATCH] = velocity
    target = lax.broadcasted_iota(jnp.int32, (LANES, rows), 0)
    source = lax.broadcasted_iota(jnp.int32, (LANES, rows), 1)
    moved = target // 64 * 16 + target % 32 // 4 * 2 + target // 32 % 2
    moved = moved * SUB + target % 4 * 2
    for copy in flying:
        copy.wait()
    arrived = back[0].astype(jnp.bfloat16)
    for j in range(2):
        order = jnp.where(moved + j == source, 1.0, 0.0).astype(jnp.bfloat16)
        piece = jnp.dot(order, arrived, preferred_element_type=jnp.float32)
        again[j] = piece.astype(jnp.bfloat16)
    shares = share(1, again)
    for copy in gather.started:
        copy.wait_send()
    for copy in spatial(1, shares, lambda: None):
        copy.wait()
    stepped, velocity = temporal(1)
    outgoing[1, :, :PATCH] = stepped
    outgoing[1, :, PATCH : 2 * PATCH] = state[:, PATCH : 2 * PATCH]
    outgoing[1, :, 2 * PATCH : 3 * PATCH] = velocity
    for copy in swap_rows(outgoing.at[1], back.at[1], swap_send.at[1], swap_recv.at[1]):
        copy.wait()
    for j in range(2):
        piece = back[1, pl.ds(j, LANES, stride=2), :]
        queue[j] = piece[:, :PATCH]
        velocities[0, j] = piece[:, PATCH : 2 * PATCH]
        velocities[1, j] = piece[:, 2 * PATCH : 3 * PATCH]


def network(offsets, *arrays):
    width, local_heads, rows = HEADS * HEAD, HEADS // GROUPS, 2 * LANES
    vmem = pl.BlockSpec(memory_space=pltpu.VMEM)
    shape = (2, LANES, PATCH)
    bf16, f32, dma = jnp.bfloat16, jnp.float32, pltpu.SemaphoreType.DMA
    return pl.pallas_call(
        network_kernel,
        out_shape=[
            jax.ShapeDtypeStruct(shape, f32),
            jax.ShapeDtypeStruct((STEPS, *shape), f32),
        ],
        in_specs=[pl.BlockSpec(memory_space=pltpu.SMEM)] + [vmem] * len(arrays),
        out_specs=[vmem] * 2,
        scratch_shapes=[
            pltpu.VMEM((32, CHUNKS[-1][1], TOP, LANES), bf16),
            pltpu.VMEM((SUB, 48 * LANES), f32),
            pltpu.VMEM((width, 7 * LANES), bf16),
            pltpu.VMEM((width, 5 * width), bf16),
            pltpu.VMEM((rows, 3 * LANES), f32),
            pltpu.VMEM((4, rows, width), f32),
            pltpu.VMEM((STEPS, 8 * LANES, LANES), bf16),
            pltpu.VMEM((STEPS, 8 * LANES, 3 * LANES), bf16),
            pltpu.VMEM((STEPS, GROUPS, rows, 3 * LANES), bf16),
            pltpu.VMEM((STEPS, rows, width), bf16),
            pltpu.VMEM((STEPS, rows, width), bf16),
            pltpu.VMEM((rows, LANES), f32),
            pltpu.VMEM((STEPS, rows, LANES), f32),
            pltpu.VMEM((STEPS, rows, LANES), f32),
            pltpu.VMEM((2, LANES, LANES), bf16),
            pltpu.VMEM((rows, 3 * width), f32),
            pltpu.VMEM((local_heads, 8 * LANES, HEAD), bf16),
            pltpu.VMEM((local_heads, 8 * LANES, HEAD), bf16),
            pltpu.VMEM((local_heads, 8 * LANES, LANES), bf16),
            pltpu.VMEM((rows, width), bf16),
            dma((40, 3)), dma((40, 3)), dma((31,)), dma((31,)), dma((STEPS, 7)), dma((STEPS, 7)),
            dma((STEPS, 31)), dma((STEPS, 31)), dma((STEPS, 7, 2)), dma((STEPS, 7, 2)),
            dma((STEPS, 31)), dma((STEPS, 31)),
        ],
        compiler_params=pltpu.CompilerParams(
            collective_id=0, has_side_effects=True, vmem_limit_bytes=VMEM_BYTES
        ),
        name="network",
    )(offsets, *arrays)


def row_facts(latents, step_size, features):
    count, tokens, size = latents.shape
    rows = latents.reshape(count, 32, tokens // 32, size)
    rows = jnp.transpose(rows, (1, 2, 0, 3)).reshape(2 * tokens, size)
    steps = jnp.broadcast_to(step_size[None], (tokens, count)).reshape(2 * tokens, 1)
    wide = jnp.broadcast_to(features.astype(jnp.float32)[None], (tokens, count, 2 * LANES))
    gap = jnp.zeros((2 * tokens, LANES - size - 1), jnp.float32)
    return jnp.concatenate([rows, steps, gap, wide.reshape(2 * tokens, 2 * LANES)], -1)


def plane_rows(latents):
    rows = latents.astype(jnp.bfloat16).reshape(2, 2, 8, 2, 4, PATCH)
    rows = jnp.swapaxes(rows, 2, 3).reshape(2, LANES, PATCH)
    return jnp.pad(rows, ((0, 0), (0, 0), (0, LANES - PATCH)))


def local(
    latents,
    fresh_noise,
    levels,
    timesteps,
    window_offsets,
    time_proj,
    embed_in,
    spatial_proj,
    spatial_out,
    temporal_proj,
    temporal_out,
    embed_out,
):
    which, row = lax.axis_index("space") % 2, lax.axis_index("frame")
    time_value = lookup_table(levels, timesteps)
    earlier = lookup_table(levels - 1, timesteps)
    features = time_features(time_value, time_proj.shape[0] // 2)
    facts = row_facts(latents, (earlier - time_value) / 1000.0, features)
    own = jnp.broadcast_to(lax.dynamic_index_in_dim(features, which, 0), (TILE, 2 * LANES))
    fresh = lax.dynamic_slice_in_dim(fresh_noise[0], row * 4, 4)
    fresh = jnp.pad(jnp.repeat(fresh, 2, axis=0), ((0, 0), (0, LANES - PATCH)))
    return network(
        window_offsets,
        plane_rows(latents),
        own,
        facts,
        fresh,
        time_proj,
        embed_in,
        embed_out,
        spatial_proj,
        spatial_out,
        temporal_proj,
        temporal_out,
    )


def solution(mesh):
    return jax.shard_map(
        local,
        mesh=mesh,
        in_specs=(
            P("frame", "space", None),
            P(None, "space", None),
            P("frame"),
            P(),
            P(),
            P(),
            P(),
            P("frame", None),
            P("frame", None),
            P("frame", None),
            P("frame", None),
            P(),
        ),
        out_specs=(P("frame", "space", None), P(None, "frame", "space", None)),
        check_vma=False,
    )
```

time: 597 us -> 229 us (0.38); the launches traced: 587 us -> 226 us
  waiting for transfers between devices: 265 us -> 0 us
  Pallas kernels: 0 us -> 214 us
  blocking collectives: 106 us -> 0 us
  local copies, waits for them, and re-layouts: 97.8 us -> 8.29 us
  matrix products: 57.9 us -> 0 us
  starting transfers between devices: 29.7 us -> 0 us
  between operations: 15.3 us -> 0.96 us
  other arithmetic: 15.4 us -> 2.6 us
    all_gather x4 -> x0, waiting for transfers between devices: 229 us -> none  [the longest x1 89.5 us: local(): temporal_full = lax.all_gather(temporal_proj, 'frame', axis=0, tiled=True)]
    pallas_call x0 -> x1, Pallas kernels: none -> 214 us  [network(): pl.pallas_call(network_kernel, out_shape=[jax.ShapeDtypeStruct(shape, f32...]
    dot_general x23 -> x0, matrix products: 57.9 us -> none  [the longest x2 14.9 us: temporal_block(): jnp.dot(normed, proj, preferred_element_type=jnp.float32)]
    all_gather x2 -> x0, blocking collectives: 44 us -> none  [local(): whole = lax.all_gather(by_frame, 'space', axis=1, tiled=True)]
    all_to_all x3 -> x0, blocking collectives: 43.3 us -> none  [the longest x2 30 us: to_frames(): lax.all_to_all(values, 'frame', split_axis=0, concat_axis=1, tiled=True)]
    unnamed x71 -> x4, local copies, waits for them, and re-layouts: 40.4 us -> 2.48 us
    all_to_all x4 -> x0, waiting for transfers between devices: 34.5 us -> none  [the longest x3 25.3 us: to_tokens(): lax.all_to_all(values, 'frame', split_axis=1, concat_axis=0, tiled=True)]
    all_to_all x4 -> x0, starting transfers between devices: 29.5 us -> none  [the longest x3 25.3 us: to_tokens(): lax.all_to_all(values, 'frame', split_axis=1, concat_axis=0, tiled=True)]
  transfers between devices with their start and end apart: 8 -> 0, of which waited for: 7 -> 0; matrix products, arithmetic and copies ran while one was open for 8% -> 0% of each run, Pallas kernels for 0% -> 0%
where the time goes in v5:
time: 229 us; the launch traced here: 226 us
  Pallas kernels  214 us (93%)
  local copies, waits for them, and re-layouts  8.29 us (4%)
  other arithmetic  2.6 us (1%)
    pallas_call x1, Pallas kernels, network(): pl.pallas_call(network_kernel, out_shape=[jax.ShapeDtypeStruct(shape, f32...  214 us

profile of v5, /device:TPU:1, one launch (start us, length us, event | category | flops | bytes accessed | tf_op | source)
XLA Modules:
  0.0 225.6 jit_solution(2490784736851193380)
XLA Ops:
  0.6 0.0 copy-start
  0.7 0.7 broadcast_add_fusion
  1.3 0.9 fusion.3
  2.2 0.1 fusion
  2.4 0.1 pad.12.clone
  2.5 0.6 broadcast_in_dim.52.features
  3.1 0.0 copy-done
  3.1 0.1 constant_dynamic-slice_fusion
  3.2 0.1 copy.34
  3.2 0.6 pad.9.fresh
  3.9 0.1 reshape.90
  3.9 0.8 copy.29
  4.8 0.6 pad.8.latents
  5.5 0.1 copy.32
  5.6 0.1 broadcast_in_dim.55
  5.6 0.2 reshape.88
  5.8 0.9 pad_maximum_fusion.facts
  6.7 1.7 copy.35.embed_out
  8.4 213.8 %network.1 = (f32[2,128,16]{2,1,0:T(8,128)}, f32[2,2,128,16]{3,2,1,0:T(8,128)}) custom-call(s32[2]{0:T(128)} %offsets.1, bf16[2,128,128]{2,1,0:T(8,128)(2,1)} %pad.8.latents, bf16[16,256]{1,0:T(8,128)(2,1)} %broadcast_in_dim.52.features, f32[256,384]{1,0:T(8,128)} %pad_maximum_fusion.facts, f32[8,128]{1,0:T(8,128)} %pad.9.fresh, ...), custom_call_target="tpu_custom_call" | custom-call | tf_op jit(solution)/shard_map/network/pallas_call | solution.py:567
  222.1 1.6 copy.36
  223.7 1.7 copy.37
  (10 shorter events, 0.1 us)
Async XLA Ops:
  0.6 2.5 %copy-start = (f32[1,128,16]{1,2,0:T(8,128)S(1)}, f32[1,128,16]{1,2,0:T(8,128)}, u32[]{:S(2)}) copy-start(f32[1,128,16]{1,2,0:T(8,128)} %param.13) | copy-start | bytes 24580

commit v6 on v5

--- a/solution.py
+++ b/solution.py
@@ -70,11 +70,11 @@
     return {"frame": high * 16 + z * 2 + core, "space": y * 2 + low}
 
 
-def meet(peers):
+def greet(peers):
     barrier = pltpu.get_barrier_semaphore()
     for peer in peers:
         pl.semaphore_signal(barrier, inc=1, device_id=peer, device_id_type=MESH)
-    pl.semaphore_wait(barrier, len(peers))
+    return lambda: pl.semaphore_wait(barrier, len(peers))
 
 
 def swap_rows(source, landing, send_sem, recv_sem):
@@ -92,8 +92,6 @@
                 {"frame": peer, "space": space},
             )
         )
-    for copy in flying:
-        copy.start()
     landing[here, :] = source[here, :]
     return flying
 
@@ -129,6 +127,7 @@
         self.across = site_id(1 - high, z, core, y, 1 - low)
         self.north = site_id(high, z, core, (y + 1) % 4, low)
         self.south = site_id(high, z, core, (y + 3) % 4, low)
+        self.inner = site_id(high, z, core, y, 1 - low)
         self.sibling = site_id(high, z, 1 - core, y, low)
         self.mine = self.slot(high, z)
         self.handed = ([], [], [])
@@ -184,42 +183,38 @@
         if kind == 0:
             for which in (lower, upper)[hop // 4 :]:
                 self.pass_across(which)
-        elif hop == 2:
-            self.send(kind, self.slot(high, z + y + 7), self.across, 8)
-        elif hop == 4:
-            self.send(kind, self.slot(high, z + y + 3), self.across, 9)
+        elif hop % 2 == 0:
+            self.send(kind, self.brought(hop // 2 - 1, y, 1 - low, high), self.across, 7 + hop // 2)
         for which in (lower, upper)[hop // 4 :]:
             self.hand(kind, which)
 
-    def finish_own(self):
-        for index, which in enumerate(self.passed):
+    def finish_own(self, first, last):
+        for index in range(first, last):
+            which = self.passed[index]
             other = which + 16 - 32 * self.place[0]
             self.arrive(0, other, self.across, ACROSS + index)
             self.hand(0, other)
 
-    def cross(self, kind, far):
+    def brought(self, far, y, low, half):
+        return self.slot(half, self.place[1] + y % 2 * 2 + low + (3 if far else 7))
+
+    def leg(self, kind, leg, far):
         high, z, core, y, low = self.place
-        which = self.slot(1 - high, z + y + (3 if far else 7))
-        self.arrive(kind, which, self.across, 8 + far)
-        self.send(kind, which, self.north, 10 + far)
-        self.send(kind, which, self.south, 12 + far)
-        self.hand(kind, which)
-
-    def round_y(self, kind, step):
-        high, z, core, y, low = self.place
-        turn, shift, north, index, onward = (
-            (3, 7, True, 10, 14),
-            (1, 7, False, 12, None),
-            (1, 3, False, 13, 15),
-            (3, 3, True, 11, None),
-            (2, 7, True, 14, None),
-            (2, 3, False, 15, None),
-        )[step]
-        way = self.north if north else self.south
-        which = self.slot(1 - high, z + (y + turn) % 4 + shift)
-        self.arrive(kind, which, way, index)
-        if onward is not None:
-            self.send(kind, which, way, onward)
+        if leg == 0:
+            which, index, peer = self.brought(far, y, low, 1 - high), 8, self.across
+            onward = ((self.inner, 10), (self.north, 12))
+        elif leg == 1:
+            which, index, peer = self.brought(far, y, 1 - low, 1 - high), 10, self.inner
+            onward = ((self.south, 14),)
+        elif leg == 2:
+            which, index, peer = self.brought(far, y + 1, low, 1 - high), 12, self.north
+            onward = ()
+        else:
+            which, index, peer = self.brought(far, y + 1, 1 - low, 1 - high), 14, self.south
+            onward = ()
+        self.arrive(kind, which, peer, index + far)
+        for target, number in onward:
+            self.send(kind, which, target, number + far)
         self.hand(kind, which)
 
     def collect(self, kind):
@@ -227,17 +222,21 @@
             self.arrive(kind, which + 1 - 2 * self.place[2], self.sibling, HANDED + index)
 
     def events(self):
-        kinds = (1, 2)
-        plan = [functools.partial(self.hop, kind, hop) for hop in (1, 2, 3) for kind in kinds]
-        plan += [functools.partial(self.cross, kind, 0) for kind in kinds]
-        plan += [functools.partial(self.hop, kind, 4) for kind in kinds]
-        plan += [functools.partial(self.round_y, kind, step) for step in (0, 1) for kind in kinds]
-        plan += [functools.partial(self.cross, kind, 1) for kind in kinds]
-        plan += [functools.partial(self.round_y, kind, step) for step in (4, 2, 3, 5) for kind in kinds]
+        def hop(kind, number):
+            return lambda: self.hop(kind, number)
+
+        def leg(kind, number, far):
+            return lambda: self.leg(kind, number, far)
+
+        plan = [hop(1, 1), lambda: self.begin(2), hop(1, 2), hop(2, 1)]
+        plan += [leg(1, 0, 0), hop(1, 3), hop(2, 2), leg(1, 1, 0), leg(1, 2, 0), hop(1, 4), hop(2, 3)]
+        plan += [leg(2, 0, 0), hop(2, 4), leg(1, 3, 0), leg(2, 1, 0), leg(2, 2, 0), leg(1, 0, 1)]
+        plan += [leg(2, 0, 1), leg(2, 3, 0), leg(1, 1, 1), leg(1, 2, 1), leg(2, 1, 1), leg(2, 2, 1)]
+        plan += [leg(1, 3, 1), leg(2, 3, 1)]
         return plan
 
 
-def pack_rows(blocks, mine, first, tail, pieces):
+def pack_rows(blocks, mine, first, rest, tail, pieces):
     tile = 0
     for count, top, low in pieces:
         for number in range(count):
@@ -248,7 +247,6 @@
     if total > tile:
         tail[0:4, tile * LANES :] = jnp.zeros((4, (total - tile) * LANES), jnp.float32)
     quarter = total // 4
-    rest = first + tile
     for number in range(quarter):
         rows = [
             tail[0:4, (a * quarter + number) * LANES : (a * quarter + number + 1) * LANES]
@@ -258,11 +256,12 @@
         blocks[mine, rest + number // 2, number % 2 * TILE : (number % 2 + 1) * TILE, :] = packed
 
 
-def restore_rows(blocks, whole, first, tiles, quarter):
-    rest = first + tiles
+def restore_rows(blocks, whole, first, rest, quarter, tiles):
     for a in range(4):
+        start, stop = max(a * quarter, tiles[0]), min((a + 1) * quarter, tiles[1])
+        if start >= stop:
+            continue
         order = restore_order(a)
-        start, stop = a * quarter, min((a + 1) * quarter, tiles)
 
         @pl.loop(0, 8)
         def _(quad):
@@ -272,7 +271,7 @@
                 end = min(begin + 4, stop)
                 columns = []
                 for tile in range(begin, end):
-                    number = tile - start
+                    number = tile - a * quarter
                     low = blocks[
                         four, rest + number // 2, number % 2 * TILE : (number % 2 + 1) * TILE, :
                     ]
@@ -306,10 +305,31 @@
     offs = [(dy, a, b, c) for dy in range(4) for a in range(2) for b in range(2) for c in range(2)]
     above = [site_id(high, (z + d) % 8, core, y, low) for d in range(1, 8)]
     frames = [(h, d, c) for h in range(2) for d in range(1, 8) for c in range(2)]
-    meet(
+    everyone_here = greet(
         [plane_peer(*offset) for offset in offs[1:]]
         + [site_id((high + h) % 2, (z + d) % 8, (core + c) % 2, y, low) for h, d, c in frames]
     )
+
+    mine = pl.ds(pl.multiple_of(place * LANES, LANES), LANES)
+    near = [(dy, a) for dy in range(4) for a in range(2)]
+    later = []
+
+    def share(step, source):
+        flying = [None]
+        for index, (dy, a) in enumerate(near[1:]):
+            other = (y + dy) % 4 * 2 + (low + a) % 2
+            copy = remote(
+                source.at[(low + a) % 2],
+                tokens.at[step, mine, :],
+                share_send.at[step, index],
+                share_recv.at[step, index],
+                {"frame": row, "space": other},
+            )
+            copy.start()
+            flying.append(copy)
+            later.append(copy)
+        tokens[step, mine, :] = source[low]
+        return flying
 
     gather = Gather(blocks, gather_send, gather_recv)
     source = lax.broadcasted_iota(jnp.int32, (width, span), 0)
@@ -328,8 +348,10 @@
     def wide_rest(number):
         return own_rows[TOP:36, number * LANES : (number + 1) * LANES]
 
-    pack_rows(blocks, gather.mine, 0, tail.at[:, : 8 * LANES], [(7, wide_piece, wide_rest)])
+    pack_rows(blocks, gather.mine, 1, 0, tail.at[:, : 8 * LANES], [(7, wide_piece, wide_rest)])
+    everyone_here()
     gather.begin(0)
+    shares = share(0, latents)
 
     def pieces(ref):
         return (
@@ -338,54 +360,35 @@
             lambda number: ref[TOP:, number * LANES : (number + 1) * LANES].astype(jnp.float32),
         )
 
-    pack_rows(blocks, gather.mine, 8, tail, [pieces(out_s), pieces(proj_t), pieces(out_t)])
-    gather.begin(1)
-    gather.begin(2)
-
-    mine = pl.ds(pl.multiple_of(place * LANES, LANES), LANES)
-
-    def share(step, source):
-        flying = []
-        for d in range(1, 8):
-            other = (place + d) % 8
-            copy = remote(
-                source.at[other % 2],
-                tokens.at[step, mine, :],
-                share_send.at[step, d - 1],
-                share_recv.at[step, d - 1],
-                {"frame": row, "space": other},
-            )
-            copy.start()
-            flying.append(copy)
-        tokens[step, mine, :] = source[low]
-        return flying
-
-    shares = share(0, latents)
-    fact_copies = swap_rows(facts, info, fact_send, fact_recv)
+    pack_rows(blocks, gather.mine, 14, 8, tail, [pieces(out_s), pieces(proj_t), pieces(out_t)])
+
     plan = gather.events()
 
     def advance(count):
         for _ in range(min(count, len(plan))):
             plan.pop(0)()
 
+    gather.begin(1)
     gather.hop(0, 1)
     gather.hop(0, 2)
-    advance(1)
+    advance(2)
     gather.hop(0, 3)
-    advance(1)
     gather.hop(0, 4)
-    gather.finish_own()
+    gather.finish_own(0, 5)
+    advance(2)
+    gather.finish_own(5, 8)
     gather.collect(0)
-    restore_rows(blocks, own, 0, 7, 2)
+    restore_rows(blocks, own, 1, 0, 2, (0, 7))
     first_mods = jnp.dot(features[...], time_proj[:, : 2 * width], preferred_element_type=jnp.float32)
     shift, scale = first_mods[:1, :width], 1.0 + first_mods[:1, width:]
     mixed[:, :, span:] = jnp.zeros((STEPS, 8 * LANES, 3 * LANES - span), jnp.bfloat16)
 
     def spatial(step, shares, between):
-        for copy in shares:
-            copy.wait()
-        for first in range(0, 8 * LANES, BLOCK):
-            here = pl.ds(first, BLOCK)
+        for dy in range(4):
+            for a in range(2):
+                if (dy, a) != (0, 0):
+                    shares[near.index((-dy % 4, a))].wait_recv()
+            here = pl.ds(pl.multiple_of((y + dy) % 4 * BLOCK, BLOCK), BLOCK)
             hidden = jnp.dot(
                 tokens[step, here, :PATCH], embed_in[...], preferred_element_type=jnp.float32
             )
@@ -430,8 +433,10 @@
                 copy.start()
                 sent.append(copy)
             between()
+        between()
         for copy in sent:
-            copy.wait()
+            copy.wait_recv()
+        later.extend(sent)
         target = lax.broadcasted_iota(jnp.int32, (2 * LANES, 2 * LANES), 0)
         source = lax.broadcasted_iota(jnp.int32, (2 * LANES, 2 * LANES), 1)
         moved = target % 32 // 8 * 64 + target % 2 * 32 + target // 32 * 4 + target % 8 // 2
@@ -457,6 +462,7 @@
             origin = pl.ds(pl.multiple_of(z * 32 + half * TILE, TILE), TILE)
             goal = pl.ds(pl.multiple_of(half * LANES + z * TILE, TILE), TILE)
             landing[step, goal, :] = stage[step, origin, :]
+        later.extend(flying)
         return flying
 
     rows = 2 * LANES
@@ -495,28 +501,35 @@
             mix[:, head * HEAD : (head + 1) * HEAD] = part.astype(jnp.bfloat16)
         out = jnp.dot(mix[...], shared[:, 4 * width :], preferred_element_type=jnp.float32)
         hidden = hidden + mods[3] * out
-        velocity = jnp.dot(
-            layer_norm(hidden).astype(jnp.bfloat16),
-            embed_out[...],
-            preferred_element_type=jnp.float32,
-        )
+        velocity = contract_last(layer_norm(hidden).astype(jnp.bfloat16), embed_out[...])
         return state[:, :PATCH] + info[:, PATCH : PATCH + 1] * velocity, velocity
 
-    pace = [1, 1, 1, 1, 1, 1, 1, 1]
-    flying = spatial(0, shares, lambda: advance(pace.pop(0)))
+    pace = [1, 2, 1, 1, 2, 1, 1, 1, 2]
+    fact_copies = swap_rows(facts, info, fact_send, fact_recv)
+    waiting = list(fact_copies)
+
+    def between():
+        for _ in range(min(5, len(waiting))):
+            waiting.pop(0).start()
+        advance(pace.pop(0))
+
+    flying = spatial(0, shares, between)
     for copy in fact_copies:
-        copy.wait()
+        copy.wait_recv()
+    later.extend(fact_copies)
     facts_rows = info[:, LANES:].astype(jnp.bfloat16)
     for part in range(4):
         columns = time_proj[:, (part + 2) * width : (part + 3) * width]
         mods[part] = jnp.dot(facts_rows, columns, preferred_element_type=jnp.float32)
     state[...] = info[:, :LANES]
-    advance(len(plan))
-    for kind in (1, 2):
-        gather.collect(kind)
-    restore_rows(blocks, shared, 8, 45, 12)
+    advance(len(plan) - 1)
+    gather.collect(1)
+    restore_rows(blocks, shared, 14, 8, 12, (0, 19))
+    advance(1)
+    gather.collect(2)
+    restore_rows(blocks, shared, 14, 8, 12, (19, 45))
     for copy in flying:
-        copy.wait()
+        copy.wait_recv()
     stepped, velocity = temporal(0)
     outgoing[...] = jnp.zeros((STEPS, rows, LANES), jnp.float32)
     outgoing[0, :, :PATCH] = stepped
@@ -528,6 +541,9 @@
     ahead = jnp.where(first | (index < rows - SUB), ahead, added)
     outgoing[0] = ahead
     flying = swap_rows(outgoing.at[0], back.at[0], swap_send.at[0], swap_recv.at[0])
+    for copy in flying:
+        copy.start()
+    later.extend(flying)
     state[:, :PATCH] = ahead[:, :PATCH]
     state[:, PATCH : 2 * PATCH] = velocity
     target = lax.broadcasted_iota(jnp.int32, (LANES, rows), 0)
@@ -535,34 +551,38 @@
     moved = target // 64 * 16 + target % 32 // 4 * 2 + target // 32 % 2
     moved = moved * SUB + target % 4 * 2
     for copy in flying:
-        copy.wait()
+        copy.wait_recv()
     arrived = back[0].astype(jnp.bfloat16)
     for j in range(2):
         order = jnp.where(moved + j == source, 1.0, 0.0).astype(jnp.bfloat16)
         piece = jnp.dot(order, arrived, preferred_element_type=jnp.float32)
         again[j] = piece.astype(jnp.bfloat16)
     shares = share(1, again)
-    for copy in gather.started:
+    flying = spatial(1, shares, lambda: None)
+    for copy in gather.started + later:
         copy.wait_send()
-    for copy in spatial(1, shares, lambda: None):
-        copy.wait()
+    for copy in flying:
+        copy.wait_recv()
     stepped, velocity = temporal(1)
     outgoing[1, :, :PATCH] = stepped
     outgoing[1, :, PATCH : 2 * PATCH] = state[:, PATCH : 2 * PATCH]
     outgoing[1, :, 2 * PATCH : 3 * PATCH] = velocity
-    for copy in swap_rows(outgoing.at[1], back.at[1], swap_send.at[1], swap_recv.at[1]):
+    flying = swap_rows(outgoing.at[1], back.at[1], swap_send.at[1], swap_recv.at[1])
+    for copy in flying:
+        copy.start()
+    for copy in flying:
         copy.wait()
     for j in range(2):
-        piece = back[1, pl.ds(j, LANES, stride=2), :]
-        queue[j] = piece[:, :PATCH]
-        velocities[0, j] = piece[:, PATCH : 2 * PATCH]
-        velocities[1, j] = piece[:, 2 * PATCH : 3 * PATCH]
+        piece = jnp.transpose(back[1, pl.ds(j, LANES, stride=2), :])
+        queue[j] = piece[:PATCH]
+        velocities[0, j] = piece[PATCH : 2 * PATCH]
+        velocities[1, j] = piece[2 * PATCH : 3 * PATCH]
 
 
 def network(offsets, *arrays):
     width, local_heads, rows = HEADS * HEAD, HEADS // GROUPS, 2 * LANES
     vmem = pl.BlockSpec(memory_space=pltpu.VMEM)
-    shape = (2, LANES, PATCH)
+    shape = (2, PATCH, LANES)
     bf16, f32, dma = jnp.bfloat16, jnp.float32, pltpu.SemaphoreType.DMA
     return pl.pallas_call(
         network_kernel,
@@ -642,7 +662,7 @@
     own = jnp.broadcast_to(lax.dynamic_index_in_dim(features, which, 0), (TILE, 2 * LANES))
     fresh = lax.dynamic_slice_in_dim(fresh_noise[0], row * 4, 4)
     fresh = jnp.pad(jnp.repeat(fresh, 2, axis=0), ((0, 0), (0, LANES - PATCH)))
-    return network(
+    queue, velocities = network(
         window_offsets,
         plane_rows(latents),
         own,
@@ -650,12 +670,13 @@
         fresh,
         time_proj,
         embed_in,
-        embed_out,
+        embed_out.T,
         spatial_proj,
         spatial_out,
         temporal_proj,
         temporal_out,
     )
+    return jnp.swapaxes(queue, 1, 2), jnp.swapaxes(velocities, 2, 3)
 
 
 def solution(mesh):

time: 229 us -> 211 us (0.921)
  Pallas kernels: 214 us -> 198 us
    pallas_call x1, Pallas kernels: 214 us -> 198 us  [network(): pl.pallas_call(network_kernel, out_shape=[jax.ShapeDtypeStruct(shape, f32...]
    pallas_call x2 -> x0, local copies, waits for them, and re-layouts: 3.25 us -> none  [network(): pl.pallas_call(network_kernel, out_shape=[jax.ShapeDtypeStruct(shape, f32...]
where the time goes in v6:
time: 211 us; the launch traced here: 208 us
  Pallas kernels  198 us (94%)
  local copies, waits for them, and re-layouts  6.08 us (3%)
  other arithmetic  2.6 us (1%)
    pallas_call x1, Pallas kernels, network(): pl.pallas_call(network_kernel, out_shape=[jax.ShapeDtypeStruct(shape, f32...  198 us

profile of v6, /device:TPU:1, one launch (start us, length us, event | category | flops | bytes accessed | tf_op | source)
XLA Modules:
  0.0 208.0 jit_solution(12595190499932432935)
XLA Ops:
  0.6 0.0 copy-start
  0.6 0.8 copy.23
  1.5 0.6 pad.8.latents
  2.2 0.7 broadcast_add_fusion
  2.8 0.9 fusion.3
  3.7 0.1 fusion
  3.9 0.6 broadcast_in_dim.52.features
  4.5 0.1 broadcast_in_dim.55
  4.6 0.2 reshape.88
  4.8 0.1 reshape.90
  4.9 0.1 copy.26
  5.0 0.1 pad.12.clone
  5.1 0.9 pad_maximum_fusion.facts
  5.9 0.0 copy-done
  5.9 0.1 constant_dynamic-slice_fusion
  6.0 0.1 copy.28
  6.1 0.6 pad.9.fresh
  6.7 198.3 %network.1 = (f32[2,16,128]{2,1,0:T(8,128)}, f32[2,2,16,128]{3,2,1,0:T(8,128)}) custom-call(s32[2]{0:T(128)} %offsets.1, bf16[2,128,128]{2,1,0:T(8,128)(2,1)} %pad.8.latents, bf16[16,256]{1,0:T(8,128)(2,1)} %broadcast_in_dim.52.features, f32[256,384]{1,0:T(8,128)} %pad_maximum_fusion.facts, f32[8,128]{1,0:T(8,128)} %pad.9.fresh, ...), custom_call_target="tpu_custom_call" | custom-call | tf_op jit(solution)/shard_map/network/pallas_call | solution.py:587
  205.0 1.3 copy.31
  206.4 1.4 copy.32
  (10 shorter events, 0.1 us)
Async XLA Ops:
  0.6 5.3 %copy-start = (f32[1,128,16]{1,2,0:T(8,128)S(1)}, f32[1,128,16]{1,2,0:T(8,128)}, u32[]{:S(2)}) copy-start(f32[1,128,16]{1,2,0:T(8,128)} %param.13) | copy-start | bytes 24580

commit v7 on v6

--- a/solution.py
+++ b/solution.py
@@ -105,16 +105,6 @@
         device_id=peer,
         device_id_type=MESH,
     )
-
-
-def restore_order(quarter):
-    row = lax.broadcasted_iota(jnp.int32, (144, 4 * TOP + 4 * TILE), 0)
-    column = lax.broadcasted_iota(jnp.int32, (144, 4 * TOP + 4 * TILE), 1)
-    device, inner = row // 36, row % 36
-    source = jnp.where(
-        inner < TOP, device * TOP + inner, 4 * TOP + device * TILE + quarter * 4 + inner - TOP
-    )
-    return jnp.where(source == column, 1.0, 0.0).astype(jnp.bfloat16)
 
 
 class Gather:
@@ -257,33 +247,20 @@
 
 
 def restore_rows(blocks, whole, first, rest, quarter, tiles):
-    for a in range(4):
-        start, stop = max(a * quarter, tiles[0]), min((a + 1) * quarter, tiles[1])
-        if start >= stop:
-            continue
-        order = restore_order(a)
-
-        @pl.loop(0, 8)
-        def _(quad):
-            four = pl.ds(quad * 4, 4)
-            rows = pl.ds(pl.multiple_of(quad * 144, 16), 144)
-            for begin in range(start, stop, 4):
-                end = min(begin + 4, stop)
-                columns = []
-                for tile in range(begin, end):
-                    number = tile - a * quarter
-                    low = blocks[
-                        four, rest + number // 2, number % 2 * TILE : (number % 2 + 1) * TILE, :
-                    ]
-                    top = blocks[four, first + tile]
-                    columns.append(
-                        jnp.concatenate(
-                            [top.reshape(4 * TOP, LANES), low.reshape(4 * TILE, LANES)], 0
-                        )
-                    )
-                joined = jnp.concatenate(columns, 1)
-                result = jnp.dot(order, joined, preferred_element_type=jnp.float32)
-                whole[rows, begin * LANES : end * LANES] = result.astype(jnp.bfloat16)
+    @pl.loop(0, 8)
+    def _(quad):
+        rows = pl.ds(pl.multiple_of(quad * 144, 16), 144)
+        for tile in range(*tiles):
+            a, number = tile // quarter, tile % quarter
+            half = number % 2 * TILE
+            pieces = []
+            for device in range(4):
+                which = quad * 4 + device
+                pieces.append(blocks[which, first + tile].astype(jnp.float32))
+                low = blocks[which, rest + number // 2, half : half + TILE, :].astype(jnp.float32)
+                pieces.append(low[a * 4 : a * 4 + 4])
+            joined = jnp.concatenate(pieces, 0)
+            whole[rows, tile * LANES : (tile + 1) * LANES] = joined.astype(jnp.bfloat16)
 
 
 def network_kernel(
@@ -467,17 +444,19 @@
 
     rows = 2 * LANES
 
-    def temporal(step):
+    def temporal_head(step):
         hidden_in = jnp.dot(
             state[:, :PATCH].astype(jnp.bfloat16), embed_in[...], preferred_element_type=jnp.float32
         )
         out = jnp.dot(landing[step], shared[:, :width], preferred_element_type=jnp.float32)
         hidden = hidden_in + mods[0] * out
         normed = layer_norm(hidden) * (1.0 + mods[2]) + mods[1]
+        mix[...] = normed.astype(jnp.bfloat16)
+        return hidden
+
+    def temporal(step, hidden):
         triple[...] = jnp.dot(
-            normed.astype(jnp.bfloat16),
-            shared[:, width : 4 * width],
-            preferred_element_type=jnp.float32,
+            mix[...], shared[:, width : 4 * width], preferred_element_type=jnp.float32
         )
 
         def place_of(index):
@@ -525,12 +504,13 @@
     advance(len(plan) - 1)
     gather.collect(1)
     restore_rows(blocks, shared, 14, 8, 12, (0, 19))
+    for copy in flying:
+        copy.wait_recv()
+    hidden = temporal_head(0)
     advance(1)
     gather.collect(2)
     restore_rows(blocks, shared, 14, 8, 12, (19, 45))
-    for copy in flying:
-        copy.wait_recv()
-    stepped, velocity = temporal(0)
+    stepped, velocity = temporal(0, hidden)
     outgoing[...] = jnp.zeros((STEPS, rows, LANES), jnp.float32)
     outgoing[0, :, :PATCH] = stepped
     wide = outgoing[0]
@@ -563,7 +543,7 @@
         copy.wait_send()
     for copy in flying:
         copy.wait_recv()
-    stepped, velocity = temporal(1)
+    stepped, velocity = temporal(1, temporal_head(1))
     outgoing[1, :, :PATCH] = stepped
     outgoing[1, :, PATCH : 2 * PATCH] = state[:, PATCH : 2 * PATCH]
     outgoing[1, :, 2 * PATCH : 3 * PATCH] = velocity

time: 211 us -> 203 us (0.962)
  Pallas kernels: 198 us -> 190 us
    pallas_call x1, Pallas kernels: 198 us -> 190 us  [network(): pl.pallas_call(network_kernel, out_shape=[jax.ShapeDtypeStruct(shape, f32...]
where the time goes in v7:
time: 203 us; the launch traced here: 200 us
  Pallas kernels  190 us (94%)
  local copies, waits for them, and re-layouts  6.08 us (3%)
  other arithmetic  2.6 us (1%)
    pallas_call x1, Pallas kernels, network(): pl.pallas_call(network_kernel, out_shape=[jax.ShapeDtypeStruct(shape, f32...  190 us

profile of v7, /device:TPU:1, one launch (start us, length us, event | category | flops | bytes accessed | tf_op | source)
XLA Modules:
  0.0 200.0 jit_solution(5103112396781221533)
XLA Ops:
  0.6 0.0 copy-start
  0.6 0.8 copy.23
  1.5 0.6 pad.8.latents
  2.2 0.7 broadcast_add_fusion
  2.8 0.9 fusion.3
  3.7 0.1 fusion
  3.9 0.6 broadcast_in_dim.52.features
  4.5 0.1 broadcast_in_dim.55
  4.6 0.2 reshape.88
  4.8 0.1 reshape.90
  4.9 0.1 copy.26
  5.0 0.1 pad.12.clone
  5.1 0.9 pad_maximum_fusion.facts
  5.9 0.0 copy-done
  5.9 0.1 constant_dynamic-slice_fusion
  6.0 0.1 copy.28
  6.1 0.6 pad.9.fresh
  6.7 190.4 %network.1 = (f32[2,16,128]{2,1,0:T(8,128)}, f32[2,2,16,128]{3,2,1,0:T(8,128)}) custom-call(s32[2]{0:T(128)} %offsets.1, bf16[2,128,128]{2,1,0:T(8,128)(2,1)} %pad.8.latents, bf16[16,256]{1,0:T(8,128)(2,1)} %broadcast_in_dim.52.features, f32[256,384]{1,0:T(8,128)} %pad_maximum_fusion.facts, f32[8,128]{1,0:T(8,128)} %pad.9.fresh, ...), custom_call_target="tpu_custom_call" | custom-call | tf_op jit(solution)/shard_map/network/pallas_call | solution.py:567
  197.1 1.3 copy.31
  198.4 1.4 copy.32
  (10 shorter events, 0.1 us)
Async XLA Ops:
  0.6 5.3 %copy-start = (f32[1,128,16]{1,2,0:T(8,128)S(1)}, f32[1,128,16]{1,2,0:T(8,128)}, u32[]{:S(2)}) copy-start(f32[1,128,16]{1,2,0:T(8,128)} %param.13) | copy-start | bytes 24580

commit v8 on v7

--- a/solution.py
+++ b/solution.py
@@ -264,7 +264,7 @@
 
 
 def network_kernel(
-    offsets, latents, features, facts, fresh, time_proj, embed_in, embed_out,
+    offsets, latents, facts, fresh, time_proj, embed_in, embed_out,
     proj_s, out_s, proj_t, out_t, queue, velocities,
     blocks, tail, own, shared, info, mods, tokens, mixed, parts, stage, landing,
     state, outgoing, back, again, triple, qs, ks, vs, mix,
@@ -356,7 +356,9 @@
     gather.finish_own(5, 8)
     gather.collect(0)
     restore_rows(blocks, own, 1, 0, 2, (0, 7))
-    first_mods = jnp.dot(features[...], time_proj[:, : 2 * width], preferred_element_type=jnp.float32)
+    features = jnp.where(low == 0, facts[0:1, LANES:], facts[1:2, LANES:])
+    features = jnp.broadcast_to(features, (SUB, 2 * LANES)).astype(jnp.bfloat16)
+    first_mods = jnp.dot(features, time_proj[:, : 2 * width], preferred_element_type=jnp.float32)
     shift, scale = first_mods[:1, :width], 1.0 + first_mods[:1, width:]
     mixed[:, :, span:] = jnp.zeros((STEPS, 8 * LANES, 3 * LANES - span), jnp.bfloat16)
 
@@ -634,18 +636,16 @@
     temporal_out,
     embed_out,
 ):
-    which, row = lax.axis_index("space") % 2, lax.axis_index("frame")
+    row = lax.axis_index("frame")
     time_value = lookup_table(levels, timesteps)
     earlier = lookup_table(levels - 1, timesteps)
     features = time_features(time_value, time_proj.shape[0] // 2)
     facts = row_facts(latents, (earlier - time_value) / 1000.0, features)
-    own = jnp.broadcast_to(lax.dynamic_index_in_dim(features, which, 0), (TILE, 2 * LANES))
     fresh = lax.dynamic_slice_in_dim(fresh_noise[0], row * 4, 4)
     fresh = jnp.pad(jnp.repeat(fresh, 2, axis=0), ((0, 0), (0, LANES - PATCH)))
     queue, velocities = network(
         window_offsets,
         plane_rows(latents),
-        own,
         facts,
         fresh,
         time_proj,

time: 203 us -> 202 us (level)
  no operation moved by 1% of the time
where the time goes in v8:
time: 202 us; the launch traced here: 199 us
  Pallas kernels  190 us (94%)
  local copies, waits for them, and re-layouts  5.47 us (3%)
  other arithmetic  2.57 us (1%)
    pallas_call x1, Pallas kernels, network(): pl.pallas_call(network_kernel, out_shape=[jax.ShapeDtypeStruct(shape, f32...  190 us

profile of v8, /device:TPU:1, one launch (start us, length us, event | category | flops | bytes accessed | tf_op | source)
XLA Modules:
  0.0 199.4 jit_solution(3410218494176929459)
XLA Ops:
  0.6 0.0 copy-start
  0.6 0.8 copy.23
  1.5 0.6 pad.8.latents
  2.2 0.7 broadcast_add_fusion
  2.8 0.9 fusion.2
  3.7 0.1 fusion
  3.8 0.1 broadcast_in_dim.46
  3.9 0.2 reshape.88
  4.1 0.1 reshape.90
  4.2 0.1 copy.26
  4.4 0.1 pad.12.clone
  4.4 0.9 pad_maximum_fusion.facts
  5.3 0.0 copy-done
  5.3 0.1 constant_dynamic-slice_fusion
  5.4 0.1 copy.28
  5.5 0.6 pad.9.fresh
  6.1 190.4 %network.1 = (f32[2,16,128]{2,1,0:T(8,128)}, f32[2,2,16,128]{3,2,1,0:T(8,128)}) custom-call(s32[2]{0:T(128)} %offsets.1, bf16[2,128,128]{2,1,0:T(8,128)(2,1)} %pad.8.latents, f32[256,384]{1,0:T(8,128)} %pad_maximum_fusion.facts, f32[8,128]{1,0:T(8,128)} %pad.9.fresh, bf16[256,6912]{1,0:T(8,128)(2,1)} %time_proj.1, bf16[16,1152]{1,0:T(8,128)(2,1)} %embed_in.1, ...), custom_call_target="tpu_custom_call" | custom-call | tf_op jit(solution)/shard_map/network/pallas_call | solution.py:569
  196.5 1.3 copy.31
  197.8 1.4 copy.32
  (9 shorter events, 0.1 us)
Async XLA Ops:
  0.6 4.7 %copy-start = (f32[1,128,16]{1,2,0:T(8,128)S(1)}, f32[1,128,16]{1,2,0:T(8,128)}, u32[]{:S(2)}) copy-start(f32[1,128,16]{1,2,0:T(8,128)} %param.13) | copy-start | bytes 24580
